TPU v7x, 256 devices: a whole 4x4x8 slice. The times are simulated.
256 devices in a mesh: dp: 4 (over y), expert: 64 (over z, x, core).
Axes of the slice: x: 4, y: 4, z: 8, core: 2. Of those that a mesh axis runs over, the one named last changes fastest.
Arguments:
- out_grad: bfloat16 [4, 8192, 4096], P('dp', 'expert'), may hold values from -6 to 6
- count: int32 [4, 8192], P('dp', 'expert'), may hold values from 0 to 64, as said below
- chosen: int32 [4, 128, 128], P('dp', 'expert'), may hold values from 0 to 8191, as said below
- gates: float32 [4, 128, 128], P('dp', 'expert'), may hold values from 0.1 to 1
- x_slots: bfloat16 [4, 128, 128, 4096], P('dp', 'expert'), may hold values from -6 to 6
- w_in: bfloat16 [128, 4096, 512], P('expert', None, 'dp'), may hold values from -0.09375 to 0.09375
- w_out: bfloat16 [128, 512, 4096], P('expert', 'dp'), may hold values from -0.25 to 0.25
Outputs:
- token_grad: bfloat16 [4, 8192, 4096], P('dp', 'expert')
- gate_grad: float32 [4, 128, 128], P('dp', 'expert')
- w_in_grad: bfloat16 [128, 4096, 512], P('expert', None, 'dp')
- w_out_grad: bfloat16 [128, 512, 4096], P('expert', 'dp')
Inputs may be any that keep to these rules, and one draw needn't show every extreme that they name: `chosen`: in each group, one expert's 128 slots name different tokens, and one device's 2 experts together name different tokens. Within a group, the slots of one device's experts name at most 6 tokens of any one device (device j of expert holds the group's tokens j * 128 to (j + 1) * 128 - 1), and every such device's experts name exactly 6 tokens of some device. count[g,t] is the number of slots of group g, over all experts, whose chosen token is t; each device of expert contributes at most one.
All inputs are finite; a program needn't handle non-finite values.
Results may differ from a plain program's by a relative error of at most 0.007.
Values may be sent and summed in bfloat16 or wider, within the bound.
No kernel may reach another device: no remote copies, remote signals or barrier semaphores. Data moves between devices by JAX's collectives and lax.ppermute only.
A program may use at most 128 MiB of HBM per device.

v0:
```python
import jax
import jax.numpy as jnp
from jax import lax
from jax.sharding import PartitionSpec as P

SQRT_HALF = 0.7071067811865476
INV_ROOT_TWO_PI = 0.3989422804014327


def expert_terms(inputs, upstream, scale_w, count_f, proj_in, proj_out):
    pre = jnp.einsum("gecd,edf->gecf", inputs, proj_in, preferred_element_type=jnp.float32)
    normal_cdf = 0.5 * (1.0 + lax.erf(pre * SQRT_HALF))
    slope = normal_cdf + pre * jnp.exp(-0.5 * pre * pre) * INV_ROOT_TWO_PI
    hidden = (pre * normal_cdf).astype(jnp.bfloat16)
    project = jnp.einsum("gecd,efd->gecf", upstream, proj_out, preferred_element_type=jnp.float32)
    gate_part = jnp.sum(hidden.astype(jnp.float32) * project, axis=3) / count_f
    pre_grad = (scale_w[..., None] * project * slope).astype(jnp.bfloat16)
    out_slot = (scale_w[..., None] * upstream.astype(jnp.float32)).astype(jnp.bfloat16)
    back_part = jnp.einsum("gecf,edf->gecd", pre_grad, proj_in, preferred_element_type=jnp.float32)
    grad_in = jnp.einsum("gecd,gecf->gedf", inputs, pre_grad, preferred_element_type=jnp.float32)
    grad_out = jnp.einsum("gecf,gecd->gefd", hidden, out_slot, preferred_element_type=jnp.float32)
    return (back_part, gate_part, grad_in, grad_out)


def shards(out_grad, count, chosen, gates, x_slots, w_in, w_out):
    tok_rows = out_grad.shape[1]
    width = out_grad.shape[2]
    local_experts = chosen.shape[1]
    capacity = chosen.shape[2]
    slots = local_experts * capacity
    owners = lax.axis_size("expert")
    per_peer = 3 * tok_rows // owners
    token_ids = chosen.reshape(slots)
    source = token_ids // tok_rows
    local_row = token_ids % tok_rows
    onehot = (source[:, None] == jnp.arange(owners, dtype=jnp.int32)[None, :]).astype(jnp.int32)
    slot_rank = jnp.sum((jnp.cumsum(onehot, axis=0) - onehot) * onehot, axis=1)
    slot_place = source * per_peer + slot_rank
    request = jnp.full((owners * per_peer,), -1, jnp.int32).at[slot_place].set(local_row)
    asked_rows = lax.all_to_all(
        request.reshape(owners, per_peer), "expert", split_axis=0, concat_axis=0, tiled=True
    )
    is_valid = asked_rows >= 0
    safe_rows = jnp.where(is_valid, asked_rows, 0)
    sent_rows = jnp.where(is_valid[..., None], out_grad[0][safe_rows], 0)
    sent_counts = jnp.where(is_valid, count[0][safe_rows], 1).astype(jnp.bfloat16)
    got_rows, got_counts = (
        lax.all_to_all(sent_rows, "expert", split_axis=0, concat_axis=0, tiled=True),
        lax.all_to_all(sent_counts, "expert", split_axis=0, concat_axis=0, tiled=True),
    )
    slot_grad = got_rows.reshape(owners * per_peer, width)[slot_place]
    slot_count = got_counts.reshape(owners * per_peer)[slot_place].astype(jnp.float32)
    slot_scale = gates.reshape(slots) / slot_count
    inputs = x_slots.reshape(slots, width)
    groups = lax.axis_size("dp")
    all_inputs, all_grad = (
        lax.all_gather(inputs, "dp", axis=0, tiled=True),
        lax.all_gather(slot_grad, "dp", axis=0, tiled=True),
    )
    all_scales = lax.all_gather(jnp.stack([slot_scale, slot_count]), "dp", axis=1, tiled=True)
    back_part, gate_part, grad_in, grad_out = expert_terms(
        all_inputs.reshape(groups, local_experts, capacity, width),
        all_grad.reshape(groups, local_experts, capacity, width),
        all_scales[0].reshape(groups, local_experts, capacity),
        all_scales[1].reshape(groups, local_experts, capacity),
        w_in,
        w_out,
    )
    rounded_in = lax.optimization_barrier(grad_in.astype(jnp.bfloat16)).astype(jnp.float32)
    rounded_out = lax.optimization_barrier(grad_out.astype(jnp.bfloat16)).astype(jnp.float32)
    w_in_grad = jnp.sum(rounded_in, axis=0).astype(jnp.bfloat16)
    w_out_grad = jnp.sum(rounded_out, axis=0).astype(jnp.bfloat16)
    back_own, gate_own = (
        lax.psum_scatter(
            back_part.reshape(groups * slots, width), "dp", scatter_dimension=0, tiled=True
        ),
        lax.psum_scatter(gate_part.reshape(groups * slots), "dp", scatter_dimension=0, tiled=True),
    )
    slot_back = back_own.astype(jnp.bfloat16)
    outgoing = jnp.zeros((owners * per_peer, width), jnp.bfloat16).at[slot_place].set(slot_back)
    returned = lax.all_to_all(
        outgoing.reshape(owners, per_peer, width), "expert", split_axis=0, concat_axis=0, tiled=True
    )
    target = jnp.where(is_valid, asked_rows, tok_rows).reshape(-1)
    token_sum = (
        jnp.zeros((tok_rows, width), jnp.float32)
        .at[target]
        .add(returned.reshape(owners * per_peer, width).astype(jnp.float32), mode="drop")
    )
    token_grad = token_sum.astype(jnp.bfloat16)[None]
    gate_grad = gate_own.reshape(1, local_experts, capacity)
    return (token_grad, gate_grad, w_in_grad, w_out_grad)


def solution(mesh):
    return jax.shard_map(
        shards,
        mesh=mesh,
        in_specs=(
            P("dp", "expert", None),
            P("dp", "expert"),
            P("dp", "expert", None),
            P("dp", "expert", None),
            P("dp", "expert", None, None),
            P("expert", None, "dp"),
            P("expert", "dp", None),
        ),
        out_specs=(
            P("dp", "expert", None),
            P("dp", "expert", None),
            P("expert", None, "dp"),
            P("expert", "dp", None),
        ),
        check_vma=False,
    )
```

profile of v0, /device:TPU:1, one launch (start us, length us, event | category | flops | bytes accessed | tf_op | source)
XLA Modules:
  0.0 563.2 jit_solution(5010900081813211126)
XLA Ops:
  7.2 0.7 all-gather.4.cloned.1.call-update
  7.9 0.7 and_select_fusion.2
  8.6 0.6 reduce-window.6
  9.2 0.2 slice_reduce_fusion
  9.5 0.7 and_select_fusion.1
  10.3 0.7 compare_select_fusion.4
  11.0 1.4 scatter_custom_fusion
  12.4 0.1 all_to_all.20
  12.5 22.2 %all_to_all.31 = s32[64,1,6]{2,1,0:T(1,128)S(1)} all-to-all(s32[64,1,6]{2,1,0:T(1,128)S(1)} %bitcast.113), channel_id=1, replica_groups=mesh['dp'=4,'expert'=64] {'expert'}, dimensions={0} | all-to-all | bytes 3072 | tf_op jit(solution)/shard_map/all_to_all | solution.py:40
  34.7 0.1 reshape.278
  34.8 2.7 gather_fusion
  37.5 0.1 gather.15
  37.8 0.1 copy.59
  38.0 4.0 gather_fusion.2
  42.0 5.7 %reshape.293 = bf16[64,6,4096]{2,1,0:T(8,128)(2,1)} reshape(bf16[384,4096]{1,0:T(8,128)(2,1)} %gather_fusion.2) | data formatting | bytes 6291456 | tf_op jit(solution)/shard_map/gather | solution.py:45
  47.7 4.6 broadcast_select_fusion
  52.3 5.7 %all-to-all-start.2 = ((bf16[64,6,4096]{2,1,0:T(8,128)(2,1)}), bf16[64,6,4096]{2,1,0:T(8,128)(2,1)}, u32[]{:S(2)}, u32[]{:S(2)}) async-start(bf16[64,6,4096]{2,1,0:T(8,128)(2,1)} %broadcast_select_fusion), calls=%async_computation.2 | async-start | bytes 8388608 | tf_op jit(solution)/shard_map/all_to_all | solution.py:48
  58.0 94.6 %all-to-all-done.2 = bf16[64,6,4096]{2,1,0:T(8,128)(2,1)} async-done(((bf16[64,6,4096]{2,1,0:T(8,128)(2,1)}), bf16[64,6,4096]{2,1,0:T(8,128)(2,1)}, u32[]{:S(2)}, u32[]{:S(2)}) %all-to-all-start.2) | async-done | bytes 3145760 | tf_op jit(solution)/shard_map/all_to_all | solution.py:48
  152.6 5.7 %reshape.267 = bf16[384,4096]{1,0:T(8,128)(2,1)} reshape(bf16[64,6,4096]{2,1,0:T(8,128)(2,1)} %all-to-all-done.2) | data formatting | bytes 6291456 | tf_op jit(solution)/shard_map/reshape | solution.py:51
  158.4 7.5 %gather_fusion.3 = bf16[256,4096]{1,0:T(8,128)(2,1)} fusion(bf16[384,4096]{1,0:T(8,128)(2,1)} %reshape.267, s32[1024]{0:T(1024)S(1)} %pad_clamp_fusion), kind=kCustom, calls=%fused_computation.3 | custom fusion | bytes 4195328 | tf_op jit(solution)/shard_map/gather | solution.py:51
  166.1 16.8 %all_to_all.32 = bf16[64,1,6]{2,1,0:T(2,128)(2,1)S(1)} all-to-all(bf16[64,1,6]{2,1,0:T(2,128)(2,1)S(1)} %copy.57), channel_id=1, replica_groups=mesh['dp'=4,'expert'=64] {'expert'}, dimensions={0} | all-to-all | bytes 1536 | tf_op jit(solution)/shard_map/all_to_all | solution.py:49
  182.9 0.1 reshape.266
  183.1 1.9 gather_fusion.1
  185.1 9.7 %all_gather.9 = f32[2,1024]{1,0:T(2,128)S(1)} all-gather(f32[2,256]{1,0:T(2,128)S(1)} %pad_maximum_fusion), channel_id=1, replica_groups=mesh['dp'=4,'expert'=64] {'dp'}, dimensions={1}, use_global_device_ids=true | all-gather | bytes 10240 | tf_op jit(solution)/shard_map/all_gather | solution.py:60
  194.8 7.2 %fusion.18 = f32[4,2,128,128]{2,3,0,1:T(8,128)} fusion(bf16[4,2,128,4096]{3,2,1,0:T(8,128)(2,1)} %bitcast.109, bf16[2,4096,128]{2,1,0:T(8,128)(2,1)S(1)} %copy-done), kind=kOutput, calls=%fused_computation.25 | convolution fusion | flops 1073741824 | bytes 11010048 | tf_op jit(solution)/shard_map/gecd,edf->gecf/dot_general | solution.py:11
  202.0 47.7 %all-gather.6.cloned.1.call-done = bf16[1024,4096]{1,0:T(8,128)(2,1)} async-done(((bf16[256,4096]{1,0:T(8,128)(2,1)}), bf16[1024,4096]{1,0:T(8,128)(2,1)}) %all-gather.6.cloned.1.call-update) | async-done | bytes 8388624 | tf_op jit(solution)/shard_map/all_gather | solution.py:58
  249.8 7.1 %multiply_reduce_fusion = (f32[4,2,128]{2,0,1:T(4,128)S(1)}, bf16[4,2,128,128]{2,3,0,1:T(8,128)(2,1)S(1)}, bf16[4,2,128,128]{2,3,0,1:T(8,128)(2,1)S(1)}) fusion(f32[4,2,128,128]{2,3,0,1:T(8,128)} %fusion.18, f32[4,2,128]{2,0,1:T(4,128)S(1)} %copy.58, bf16[2,128,4096]{2,1,0:T(8,128)(2,1)} %param.13, bf16[4,2,128,4096]{3,2,1,0:T(8,128)(2,1)} %bitcast.107), kind=kOutput, calls=%fused_computation.36 | convolution fusion | flops 1075837952 | bytes 11542528 | tf_op jit(solution)/shard_map/gecd,efd->gecf/dot_general | solution.py:15
  256.9 2.4 convolution_bitcast_fusion
  259.2 6.0 %copy.64 = f32[4,2,128,4096]{3,2,1,0:T(8,128)} copy(f32[4,2,128,4096]{3,2,0,1:T(8,128)S(1)} %convolution_bitcast_fusion) | data formatting | bytes 33554432 | tf_op jit(solution)/shard_map/gecf,edf->gecd/transpose | solution.py:19
  265.3 151.6 %reduce-scatter.2.cloned.1.call-done = f32[256,4096]{1,0:T(8,128)} async-done(((f32[1024,4096]{1,0:T(8,128)}), f32[256,4096]{1,0:T(8,128)}) %reduce-scatter.2.cloned.1.call-update) | async-done | bytes 4194320 | tf_op jit(solution)/shard_map/reduce_scatter | solution.py:74
  416.9 7.3 %scatter_custom_fusion.1 = bf16[384,4096]{1,0:T(8,128)(2,1)} fusion(s32[256]{0:T(256)S(1)} %bitcast.122, f32[256,4096]{1,0:T(8,128)} %reduce-scatter.2.cloned.1.call-done, bf16[]{:T(256)} %constant.56.clone.1), kind=kCustom, calls=%fused_computation.21 | custom fusion | flops 1048576 | bytes 7340034 | tf_op jit(solution)/shard_map/scatter | solution.py:80
  424.2 5.6 %reshape.272 = bf16[64,6,4096]{2,1,0:T(8,128)(2,1)} reshape(bf16[384,4096]{1,0:T(8,128)(2,1)} %scatter_custom_fusion.1) | data formatting | bytes 6291456 | tf_op jit(solution)/shard_map/reshape | solution.py:82
  429.8 10.9 %all-to-all-start.3 = ((bf16[64,6,4096]{2,1,0:T(8,128)(2,1)}), bf16[64,6,4096]{2,1,0:T(8,128)(2,1)}, u32[]{:S(2)}, u32[]{:S(2)}) async-start(bf16[64,6,4096]{2,1,0:T(8,128)(2,1)} %reshape.272), calls=%async_computation.4 | async-start | bytes 8388608 | tf_op jit(solution)/shard_map/all_to_all | solution.py:81
  440.7 0.6 dynamic-slice
  442.0 0.5 broadcast.263
  442.5 0.7 reduce.10
  443.2 0.1 all_to_all.22
  443.4 8.9 %convert_bitcast_fusion = bf16[4,2,4096,128]{2,3,1,0:T(8,128)(2,1)} fusion(bf16[4,2,128,4096]{3,2,1,0:T(8,128)(2,1)} %bitcast.110, bf16[4,2,128,128]{2,3,0,1:T(8,128)(2,1)S(1)} %get-tuple-element.20), kind=kOutput, calls=%fused_computation.15 | convolution fusion | flops 1077936128 | bytes 17039360 | tf_op jit(solution)/shard_map/gecd,gecf->gedf/dot_general | solution.py:20
  452.3 5.2 reduce_sum.50
  457.5 2.5 copy.68
  459.9 9.0 %fusion.6 = bf16[4,2,128,4096]{3,2,1,0:T(8,128)(2,1)} fusion(bf16[4,2,128,4096]{3,2,1,0:T(8,128)(2,1)} %bitcast.108, f32[4,2,128]{2,1,0:T(2,128)S(1)} %bitcast.115, bf16[4,2,128,128]{2,3,0,1:T(8,128)(2,1)S(1)} %get-tuple-element.17), kind=kOutput, calls=%fused_computation.16 | convolution fusion | flops 1090519040 | bytes 17043456 | tf_op jit(solution)/shard_map/gecf,gecd->gefd/dot_general | solution.py:21
  469.0 6.9 %reduce_sum.51 = bf16[2,128,4096]{2,1,0:T(8,128)(2,1)} reduce(bf16[4,2,128,4096]{3,2,1,0:T(8,128)(2,1)} %fusion.6, bf16[]{:T(256)} %constant.56.clone.1), dimensions={0}, to_apply=%region_10.11 | reduce | flops 3145728 | bytes 10485762 | tf_op jit(solution)/shard_map/reduce_sum | solution.py:72
  475.9 7.5 %all-reduce = f32[1024]{0:T(1024)S(1)} all-reduce(f32[1024]{0:T(1024)S(1)} %div.55), channel_id=4, replica_groups=mesh['dp'=4,'expert'=64] {'dp'}, use_global_device_ids=true, to_apply=%region_8.9.clone | all-reduce | flops 1024 | bytes 8192
  483.4 0.6 dynamic-slice_bitcast_fusion
  484.1 51.1 %all-to-all-done.3 = bf16[64,6,4096]{2,1,0:T(8,128)(2,1)} async-done(((bf16[64,6,4096]{2,1,0:T(8,128)(2,1)}), bf16[64,6,4096]{2,1,0:T(8,128)(2,1)}, u32[]{:S(2)}, u32[]{:S(2)}) %all-to-all-start.3) | async-done | bytes 3145760 | tf_op jit(solution)/shard_map/all_to_all | solution.py:81
  535.1 6.5 %reshape.328 = f32[384,4096]{1,0:T(8,128)} reshape(bf16[64,6,4096]{2,1,0:T(8,128)(2,1)} %all-to-all-done.3) | data formatting | bytes 9437184 | tf_op jit(solution)/shard_map/convert_element_type | solution.py:88
  541.6 12.2 %scatter_custom_fusion.2 = f32[128,4096]{1,0:T(8,128)} fusion(s32[384]{0:T(512)S(1)} %fusion.37, f32[384,4096]{1,0:T(8,128)} %reshape.328, f32[]{:T(128)} %constant.24.clone.1), kind=kCustom, calls=%fused_computation.27 | custom fusion | flops 1572864 | bytes 2097664 | tf_op jit(solution)/shard_map/scatter-add | solution.py:88
  553.8 2.7 convert_bitcast_fusion.1
  (38 shorter events, 0.8 us)
Async XLA Ops:
  7.2 187.7 %copy-start = (bf16[2,4096,128]{2,1,0:T(8,128)(2,1)S(1)}, bf16[2,4096,128]{2,1,0:T(8,128)(2,1)}, u32[]{:S(2)}) copy-start(bf16[2,4096,128]{2,1,0:T(8,128)(2,1)} %param.12) | copy-start | bytes 6291460
  7.2 27.6 %copy-start.2 = (s32[1,128]{1,0:T(1,128)S(1)}, s32[1,128]{1,0:T(1,128)}, u32[]{:S(2)}) copy-start(s32[1,128]{1,0:T(1,128)} %param.8) | copy-start | bytes 1540
  7.2 187.6 %all-gather.4.cloned.1.call-start = ((), (), s32[]{:S(2)}) async-start(), calls=%async_computation.5 | async-start | bytes 10485760 | tf_op jit(solution)/shard_map/all_gather | solution.py:57
  34.8 3.1 copy-start.3
  52.3 100.4 %all-to-all-start.2 = ((bf16[64,6,4096]{2,1,0:T(8,128)(2,1)}), bf16[64,6,4096]{2,1,0:T(8,128)(2,1)}, u32[]{:S(2)}, u32[]{:S(2)}) async-start(bf16[64,6,4096]{2,1,0:T(8,128)(2,1)} %broadcast_select_fusion), calls=%async_computation.2 | async-start | bytes 8388608 | tf_op jit(solution)/shard_map/all_to_all | solution.py:48
  58.0 191.8 %all-gather.6.cloned.1.call-start = ((), (), s32[]{:S(2)}) async-start(), calls=%async_computation.7 | async-start | bytes 10485760 | tf_op jit(solution)/shard_map/all_gather | solution.py:58
  158.4 26.7 %copy-start.4 = (f32[1,2,128]{2,1,0:T(2,128)S(1)}, f32[1,2,128]{2,1,0:T(2,128)}, u32[]{:S(2)}) copy-start(f32[1,2,128]{2,1,0:T(2,128)} %param.10) | copy-start | bytes 3076
  165.9 251.0 %reduce-scatter.2.cloned.1.call-start = ((), (), s32[]{:S(2)}) async-start(), calls=%async_computation.6 | async-start | bytes 20971520 | tf_op jit(solution)/shard_map/reduce_scatter | solution.py:74
  429.8 10.9 %copy-start.5 = (u32[256]{0:T(256)S(1)}, u32[256]{0:T(256)}, u32[]{:S(2)}) copy-start(u32[256]{0:T(256)} %constant.71) | copy-start | bytes 3076
  429.8 105.3 %all-to-all-start.3 = ((bf16[64,6,4096]{2,1,0:T(8,128)(2,1)}), bf16[64,6,4096]{2,1,0:T(8,128)(2,1)}, u32[]{:S(2)}, u32[]{:S(2)}) async-start(bf16[64,6,4096]{2,1,0:T(8,128)(2,1)} %reshape.272), calls=%async_computation.4 | async-start | bytes 8388608 | tf_op jit(solution)/shard_map/all_to_all | solution.py:81
  535.1 21.3 %copy-start.1 = (bf16[2,4096,128]{2,1,0:T(8,128)(2,1)S(1)}, bf16[2,4096,128]{2,1,0:T(8,128)(2,1)}, u32[]{:S(2)}) copy-start(bf16[2,4096,128]{2,1,0:T(8,128)(2,1)} %param.12) | copy-start | bytes 6291460
Sparse Core Ops, SparseCore 0:
  9.8 89.4 all-gather.3
  166.0 83.6 all-gather.5
  265.4 151.4 reduce-scatter.1
where the time goes:
time: 573 us; the launch traced here: 563 us
  waiting for transfers between devices  346 us (60%)
  blocking collectives  56.2 us (10%)
  local copies, waits for them, and re-layouts  52.6 us (9%)
  other arithmetic  42.5 us (7%)
  matrix products  34.6 us (6%)
  starting transfers between devices  16.7 us (3%)
  between operations  14.9 us (3%)
    reduce_scatter x1, waiting for transfers between devices, shards(): lax.psum_scatter(back_part.reshape(groups * slots, width), 'dp', scatter_...  152 us
    all_to_all x1, waiting for transfers between devices, shards(): lax.all_to_all(sent_rows, 'expert', split_axis=0, concat_axis=0, tiled=True)  94.6 us
    all_to_all x1, waiting for transfers between devices, shards(): lax.all_to_all(outgoing.reshape(owners, per_peer, width), 'expert', split...  51.1 us
    all_gather x1, waiting for transfers between devices, shards(): lax.all_gather(slot_grad, 'dp', axis=0, tiled=True)  47.7 us
    all_to_all x1, blocking collectives, shards(): lax.all_to_all(request.reshape(owners, per_peer), 'expert', split_axis=0,...  22.2 us
    all_to_all x1, blocking collectives, shards(): lax.all_to_all(sent_counts, 'expert', split_axis=0, concat_axis=0, tiled=...  16.8 us
    scatter-add x1, other arithmetic, shards(): token_sum = jnp.zeros((tok_rows, width), jnp.float32).at[target].add(retu...  12.2 us
  transfers between devices with their start and end apart: 5, of which 4 were waited for; matrix products, arithmetic and copies ran while one was open for 14% of the time, Pallas kernels for 0%

commit v1 on v0

v1 whole, which is shorter than its diff:
```python
import functools

import jax
import jax.numpy as jnp
from jax import lax
from jax.experimental import pallas as pl
from jax.experimental.pallas import tpu as pltpu
from jax.sharding import PartitionSpec as P

SQRT_HALF = 0.7071067811865476
INV_ROOT_TWO_PI = 0.3989422804014327
PEER = 6
F32 = jnp.float32
BF16 = jnp.bfloat16
VMEM_BYTES = 40 * 1024 * 1024


def dot(a, b, dims):
    return lax.dot_general(a, b, (dims, ((), ())), preferred_element_type=F32)


def whole(shape):
    return pl.BlockSpec(shape, lambda *_: (0,) * len(shape))


def call(kernel, outs, args, in_specs=None, out_specs=None, grid=(1,), scratch=(), flops=0, scalars=0):
    shapes = [jax.ShapeDtypeStruct(shape, dtype) for shape, dtype in outs]
    sizes = [a.size * a.dtype.itemsize for a in args]
    sizes += [s.size * s.dtype.itemsize for s in shapes]
    in_specs = in_specs or [whole(a.shape) for a in args[scalars:]]
    out_specs = out_specs or [whole(s.shape) for s in shapes]
    return pl.pallas_call(
        kernel,
        out_shape=shapes,
        grid_spec=pltpu.PrefetchScalarGridSpec(
            num_scalar_prefetch=scalars,
            grid=grid,
            in_specs=in_specs,
            out_specs=out_specs,
            scratch_shapes=list(scratch),
        ),
        compiler_params=pltpu.CompilerParams(vmem_limit_bytes=VMEM_BYTES),
        cost_estimate=pl.CostEstimate(flops=flops, bytes_accessed=sum(sizes), transcendentals=0),
    )(*args)


def pack_kernel(n, tok, pick, *refs):
    blocks, sent, held = refs[:n], refs[n], refs[n + 1]

    @pl.when(pl.program_id(0) == 0)
    def _():
        for p in range(n):
            held[p * tok : (p + 1) * tok] = blocks[p][...]

    ids = lax.broadcasted_iota(jnp.int32, (pick.shape[0], n * tok), 1)
    onehot = jnp.where(pick[...] == ids, 1.0, 0.0).astype(BF16)
    sent[...] = dot(onehot, held[...], ((1,), (0,))).astype(BF16)


def project_kernel(n, cap, into, got, *refs):
    ws, up, outs, wide = refs[:n], refs[n], refs[n + 1 : 2 * n + 1], refs[2 * n + 1]
    share = ws[0].shape[1]
    for s in range(n):
        wide[s * share : (s + 1) * share] = ws[s][0]
    ids = lax.broadcasted_iota(jnp.int32, (n * cap, got.shape[0]), 1)
    onehot = jnp.where(into[...] == ids, 1.0, 0.0).astype(BF16)
    up[...] = dot(onehot, got[...], ((1,), (0,))).astype(BF16)
    part = dot(up[...], wide[...], ((1,), (1,)))
    for s in range(n):
        for p in range(n):
            low = ((p - s) % n) * cap
            block = part[p * cap : (p + 1) * cap, s * share : (s + 1) * share]
            outs[s][low : low + cap] = block.astype(outs[s].dtype)


def back_kernel(n, cap, me, place, *refs):
    ps, ws, out = refs[:n], refs[n : 2 * n], refs[2 * n]
    wide, tall, back = refs[2 * n + 1 :]
    experts, width, share = ws[0].shape
    thin = width // n
    step = out.shape[1] // 2
    p = pl.program_id(0)

    @pl.when(p == 0)
    def _():
        for e in range(experts):
            for s in range(n):
                wide[:, s * share : (s + 1) * share] = ws[s][e]
                for g in range(n):
                    low = (e * n + (g - s) % n) * cap
                    tall[g * cap : (g + 1) * cap, s * share : (s + 1) * share] = ps[s][low : low + cap]
            mine = dot(tall[...], wide[...], ((1,), (1,))).astype(BF16)
            for g in range(n):
                back[g, e * cap : (e + 1) * cap] = mine[g * cap : (g + 1) * cap]

    where = place[pl.ds(p, 1)]
    for t in range(2):
        ids = lax.broadcasted_iota(jnp.int32, (step, experts * cap), 0) + t * step
        total = jnp.zeros((step, thin), F32)
        for b in range(n):
            onehot = jnp.where(ids == where + b * PEER, 1.0, 0.0).astype(BF16)
            total = total + dot(onehot, back[p, :, b * thin : (b + 1) * thin], ((1,), (0,)))
        out[0, t * step : (t + 1) * step] = total.astype(BF16)


def grad_out_kernel(n, cap, *refs):
    hs, up, outs, tall = refs[:n], refs[n], refs[n + 1 : 2 * n + 1], refs[2 * n + 1]
    experts, share, _ = outs[0].shape
    for s in range(n):
        for e in range(experts):
            for p in range(n):
                low = (e * n + (p - s) % n) * cap
                high = (e * n + p) * cap
                tall[high : high + cap, s * share : (s + 1) * share] = hs[s][low : low + cap]
    for e in range(experts):
        rows = slice(e * n * cap, (e + 1) * n * cap)
        grad = dot(tall[rows], up[rows], ((0,), (0,)))
        for s in range(n):
            outs[s][e] = grad[s * share : (s + 1) * share].astype(BF16)


def sum_kernel(n, tok, home, returned, out, onehot):
    rows, thin = returned.shape[1:]

    @pl.when(pl.program_id(0) == 0)
    def _():
        ids = lax.broadcasted_iota(jnp.int32, (n * tok, rows), 0)
        onehot[...] = jnp.where(home[...] == ids, 1.0, 0.0).astype(BF16)

    total = dot(onehot[...], returned[0], ((1,), (0,))).astype(BF16)
    for b in range(n):
        out[:, b * thin : (b + 1) * thin] = total[b * tok : (b + 1) * tok]


def shards(out_grad, count, chosen, gates, x_slots, w_in, w_out):
    tok = out_grad.shape[1]
    width = out_grad.shape[2]
    experts, cap = chosen.shape[1:]
    slots = experts * cap
    share = w_in.shape[2]
    n = lax.axis_size("dp")
    owners = lax.axis_size("expert")
    me = lax.axis_index("dp")
    quarter = width // n
    thin = quarter // n
    rows = n * PEER
    every = n * slots

    def shift(x, s):
        return lax.ppermute(x, "dp", [(a, (a + s) % n) for a in range(n)])

    def at(s):
        return lax.rem(me + (s + n), n)

    def columns(x, s):
        return lax.dynamic_slice_in_dim(x, at(s) * quarter, quarter, axis=x.ndim - 1)

    def forward(blocks):
        return [blocks[0]] + [shift(blocks[s], s) for s in range(1, n)]

    def backward(blocks):
        return [blocks[0]] + [shift(blocks[s], -s) for s in range(1, n)]

    def reduced(blocks):
        total = blocks[0]
        for block in backward(blocks)[1:]:
            total = total + block.astype(F32)
        return total

    inputs = lax.all_gather(x_slots.reshape(slots, width), "dp", axis=0, tiled=True)
    inputs = inputs.reshape(n, experts, cap, width)

    def turned(x):
        return [lax.dynamic_index_in_dim(x, at(-p), 0, keepdims=False) for p in range(n)]

    facts = jnp.stack([gates.reshape(slots), chosen.reshape(slots).astype(F32)])
    facts = jnp.stack(forward([facts] * n))
    tokens = facts[:, 1].astype(jnp.int32)
    source = lax.div(tokens, tok)
    onehot = (source[:, :, None] == jnp.arange(owners, dtype=jnp.int32)).astype(BF16)
    slot_ids = jnp.arange(slots, dtype=jnp.int32)
    earlier = (slot_ids[None, :] < slot_ids[:, None]).astype(BF16)
    before = jnp.einsum("st,ptk->psk", earlier, onehot, preferred_element_type=F32)
    rank = jnp.sum(before * onehot.astype(F32), axis=2).astype(jnp.int32)
    marked = rank[:, :, None] == jnp.arange(8, dtype=jnp.int32)
    marked = jnp.where(marked, (lax.rem(tokens, tok) + 1)[:, :, None], 0).astype(BF16)
    request = jnp.einsum("psk,psr->kpr", onehot, marked, preferred_element_type=F32)
    request = request.astype(jnp.int32).reshape(owners, n * 8) - 1
    asked = lax.all_to_all(request, "expert", split_axis=0, concat_axis=0, tiled=True)
    asked = asked.reshape(owners, n, 8)[:, :, :PEER]

    spread = jnp.maximum(count[0], 1).astype(F32)[:, None]
    table = (out_grad[0].astype(F32) / spread).astype(BF16)
    held = forward([columns(table, s) for s in range(n)])

    place = source * rows + rank
    scale = facts[:, 0].reshape(n, experts, cap).transpose(1, 0, 2).reshape(every, 1)
    into = place + jnp.arange(n, dtype=jnp.int32)[:, None] * PEER
    into = into.reshape(n, experts, cap).transpose(1, 0, 2).reshape(every, 1)

    own_out = [columns(w_out, s) for s in range(n)]
    own_in = [lax.dynamic_slice_in_dim(w_in, at(s) * quarter, quarter, axis=1) for s in range(n)]
    w_out_all = forward(own_out)
    w_in_all = forward(own_in)
    inputs, w_in_all = lax.optimization_barrier((inputs, w_in_all))

    start = jnp.arange(n, dtype=jnp.int32)[None, :, None] * tok
    pick = jnp.where(asked >= 0, asked + start, -1).reshape(owners * rows, 1)
    (sent,) = call(
        functools.partial(pack_kernel, n, tok),
        [((owners * rows, quarter), BF16)],
        [pick, *held],
        [pl.BlockSpec((owners * rows // 6, 1), lambda t: (t, 0))] + [whole((tok, quarter))] * n,
        [pl.BlockSpec((owners * rows // 6, quarter), lambda t: (t, 0))],
        (6,),
        [pltpu.VMEM((n * tok, quarter), BF16)],
        flops=2 * owners * rows * n * tok * quarter,
    )
    got = lax.all_to_all(
        sent.reshape(owners, rows, quarter), "expert", split_axis=0, concat_axis=0, tiled=True
    )

    pre = jnp.einsum("gecd,edf->gecf", inputs, w_in, preferred_element_type=F32)
    pre = jnp.stack(turned(pre), 1).reshape(every, share)
    normal_cdf = 0.5 * (1.0 + lax.erf(pre * SQRT_HALF))
    slope = scale * (normal_cdf + pre * jnp.exp(-0.5 * pre * pre) * INV_ROOT_TWO_PI)
    hidden = pre * normal_cdf
    hidden_all = forward([(scale * hidden).astype(BF16)] * n)
    hidden = hidden.astype(BF16)

    partials = [((every, share), F32)] + [((every, share), BF16)] * (n - 1)
    up, *partial = call(
        functools.partial(project_kernel, n, cap),
        [((every, quarter), BF16)] + partials,
        [into, got.reshape(owners * rows, quarter), *w_out_all],
        [pl.BlockSpec((n * cap, 1), lambda e: (e, 0)), whole((owners * rows, quarter))]
        + [pl.BlockSpec((1, share, quarter), lambda e: (e, 0, 0))] * n,
        [pl.BlockSpec((n * cap, quarter), lambda e: (e, 0))]
        + [pl.BlockSpec((n * cap, share), lambda e: (e, 0))] * n,
        (experts,),
        [pltpu.VMEM((n * share, quarter), BF16)],
        flops=2 * every * quarter * (n * share + owners * rows),
    )
    project = reduced(partial)
    project, hidden_all = lax.optimization_barrier((project, hidden_all))
    gate = jnp.sum(hidden.astype(F32) * project, axis=1).reshape(experts, n, cap)
    gate = reduced([gate[:, p] for p in range(n)])
    pre_grad = forward([(project * slope).astype(BF16)] * n)
    pre_grad, gate = lax.optimization_barrier((pre_grad, gate))
    gate_grad = gate.reshape(1, experts, cap)

    out_blocks = call(
        functools.partial(grad_out_kernel, n, cap),
        [((experts, share, quarter), BF16)] * n,
        [*hidden_all, up],
        scratch=[pltpu.VMEM((every, n * share), BF16)],
        flops=2 * every * quarter * n * share,
    )
    pre_grad, out_blocks = lax.optimization_barrier((pre_grad, out_blocks))
    out_blocks = backward(out_blocks)

    (outgoing,) = call(
        functools.partial(back_kernel, n, cap),
        [((n, owners * rows, thin), BF16)],
        [me.reshape(1), place, *pre_grad, *w_in_all],
        out_specs=[
            pl.BlockSpec((1, owners * rows, thin), lambda p, m: (lax.rem(m[0] + n - p, n), 0, 0))
        ],
        grid=(n,),
        scratch=[
            pltpu.VMEM((quarter, n * share), BF16),
            pltpu.VMEM((n * cap, n * share), BF16),
            pltpu.VMEM((n, slots, quarter), BF16),
        ],
        flops=2 * every * quarter * (n * share + owners * rows),
        scalars=1,
    )
    returned = lax.all_to_all(
        outgoing.reshape(n * owners, rows, thin),
        ("dp", "expert"),
        split_axis=0,
        concat_axis=0,
        tiled=True,
    )

    own_grad = pre_grad[0].reshape(experts, n, cap, share).transpose(1, 0, 2, 3)
    own_grad = jnp.stack(turned(own_grad))
    w_in_grad = jnp.einsum("gecd,gecf->edf", inputs, own_grad, preferred_element_type=F32).astype(BF16)
    w_out_grad = jnp.zeros(w_out.shape, BF16)
    for s in range(n):
        w_out_grad = lax.dynamic_update_slice(w_out_grad, out_blocks[s], (0, 0, at(s) * quarter))

    mine = asked[:, :1]
    home = jnp.where(mine >= 0, mine + jnp.arange(n, dtype=jnp.int32)[None, :, None] * tok, -1)
    (token_grad,) = call(
        functools.partial(sum_kernel, n, tok),
        [((tok, width), BF16)],
        [home.reshape(1, owners * rows), returned.reshape(n, owners * rows, thin)],
        [whole((1, owners * rows)), pl.BlockSpec((1, owners * rows, thin), lambda q: (q, 0, 0))],
        [pl.BlockSpec((tok, quarter), lambda q: (0, q))],
        (n,),
        [pltpu.VMEM((n * tok, owners * rows), BF16)],
        flops=2 * n * tok * owners * rows * quarter,
    )
    return (token_grad[None], gate_grad, w_in_grad, w_out_grad)


def solution(mesh):
    return jax.shard_map(
        shards,
        mesh=mesh,
        in_specs=(
            P("dp", "expert", None),
            P("dp", "expert"),
            P("dp", "expert", None),
            P("dp", "expert", None),
            P("dp", "expert", None, None),
            P("expert", None, "dp"),
            P("expert", "dp", None),
        ),
        out_specs=(
            P("dp", "expert", None),
            P("dp", "expert", None),
            P("expert", None, "dp"),
            P("expert", "dp", None),
        ),
        check_vma=False,
    )
```

time: 573 us -> 302 us (0.53); the launches traced: 563 us -> 302 us
  waiting for transfers between devices: 346 us -> 148 us
  starting transfers between devices: 16.7 us -> 77.4 us
  blocking collectives: 56.2 us -> 0 us
  other arithmetic: 42.5 us -> 2.43 us
  local copies, waits for them, and re-layouts: 52.6 us -> 21.8 us
  Pallas kernels: 0 us -> 22.4 us
  matrix products: 34.6 us -> 14.8 us
    reduce_scatter x1 -> x0, waiting for transfers between devices: 152 us -> none  [shards(): lax.psum_scatter(back_part.reshape(groups * slots, width), 'dp', scatter_...]
    ppermute x0 -> x27, waiting for transfers between devices: none -> 92.7 us  [shift(): return lax.ppermute(x, 'dp', [(a, (a + s) % n) for a in range(n)])]
    all_to_all x2 -> x3, waiting for transfers between devices: 146 us -> 54.9 us  [the longest x1 25.2 us: shards(): lax.all_to_all(outgoing.reshape(n * owners, rows, thin), ('dp', 'expert')...]
    all_gather x2 -> x1, waiting for transfers between devices: 47.8 us -> 0.01 us  [shards(): lax.all_gather(x_slots.reshape(slots, width), 'dp', axis=0, tiled=True)]
    ppermute x0 -> x27, starting transfers between devices: none -> 42.4 us  [shift(): return lax.ppermute(x, 'dp', [(a, (a + s) % n) for a in range(n)])]
    all_to_all x2 -> x0, blocking collectives: 38.9 us -> none  [the longest x1 22.2 us: shards(): lax.all_to_all(request.reshape(owners, per_peer), 'expert', split_axis=0,...]
    pallas_call x0 -> x5, Pallas kernels: none -> 22.4 us  [call(): pl.pallas_call(kernel, out_shape=shapes, grid_spec=pltpu.PrefetchScalarGr...]
    gather x7 -> x0, local copies, waits for them, and re-layouts: 22 us -> none  [the longest x2 9.71 us: shards(): sent_rows = jnp.where(is_valid[..., None], out_grad[0][safe_rows], 0)]
  transfers between devices with their start and end apart: 5 -> 31, of which waited for: 4 -> 15; matrix products, arithmetic and copies ran while one was open for 14% -> 10% of each run, Pallas kernels for 0% -> 4%
where the time goes in v1:
time: 302 us
  waiting for transfers between devices  148 us (49%)
  starting transfers between devices  77.4 us (26%)
  Pallas kernels  22.4 us (7%)
  local copies, waits for them, and re-layouts  21.8 us (7%)
  matrix products  14.8 us (5%)
  between operations  14.4 us (5%)
    ppermute x27, waiting for transfers between devices, shift(): return lax.ppermute(x, 'dp', [(a, (a + s) % n) for a in range(n)])  92.7 us
    ppermute x27, starting transfers between devices, shift(): return lax.ppermute(x, 'dp', [(a, (a + s) % n) for a in range(n)])  42.4 us
    all_to_all x1, waiting for transfers between devices, shards(): lax.all_to_all(outgoing.reshape(n * owners, rows, thin), ('dp', 'expert')...  25.2 us
    pallas_call x5, Pallas kernels, call(): pl.pallas_call(kernel, out_shape=shapes, grid_spec=pltpu.PrefetchScalarGr...  22.4 us
    all_to_all x1, waiting for transfers between devices, shards(): lax.all_to_all(sent.reshape(owners, rows, quarter), 'expert', split_axis=...  20.4 us
    all_to_all x1, starting transfers between devices, shards(): lax.all_to_all(outgoing.reshape(n * owners, rows, thin), ('dp', 'expert')...  16.6 us
    all_to_all x1, starting transfers between devices, shards(): lax.all_to_all(request, 'expert', split_axis=0, concat_axis=0, tiled=True)  13.6 us
    all_to_all x1, waiting for transfers between devices, shards(): lax.all_to_all(request, 'expert', split_axis=0, concat_axis=0, tiled=True)  9.29 us
  transfers between devices with their start and end apart: 31, of which 15 were waited for; matrix products, arithmetic and copies ran while one was open for 10% of the time, Pallas kernels for 4%

profile of v1, /device:TPU:1, one launch (start us, length us, event | category | flops | bytes accessed | tf_op | source)
XLA Modules:
  0.0 301.5 jit_solution(2415531676214115031)
XLA Ops:
  8.0 3.6 %collective-permute-start.2 = (f32[2,256]{1,0:T(2,128)S(1)}, f32[2,256]{1,0:T(2,128)S(1)}, u32[]{:S(2)}, u32[]{:S(2)}) collective-permute-start(f32[2,256]{1,0:T(2,128)S(1)} %get-tuple-element.97), channel_id=1, source_target_pairs={{0,192},{64,0},{128,64},{192,128},{1,193},{65,1},{129,65},{193,129... | collective-permute-start | bytes 6152 | tf_op jit(solution)/shard_map/ppermute | solution.py:150
  13.1 1.7 collective-permute-start.3
  14.7 1.6 collective-permute-start.4
  18.5 13.6 %all-to-all-start = ((s32[64,1,32]{2,1,0:T(1,128)}), s32[64,1,32]{2,1,0:T(1,128)S(1)}, u32[]{:S(2)}, u32[]{:S(2)}) async-start(s32[64,1,32]{2,1,0:T(1,128)} %copy.37), calls=%async_computation | async-start | bytes 65536 | tf_op jit(solution)/shard_map/all_to_all | solution.py:189
  32.0 9.3 %all-to-all-done = s32[64,1,32]{2,1,0:T(1,128)S(1)} async-done(((s32[64,1,32]{2,1,0:T(1,128)}), s32[64,1,32]{2,1,0:T(1,128)S(1)}, u32[]{:S(2)}, u32[]{:S(2)}) %all-to-all-start) | async-done | bytes 8224 | tf_op jit(solution)/shard_map/all_to_all | solution.py:189
  42.6 3.0 %shard_map.102 = bf16[1536,1024]{1,0:T(8,128)(2,1)S(1)} custom-call(s32[1536,1]{1,0:T(8,128)S(1)} %reshape.204.pick, bf16[128,1024]{1,0:T(8,128)(2,1)S(1)} %get-tuple-element.83.refs_0_, bf16[128,1024]{1,0:T(8,128)(2,1)S(1)} %collective-permute-done.3.refs_1_, bf16[128,1024]{1,0:T(8,128)(2,1)S(1)} %collective-permute-done.4.refs_2_, ...), custom_call_target="tpu_custom_call" | custom-call | flops 1610612736 | bytes 4200448 | tf_op jit(solution)/shard_map/pallas_call | solution.py:32
  45.6 1.6 copy-done
  47.2 4.9 %all-to-all-start.1 = ((bf16[64,24,1024]{2,1,0:T(8,128)(2,1)}), bf16[64,24,1024]{2,1,0:T(8,128)(2,1)S(1)}, u32[]{:S(2)}, u32[]{:S(2)}) async-start(bf16[64,24,1024]{2,1,0:T(8,128)(2,1)} %bitcast.115), calls=%async_computation.1 | async-start | bytes 6291456 | tf_op jit(solution)/shard_map/all_to_all | solution.py:219
  52.1 3.1 %constant_dynamic-slice_fusion.8 = (bf16[2,128,1024]{2,1,0:T(8,128)(2,1)}, bf16[2,128,1024]{2,1,0:T(8,128)(2,1)}, bf16[2,128,1024]{2,1,0:T(8,128)(2,1)}, bf16[2,128,1024]{2,1,0:T(8,128)(2,1)}) fusion(bf16[2,128,4096]{2,1,0:T(8,128)(2,1)} %param.13, s32[]{:T(128)S(6)} %select_n.71, s32[]{:T(128)S(6)} %select_n.69, s32[]{:T(128)S(6)} %select_n.68, s32[]{:T(128)S(6)} %select_n.70), kind=kLoop, calls=%fused_computation.72 | loop fusion | bytes 4194320 | tf_op jit(solution)/shard_map/dynamic_slice | solution.py:156
  56.0 1.4 collective-permute-start.7
  57.4 1.1 collective-permute-start.8
  58.5 1.4 constant_dynamic-slice_fusion.4
  60.3 1.6 collective-permute-start.13
  61.8 19.8 %collective-permute-done.6.refs_1_ = bf16[2,128,1024]{2,1,0:T(8,128)(2,1)} collective-permute-done((bf16[2,128,1024]{2,1,0:T(8,128)(2,1)}, bf16[2,128,1024]{2,1,0:T(8,128)(2,1)}, u32[]{:S(2)}, u32[]{:S(2)}) %collective-permute-start.6) | collective-permute-done | bytes 524320 | tf_op jit(solution)/shard_map/ppermute | solution.py:150
  81.8 1.0 copy.46.into
  82.8 20.8 %collective-permute-done.7.refs_2_ = bf16[2,128,1024]{2,1,0:T(8,128)(2,1)} collective-permute-done((bf16[2,128,1024]{2,1,0:T(8,128)(2,1)}, bf16[2,128,1024]{2,1,0:T(8,128)(2,1)}, u32[]{:S(2)}, u32[]{:S(2)}) %collective-permute-start.7) | collective-permute-done | bytes 524320 | tf_op jit(solution)/shard_map/ppermute | solution.py:150
  103.5 0.9 collective-permute-done.8.refs_3_
  104.5 20.4 %all-to-all-done.1 = bf16[64,24,1024]{2,1,0:T(8,128)(2,1)S(1)} async-done(((bf16[64,24,1024]{2,1,0:T(8,128)(2,1)}), bf16[64,24,1024]{2,1,0:T(8,128)(2,1)S(1)}, u32[]{:S(2)}, u32[]{:S(2)}) %all-to-all-start.1) | async-done | bytes 3145760 | tf_op jit(solution)/shard_map/all_to_all | solution.py:219
  124.9 1.0 copy-done.3
  125.9 1.0 copy-done.7
  127.0 6.6 %shard_map.103 = (bf16[1024,1024]{1,0:T(8,128)(2,1)S(1)}, f32[1024,128]{1,0:T(8,128)S(1)}, bf16[1024,128]{1,0:T(8,128)(2,1)S(1)}, bf16[1024,128]{1,0:T(8,128)(2,1)}, bf16[1024,128]{1,0:T(8,128)(2,1)}) custom-call(s32[1024,1]{1,0:T(8,128)S(1)} %copy-done.3, bf16[1536,1024]{1,0:T(8,128)(2,1)S(1)} %bitcast.114, bf16[2,128,1024]{2,1,0:T(8,128)(2,1)S(1)} %copy-done.7, ...), custom_call_target="tpu_custom_call" | custom-call | flops 4294967296 | bytes 8654848 | tf_op jit(solution)/shard_map/pallas_call | solution.py:32
  134.3 1.3 copy-done.11
  136.5 1.4 collective-permute-start.10
  137.9 1.1 collective-permute-start.9
  139.0 5.3 %collective-permute-done.13.refs_6_ = bf16[2,1024,128]{2,1,0:T(8,128)(2,1)} collective-permute-done((bf16[2,1024,128]{2,1,0:T(8,128)(2,1)}, bf16[2,1024,128]{2,1,0:T(8,128)(2,1)}, u32[]{:S(2)}, u32[]{:S(2)}) %collective-permute-start.13) | collective-permute-done | bytes 524320 | tf_op jit(solution)/shard_map/ppermute | solution.py:150
  144.3 6.3 %fusion = f32[2,4,128,128]{3,2,1,0:T(8,128)S(1)} fusion(bf16[4,2,128,4096]{3,2,1,0:T(8,128)(2,1)} %bitcast.118, bf16[2,4096,128]{2,1,0:T(8,128)(2,1)} %param.12), kind=kOutput, calls=%fused_computation | convolution fusion | flops 1073741824 | bytes 11010048 | tf_op jit(solution)/shard_map/gecd,edf->gecf/dot_general | solution.py:223
  150.9 9.6 %collective-permute-start.15 = (bf16[1024,128]{1,0:T(8,128)(2,1)S(1)}, bf16[1024,128]{1,0:T(8,128)(2,1)S(1)}, u32[]{:S(2)}, u32[]{:S(2)}) collective-permute-start(bf16[1024,128]{1,0:T(8,128)(2,1)S(1)} %multiply_convert_fusion.refs_0_), channel_id=1, source_target_pairs={{0,64},{64,128},{128,192},{192,0},{1,65},{65,129},{129,193},{193,1... | collective-permute-start | bytes 786440 | tf_op jit(solution)/shard_map/ppermute | solution.py:150
  160.5 2.5 collective-permute-start.17
  163.2 1.9 collective-permute-done.15.refs_1_
  165.0 5.6 %collective-permute-done.16.refs_2_ = bf16[1024,128]{1,0:T(8,128)(2,1)S(1)} collective-permute-done((bf16[1024,128]{1,0:T(8,128)(2,1)S(1)}, bf16[1024,128]{1,0:T(8,128)(2,1)S(1)}, u32[]{:S(2)}, u32[]{:S(2)}) %collective-permute-start.16) | collective-permute-done | bytes 262176 | tf_op jit(solution)/shard_map/ppermute | solution.py:150
  170.6 1.2 collective-permute-done.17.refs_3_
  172.3 3.3 %collective-permute-start.23 = (f32[2,128]{1,0:T(2,128)S(1)}, f32[2,128]{1,0:T(2,128)S(1)}, u32[]{:S(2)}, u32[]{:S(2)}) collective-permute-start(f32[2,128]{1,0:T(2,128)S(1)} %bitcast.136), channel_id=1, source_target_pairs={{0,64},{64,128},{128,192},{192,0},{1,65},{65,129},{129,193},{193,1... | collective-permute-start | bytes 3080 | tf_op jit(solution)/shard_map/ppermute | solution.py:150
  175.7 1.4 collective-permute-start.19
  177.1 2.0 collective-permute-start.20
  179.1 1.6 collective-permute-start.22
  181.3 1.4 shard_map.104
  185.9 2.1 collective-permute-done.22
  188.0 2.3 collective-permute-done.21
  190.9 8.0 %shard_map.105 = bf16[4,1536,256]{2,1,0:T(8,128)(2,1)} custom-call(s32[1]{0:T(128)} %bitcast.13.me, s32[4,256]{1,0:T(4,128)S(1)} %multiply_add_fusion.place, bf16[1024,128]{1,0:T(8,128)(2,1)S(1)} %get-tuple-element.55.refs_0_, bf16[1024,128]{1,0:T(8,128)(2,1)S(1)} %collective-permute-done.18.refs_1_, bf16[1024,128]{1,0:T(8,128)(2,1)S(1)} %collective-permute-done.19.refs_2_, ...), custom_call_target="tpu_custom_call" | custom-call | flops 4294967296 | bytes 6295556 | tf_op jit(solution)/shard_map/pallas_call | solution.py:32
  198.9 16.6 %all-to-all-start.2 = ((bf16[256,24,256]{2,1,0:T(8,128)(2,1)}), bf16[256,24,256]{2,1,0:T(8,128)(2,1)S(1)}, u32[]{:S(2)}, u32[]{:S(2)}) async-start(bf16[256,24,256]{2,1,0:T(8,128)(2,1)} %bitcast.37), calls=%async_computation.2 | async-start | bytes 6291456 | tf_op jit(solution)/shard_map/all_to_all | solution.py:278
  216.5 2.7 collective-permute-start.24
  220.4 8.1 %fusion.2 = bf16[2,4096,128]{2,1,0:T(8,128)(2,1)} fusion(bf16[4,2,128,4096]{3,2,1,0:T(8,128)(2,1)} %bitcast.119, bf16[1,2,128,128]{3,2,1,0:T(8,128)(2,1)S(1)} %get-tuple-element.89, bf16[1,2,128,128]{3,2,1,0:T(8,128)(2,1)S(1)} %get-tuple-element.90, bf16[1,2,128,128]{3,2,1,0:T(8,128)(2,1)S(1)} %get-tuple-element.91, ...), kind=kOutput, calls=%fused_computation.3 | convolution fusion | flops 1075183616 | bytes 10747904 | tf_op jit(solution)/shard_map/gecd,gecf->edf/dot_general | solution.py:288
  228.5 1.6 broadcast_in_dim.51
  230.9 11.6 %collective-permute-done.24 = bf16[2,128,1024]{2,1,0:T(8,128)(2,1)S(1)} collective-permute-done((bf16[2,128,1024]{2,1,0:T(8,128)(2,1)}, bf16[2,128,1024]{2,1,0:T(8,128)(2,1)S(1)}, u32[]{:S(2)}, u32[]{:S(2)}) %collective-permute-start.24) | collective-permute-done | bytes 524320 | tf_op jit(solution)/shard_map/ppermute | solution.py:150
  243.3 0.9 collective-permute-done.25
  245.1 20.1 %collective-permute-done.26 = bf16[2,128,1024]{2,1,0:T(8,128)(2,1)S(1)} collective-permute-done((bf16[2,128,1024]{2,1,0:T(8,128)(2,1)}, bf16[2,128,1024]{2,1,0:T(8,128)(2,1)S(1)}, u32[]{:S(2)}, u32[]{:S(2)}) %collective-permute-start.26) | collective-permute-done | bytes 524320 | tf_op jit(solution)/shard_map/ppermute | solution.py:150
  266.0 25.2 %all-to-all-done.2 = bf16[256,24,256]{2,1,0:T(8,128)(2,1)S(1)} async-done(((bf16[256,24,256]{2,1,0:T(8,128)(2,1)}), bf16[256,24,256]{2,1,0:T(8,128)(2,1)S(1)}, u32[]{:S(2)}, u32[]{:S(2)}) %all-to-all-start.2) | async-done | bytes 3145760 | tf_op jit(solution)/shard_map/all_to_all | solution.py:278
  291.2 3.4 %shard_map.106 = bf16[128,4096]{1,0:T(8,128)(2,1)} custom-call(s32[1,1536]{1,0:T(1,128)S(1)} %select_n.66.home, bf16[4,1536,256]{2,1,0:T(8,128)(2,1)S(1)} %bitcast.116), custom_call_target="tpu_custom_call" | custom-call | flops 1610612736 | bytes 4200448 | tf_op jit(solution)/shard_map/pallas_call | solution.py:32
  (103 shorter events, 19.2 us)
Async XLA Ops:
  7.2 0.8 copy-start.16
  7.2 5.5 %copy-start.17 = (s32[1,128]{1,0:T(1,128)S(1)}, s32[1,128]{1,0:T(1,128)}, u32[]{:S(2)}) copy-start(s32[1,128]{1,0:T(1,128)} %param.8) | copy-start | bytes 1540
  7.2 5.5 %copy-start.14 = (bf16[1,128,4096]{2,1,0:T(8,128)(2,1)S(1)}, bf16[1,128,4096]{2,1,0:T(8,128)(2,1)}, u32[]{:S(2)}) copy-start(bf16[1,128,4096]{2,1,0:T(8,128)(2,1)} %param.7) | copy-start | bytes 3145732
  7.2 137.0 %all-gather.2.cloned.1.call-start = ((), (), s32[]{:S(2)}) async-start(), calls=%async_computation.3 | async-start | bytes 10485760 | tf_op jit(solution)/shard_map/all_gather | solution.py:170
  8.0 9.3 %collective-permute-start.2 = (f32[2,256]{1,0:T(2,128)S(1)}, f32[2,256]{1,0:T(2,128)S(1)}, u32[]{:S(2)}, u32[]{:S(2)}) collective-permute-start(f32[2,256]{1,0:T(2,128)S(1)} %get-tuple-element.97), channel_id=1, source_target_pairs={{0,192},{64,0},{128,64},{192,128},{1,193},{65,1},{129,65},{193,129... | collective-permute-start | bytes 6152 | tf_op jit(solution)/shard_map/ppermute | solution.py:150
  11.6 4.7 %collective-permute-start.1 = (f32[2,256]{1,0:T(2,128)S(1)}, f32[2,256]{1,0:T(2,128)S(1)}, u32[]{:S(2)}, u32[]{:S(2)}) collective-permute-start(f32[2,256]{1,0:T(2,128)S(1)} %get-tuple-element.97), channel_id=1, source_target_pairs={{0,128},{64,192},{128,0},{192,64},{1,129},{65,193},{129,1},{193,65... | collective-permute-start | bytes 6152 | tf_op jit(solution)/shard_map/ppermute | solution.py:150
  12.0 5.3 %collective-permute-start = (f32[2,256]{1,0:T(2,128)S(1)}, f32[2,256]{1,0:T(2,128)S(1)}, u32[]{:S(2)}, u32[]{:S(2)}) collective-permute-start(f32[2,256]{1,0:T(2,128)S(1)} %get-tuple-element.97), channel_id=1, source_target_pairs={{0,64},{64,128},{128,192},{192,0},{1,65},{65,129},{129,193},{193,1... | collective-permute-start | bytes 6152 | tf_op jit(solution)/shard_map/ppermute | solution.py:150
  13.1 29.5 %collective-permute-start.3 = (bf16[128,1024]{1,0:T(8,128)(2,1)S(1)}, bf16[128,1024]{1,0:T(8,128)(2,1)S(1)}, u32[]{:S(2)}, u32[]{:S(2)}) collective-permute-start(bf16[128,1024]{1,0:T(8,128)(2,1)S(1)} %get-tuple-element.82), channel_id=1, source_target_pairs={{0,64},{64,128},{128,192},{192,0},{1,65},{65,129},{129,193},{193,1... | collective-permute-start | bytes 786440 | tf_op jit(solution)/shard_map/ppermute | solution.py:150
  14.7 27.8 %collective-permute-start.4 = (bf16[128,1024]{1,0:T(8,128)(2,1)S(1)}, bf16[128,1024]{1,0:T(8,128)(2,1)S(1)}, u32[]{:S(2)}, u32[]{:S(2)}) collective-permute-start(bf16[128,1024]{1,0:T(8,128)(2,1)S(1)} %get-tuple-element.81), channel_id=1, source_target_pairs={{0,128},{64,192},{128,0},{192,64},{1,129},{65,193},{129,1},{193,65... | collective-permute-start | bytes 786440 | tf_op jit(solution)/shard_map/ppermute | solution.py:150
  16.3 26.3 %collective-permute-start.5 = (bf16[128,1024]{1,0:T(8,128)(2,1)S(1)}, bf16[128,1024]{1,0:T(8,128)(2,1)S(1)}, u32[]{:S(2)}, u32[]{:S(2)}) collective-permute-start(bf16[128,1024]{1,0:T(8,128)(2,1)S(1)} %get-tuple-element.80), channel_id=1, source_target_pairs={{0,192},{64,0},{128,64},{192,128},{1,193},{65,1},{129,65},{193,129... | collective-permute-start | bytes 786440 | tf_op jit(solution)/shard_map/ppermute | solution.py:150
  18.5 22.9 %all-to-all-start = ((s32[64,1,32]{2,1,0:T(1,128)}), s32[64,1,32]{2,1,0:T(1,128)S(1)}, u32[]{:S(2)}, u32[]{:S(2)}) async-start(s32[64,1,32]{2,1,0:T(1,128)} %copy.37), calls=%async_computation | async-start | bytes 65536 | tf_op jit(solution)/shard_map/all_to_all | solution.py:189
  45.6 1.6 copy-start
  47.2 77.6 %all-to-all-start.1 = ((bf16[64,24,1024]{2,1,0:T(8,128)(2,1)}), bf16[64,24,1024]{2,1,0:T(8,128)(2,1)S(1)}, u32[]{:S(2)}, u32[]{:S(2)}) async-start(bf16[64,24,1024]{2,1,0:T(8,128)(2,1)} %bitcast.115), calls=%async_computation.1 | async-start | bytes 6291456 | tf_op jit(solution)/shard_map/all_to_all | solution.py:219
  52.1 6.4 %copy-start.13 = (bf16[2,4096,128]{2,1,0:T(8,128)(2,1)S(1)}, bf16[2,4096,128]{2,1,0:T(8,128)(2,1)}, u32[]{:S(2)}) copy-start(bf16[2,4096,128]{2,1,0:T(8,128)(2,1)} %param.12) | copy-start | bytes 6291460
  55.2 26.5 %collective-permute-start.6 = (bf16[2,128,1024]{2,1,0:T(8,128)(2,1)}, bf16[2,128,1024]{2,1,0:T(8,128)(2,1)}, u32[]{:S(2)}, u32[]{:S(2)}) collective-permute-start(bf16[2,128,1024]{2,1,0:T(8,128)(2,1)} %get-tuple-element.75), channel_id=1, source_target_pairs={{0,64},{64,128},{128,192},{192,0},{1,65},{65,129},{129,193},{193,1... | collective-permute-start | bytes 1572872 | tf_op jit(solution)/shard_map/ppermute | solution.py:150
  56.0 47.5 %collective-permute-start.7 = (bf16[2,128,1024]{2,1,0:T(8,128)(2,1)}, bf16[2,128,1024]{2,1,0:T(8,128)(2,1)}, u32[]{:S(2)}, u32[]{:S(2)}) collective-permute-start(bf16[2,128,1024]{2,1,0:T(8,128)(2,1)} %get-tuple-element.77), channel_id=1, source_target_pairs={{0,128},{64,192},{128,0},{192,64},{1,129},{65,193},{129,1},{193,65... | collective-permute-start | bytes 1572872 | tf_op jit(solution)/shard_map/ppermute | solution.py:150
  57.4 47.1 %collective-permute-start.8 = (bf16[2,128,1024]{2,1,0:T(8,128)(2,1)}, bf16[2,128,1024]{2,1,0:T(8,128)(2,1)}, u32[]{:S(2)}, u32[]{:S(2)}) collective-permute-start(bf16[2,128,1024]{2,1,0:T(8,128)(2,1)} %get-tuple-element.74), channel_id=1, source_target_pairs={{0,192},{64,0},{128,64},{192,128},{1,193},{65,1},{129,65},{193,129... | collective-permute-start | bytes 1572872 | tf_op jit(solution)/shard_map/ppermute | solution.py:150
  59.9 78.0 %collective-permute-start.12 = (bf16[2,1024,128]{2,1,0:T(8,128)(2,1)}, bf16[2,1024,128]{2,1,0:T(8,128)(2,1)}, u32[]{:S(2)}, u32[]{:S(2)}) collective-permute-start(bf16[2,1024,128]{2,1,0:T(8,128)(2,1)} %get-tuple-element.72), channel_id=1, source_target_pairs={{0,64},{64,128},{128,192},{192,0},{1,65},{65,129},{129,193},{193,1... | collective-permute-start | bytes 1572872 | tf_op jit(solution)/shard_map/ppermute | solution.py:150
  60.3 84.0 %collective-permute-start.13 = (bf16[2,1024,128]{2,1,0:T(8,128)(2,1)}, bf16[2,1024,128]{2,1,0:T(8,128)(2,1)}, u32[]{:S(2)}, u32[]{:S(2)}) collective-permute-start(bf16[2,1024,128]{2,1,0:T(8,128)(2,1)} %get-tuple-element.71), channel_id=1, source_target_pairs={{0,128},{64,192},{128,0},{192,64},{1,129},{65,193},{129,1},{193,65... | collective-permute-start | bytes 1572872 | tf_op jit(solution)/shard_map/ppermute | solution.py:150
  81.7 62.6 %collective-permute-start.14 = (bf16[2,1024,128]{2,1,0:T(8,128)(2,1)}, bf16[2,1024,128]{2,1,0:T(8,128)(2,1)}, u32[]{:S(2)}, u32[]{:S(2)}) collective-permute-start(bf16[2,1024,128]{2,1,0:T(8,128)(2,1)} %get-tuple-element.70), channel_id=1, source_target_pairs={{0,192},{64,0},{128,64},{192,128},{1,193},{65,1},{129,65},{193,129... | collective-permute-start | bytes 1572872 | tf_op jit(solution)/shard_map/ppermute | solution.py:150
  124.9 1.0 copy-start.3
  125.9 1.0 copy-start.7
  133.5 0.8 copy-start.1
  134.3 1.3 copy-start.11
  135.7 24.9 %collective-permute-start.11 = (bf16[1024,128]{1,0:T(8,128)(2,1)}, bf16[1024,128]{1,0:T(8,128)(2,1)S(1)}, u32[]{:S(2)}, u32[]{:S(2)}) collective-permute-start(bf16[1024,128]{1,0:T(8,128)(2,1)} %get-tuple-element.39), channel_id=1, source_target_pairs={{0,64},{64,128},{128,192},{192,0},{1,65},{65,129},{129,193},{193,1... | collective-permute-start | bytes 786440 | tf_op jit(solution)/shard_map/ppermute | solution.py:150
  136.5 26.6 %collective-permute-start.10 = (bf16[1024,128]{1,0:T(8,128)(2,1)}, bf16[1024,128]{1,0:T(8,128)(2,1)S(1)}, u32[]{:S(2)}, u32[]{:S(2)}) collective-permute-start(bf16[1024,128]{1,0:T(8,128)(2,1)} %get-tuple-element.38), channel_id=1, source_target_pairs={{0,128},{64,192},{128,0},{192,64},{1,129},{65,193},{129,1},{193,65... | collective-permute-start | bytes 786440 | tf_op jit(solution)/shard_map/ppermute | solution.py:150
  137.9 25.1 %collective-permute-start.9 = (bf16[1024,128]{1,0:T(8,128)(2,1)S(1)}, bf16[1024,128]{1,0:T(8,128)(2,1)S(1)}, u32[]{:S(2)}, u32[]{:S(2)}) collective-permute-start(bf16[1024,128]{1,0:T(8,128)(2,1)S(1)} %get-tuple-element.37), channel_id=1, source_target_pairs={{0,192},{64,0},{128,64},{192,128},{1,193},{65,1},{129,65},{193,129... | collective-permute-start | bytes 786440 | tf_op jit(solution)/shard_map/ppermute | solution.py:150
  150.6 12.5 %copy-start.2 = (f32[1024,128]{1,0:T(8,128)S(1)}, f32[1024,128]{1,0:T(8,128)}, u32[]{:S(2)}) copy-start(f32[1024,128]{1,0:T(8,128)} %copy-done.1) | copy-start | bytes 1572868
  150.7 30.6 %copy-start.12 = (bf16[1024,1024]{1,0:T(8,128)(2,1)S(1)}, bf16[1024,1024]{1,0:T(8,128)(2,1)}, u32[]{:S(2)}) copy-start(bf16[1024,1024]{1,0:T(8,128)(2,1)} %copy-done.11) | copy-start | bytes 6291460
  150.9 14.1 %collective-permute-start.15 = (bf16[1024,128]{1,0:T(8,128)(2,1)S(1)}, bf16[1024,128]{1,0:T(8,128)(2,1)S(1)}, u32[]{:S(2)}, u32[]{:S(2)}) collective-permute-start(bf16[1024,128]{1,0:T(8,128)(2,1)S(1)} %multiply_convert_fusion.refs_0_), channel_id=1, source_target_pairs={{0,64},{64,128},{128,192},{192,0},{1,65},{65,129},{129,193},{193,1... | collective-permute-start | bytes 786440 | tf_op jit(solution)/shard_map/ppermute | solution.py:150
  160.5 10.1 %collective-permute-start.16 = (bf16[1024,128]{1,0:T(8,128)(2,1)S(1)}, bf16[1024,128]{1,0:T(8,128)(2,1)S(1)}, u32[]{:S(2)}, u32[]{:S(2)}) collective-permute-start(bf16[1024,128]{1,0:T(8,128)(2,1)S(1)} %multiply_convert_fusion.refs_0_), channel_id=1, source_target_pairs={{0,128},{64,192},{128,0},{192,64},{1,129},{65,193},{129,1},{193,65... | collective-permute-start | bytes 786440 | tf_op jit(solution)/shard_map/ppermute | solution.py:150
  160.5 11.3 %collective-permute-start.17 = (bf16[1024,128]{1,0:T(8,128)(2,1)S(1)}, bf16[1024,128]{1,0:T(8,128)(2,1)S(1)}, u32[]{:S(2)}, u32[]{:S(2)}) collective-permute-start(bf16[1024,128]{1,0:T(8,128)(2,1)S(1)} %multiply_convert_fusion.refs_0_), channel_id=1, source_target_pairs={{0,192},{64,0},{128,64},{192,128},{1,193},{65,1},{129,65},{193,129... | collective-permute-start | bytes 786440 | tf_op jit(solution)/shard_map/ppermute | solution.py:150
  172.3 18.6 %copy-start.6 = (bf16[2,1024,128]{2,1,0:T(8,128)(2,1)S(1)}, bf16[2,1024,128]{2,1,0:T(8,128)(2,1)}, u32[]{:S(2)}) copy-start(bf16[2,1024,128]{2,1,0:T(8,128)(2,1)} %get-tuple-element.59.refs_4_) | copy-start | bytes 1572868
  172.3 8.4 %collective-permute-start.23 = (f32[2,128]{1,0:T(2,128)S(1)}, f32[2,128]{1,0:T(2,128)S(1)}, u32[]{:S(2)}, u32[]{:S(2)}) collective-permute-start(f32[2,128]{1,0:T(2,128)S(1)} %bitcast.136), channel_id=1, source_target_pairs={{0,64},{64,128},{128,192},{192,0},{1,65},{65,129},{129,193},{193,1... | collective-permute-start | bytes 3080 | tf_op jit(solution)/shard_map/ppermute | solution.py:150
  175.6 15.2 %collective-permute-start.18 = (bf16[1024,128]{1,0:T(8,128)(2,1)S(1)}, bf16[1024,128]{1,0:T(8,128)(2,1)S(1)}, u32[]{:S(2)}, u32[]{:S(2)}) collective-permute-start(bf16[1024,128]{1,0:T(8,128)(2,1)S(1)} %get-tuple-element.55.refs_0_), channel_id=1, source_target_pairs={{0,64},{64,128},{128,192},{192,0},{1,65},{65,129},{129,193},{193,1... | collective-permute-start | bytes 786440 | tf_op jit(solution)/shard_map/ppermute | solution.py:150
  175.7 15.1 %collective-permute-start.19 = (bf16[1024,128]{1,0:T(8,128)(2,1)S(1)}, bf16[1024,128]{1,0:T(8,128)(2,1)S(1)}, u32[]{:S(2)}, u32[]{:S(2)}) collective-permute-start(bf16[1024,128]{1,0:T(8,128)(2,1)S(1)} %get-tuple-element.55.refs_0_), channel_id=1, source_target_pairs={{0,128},{64,192},{128,0},{192,64},{1,129},{65,193},{129,1},{193,65... | collective-permute-start | bytes 786440 | tf_op jit(solution)/shard_map/ppermute | solution.py:150
  177.1 13.8 %collective-permute-start.20 = (bf16[1024,128]{1,0:T(8,128)(2,1)S(1)}, bf16[1024,128]{1,0:T(8,128)(2,1)S(1)}, u32[]{:S(2)}, u32[]{:S(2)}) collective-permute-start(bf16[1024,128]{1,0:T(8,128)(2,1)S(1)} %get-tuple-element.55.refs_0_), channel_id=1, source_target_pairs={{0,192},{64,0},{128,64},{192,128},{1,193},{65,1},{129,65},{193,129... | collective-permute-start | bytes 786440 | tf_op jit(solution)/shard_map/ppermute | solution.py:150
  179.1 8.9 %collective-permute-start.22 = (f32[2,128]{1,0:T(2,128)S(1)}, f32[2,128]{1,0:T(2,128)S(1)}, u32[]{:S(2)}, u32[]{:S(2)}) collective-permute-start(f32[2,128]{1,0:T(2,128)S(1)} %bitcast.135), channel_id=1, source_target_pairs={{0,128},{64,192},{128,0},{192,64},{1,129},{65,193},{129,1},{193,65... | collective-permute-start | bytes 3080 | tf_op jit(solution)/shard_map/ppermute | solution.py:150
  180.7 9.6 %collective-permute-start.21 = (f32[2,128]{1,0:T(2,128)S(1)}, f32[2,128]{1,0:T(2,128)S(1)}, u32[]{:S(2)}, u32[]{:S(2)}) collective-permute-start(f32[2,128]{1,0:T(2,128)S(1)} %bitcast.134), channel_id=1, source_target_pairs={{0,192},{64,0},{128,64},{192,128},{1,193},{65,1},{129,65},{193,129... | collective-permute-start | bytes 3080 | tf_op jit(solution)/shard_map/ppermute | solution.py:150
  182.6 0.8 copy-start.4
  183.4 0.8 copy-start.8
  184.3 0.8 copy-start.9
  185.1 0.8 copy-start.10
  198.9 92.4 %all-to-all-start.2 = ((bf16[256,24,256]{2,1,0:T(8,128)(2,1)}), bf16[256,24,256]{2,1,0:T(8,128)(2,1)S(1)}, u32[]{:S(2)}, u32[]{:S(2)}) async-start(bf16[256,24,256]{2,1,0:T(8,128)(2,1)} %bitcast.37), calls=%async_computation.2 | async-start | bytes 6291456 | tf_op jit(solution)/shard_map/all_to_all | solution.py:278
  216.5 25.9 %collective-permute-start.24 = (bf16[2,128,1024]{2,1,0:T(8,128)(2,1)}, bf16[2,128,1024]{2,1,0:T(8,128)(2,1)S(1)}, u32[]{:S(2)}, u32[]{:S(2)}) collective-permute-start(bf16[2,128,1024]{2,1,0:T(8,128)(2,1)} %copy-done.10), channel_id=1, source_target_pairs={{0,192},{64,0},{128,64},{192,128},{1,193},{65,1},{129,65},{193,129... | collective-permute-start | bytes 1572872 | tf_op jit(solution)/shard_map/ppermute | solution.py:150
  219.3 25.0 %collective-permute-start.25 = (bf16[2,128,1024]{2,1,0:T(8,128)(2,1)}, bf16[2,128,1024]{2,1,0:T(8,128)(2,1)S(1)}, u32[]{:S(2)}, u32[]{:S(2)}) collective-permute-start(bf16[2,128,1024]{2,1,0:T(8,128)(2,1)} %copy-done.9), channel_id=1, source_target_pairs={{0,128},{64,192},{128,0},{192,64},{1,129},{65,193},{129,1},{193,65... | collective-permute-start | bytes 1572872 | tf_op jit(solution)/shard_map/ppermute | solution.py:150
  219.8 45.4 %collective-permute-start.26 = (bf16[2,128,1024]{2,1,0:T(8,128)(2,1)}, bf16[2,128,1024]{2,1,0:T(8,128)(2,1)S(1)}, u32[]{:S(2)}, u32[]{:S(2)}) collective-permute-start(bf16[2,128,1024]{2,1,0:T(8,128)(2,1)} %copy-done.8), channel_id=1, source_target_pairs={{0,64},{64,128},{128,192},{192,0},{1,65},{65,129},{129,193},{193,1... | collective-permute-start | bytes 1572872 | tf_op jit(solution)/shard_map/ppermute | solution.py:150
  228.5 1.6 copy-start.5
  (1 other events, 0.8 us)
Sparse Core Ops, SparseCore 0:
  9.8 132.3 all-gather.1

commit v2 on v1

--- a/solution.py
+++ b/solution.py
@@ -44,6 +44,15 @@
     )(*args)
 
 
+def column(rows):
+    size = rows.shape[1]
+    eye = lax.broadcasted_iota(jnp.int32, (size, size), 0) == lax.broadcasted_iota(jnp.int32, (size, size), 1)
+    parts = [
+        jnp.sum(jnp.where(eye, rows[k : k + 1], 0), axis=1, keepdims=True) for k in range(rows.shape[0])
+    ]
+    return jnp.concatenate(parts, axis=0)
+
+
 def pack_kernel(n, tok, pick, *refs):
     blocks, sent, held = refs[:n], refs[n], refs[n + 1]
 
@@ -63,7 +72,7 @@
     for s in range(n):
         wide[s * share : (s + 1) * share] = ws[s][0]
     ids = lax.broadcasted_iota(jnp.int32, (n * cap, got.shape[0]), 1)
-    onehot = jnp.where(into[...] == ids, 1.0, 0.0).astype(BF16)
+    onehot = jnp.where(column(into[0]) == ids, 1.0, 0.0).astype(BF16)
     up[...] = dot(onehot, got[...], ((1,), (0,))).astype(BF16)
     part = dot(up[...], wide[...], ((1,), (1,)))
     for s in range(n):
@@ -93,14 +102,21 @@
             for g in range(n):
                 back[g, e * cap : (e + 1) * cap] = mine[g * cap : (g + 1) * cap]
 
-    where = place[pl.ds(p, 1)]
-    for t in range(2):
-        ids = lax.broadcasted_iota(jnp.int32, (step, experts * cap), 0) + t * step
-        total = jnp.zeros((step, thin), F32)
-        for b in range(n):
-            onehot = jnp.where(ids == where + b * PEER, 1.0, 0.0).astype(BF16)
-            total = total + dot(onehot, back[p, :, b * thin : (b + 1) * thin], ((1,), (0,)))
-        out[0, t * step : (t + 1) * step] = total.astype(BF16)
+    owners = out.shape[1] // (n * PEER)
+    ids = lax.broadcasted_iota(jnp.int32, (owners * 8, experts * cap), 0)
+    onehot = jnp.where(ids == place[pl.ds(p, 1)], 1.0, 0.0).astype(BF16)
+    full = dot(onehot, back[p], ((1,), (0,))).reshape(owners, 8, width)
+    row = lax.broadcasted_iota(jnp.int32, (owners, 8, thin), 1)
+    first = full[:, :, :thin]
+    second = pltpu.roll(full[:, :, thin : 2 * thin], 6, 1)
+    third = pltpu.roll(full[:, :, 2 * thin : 3 * thin], 4, 1)
+    fourth = pltpu.roll(full[:, :, 3 * thin :], 2, 1)
+    tiles = [
+        jnp.where(row < 6, first, second),
+        jnp.where(row < 4, second, third),
+        jnp.where(row < 2, third, fourth),
+    ]
+    out[0] = jnp.concatenate(tiles, axis=1).reshape(owners * n * PEER, thin).astype(BF16)
 
 
 def grad_out_kernel(n, cap, *refs):
@@ -196,11 +212,12 @@
     place = source * rows + rank
     scale = facts[:, 0].reshape(n, experts, cap).transpose(1, 0, 2).reshape(every, 1)
     into = place + jnp.arange(n, dtype=jnp.int32)[:, None] * PEER
-    into = into.reshape(n, experts, cap).transpose(1, 0, 2).reshape(every, 1)
+    into = into.reshape(n, experts, cap).transpose(1, 0, 2)
 
     own_out = [columns(w_out, s) for s in range(n)]
     own_in = [lax.dynamic_slice_in_dim(w_in, at(s) * quarter, quarter, axis=1) for s in range(n)]
     w_out_all = forward(own_out)
+    own_in, w_out_all = lax.optimization_barrier((own_in, w_out_all))
     w_in_all = forward(own_in)
     inputs, w_in_all = lax.optimization_barrier((inputs, w_in_all))
 
@@ -225,7 +242,7 @@
     normal_cdf = 0.5 * (1.0 + lax.erf(pre * SQRT_HALF))
     slope = scale * (normal_cdf + pre * jnp.exp(-0.5 * pre * pre) * INV_ROOT_TWO_PI)
     hidden = pre * normal_cdf
-    hidden_all = forward([(scale * hidden).astype(BF16)] * n)
+    scaled = (scale * hidden).astype(BF16)
     hidden = hidden.astype(BF16)
 
     partials = [((every, share), F32)] + [((every, share), BF16)] * (n - 1)
@@ -233,7 +250,7 @@
         functools.partial(project_kernel, n, cap),
         [((every, quarter), BF16)] + partials,
         [into, got.reshape(owners * rows, quarter), *w_out_all],
-        [pl.BlockSpec((n * cap, 1), lambda e: (e, 0)), whole((owners * rows, quarter))]
+        [pl.BlockSpec((1, n, cap), lambda e: (e, 0, 0)), whole((owners * rows, quarter))]
         + [pl.BlockSpec((1, share, quarter), lambda e: (e, 0, 0))] * n,
         [pl.BlockSpec((n * cap, quarter), lambda e: (e, 0))]
         + [pl.BlockSpec((n * cap, share), lambda e: (e, 0))] * n,
@@ -242,27 +259,13 @@
         flops=2 * every * quarter * (n * share + owners * rows),
     )
     project = reduced(partial)
-    project, hidden_all = lax.optimization_barrier((project, hidden_all))
     gate = jnp.sum(hidden.astype(F32) * project, axis=1).reshape(experts, n, cap)
-    gate = reduced([gate[:, p] for p in range(n)])
     pre_grad = forward([(project * slope).astype(BF16)] * n)
-    pre_grad, gate = lax.optimization_barrier((pre_grad, gate))
-    gate_grad = gate.reshape(1, experts, cap)
-
-    out_blocks = call(
-        functools.partial(grad_out_kernel, n, cap),
-        [((experts, share, quarter), BF16)] * n,
-        [*hidden_all, up],
-        scratch=[pltpu.VMEM((every, n * share), BF16)],
-        flops=2 * every * quarter * n * share,
-    )
-    pre_grad, out_blocks = lax.optimization_barrier((pre_grad, out_blocks))
-    out_blocks = backward(out_blocks)
 
     (outgoing,) = call(
         functools.partial(back_kernel, n, cap),
         [((n, owners * rows, thin), BF16)],
-        [me.reshape(1), place, *pre_grad, *w_in_all],
+        [me.reshape(1), source * 8 + rank, *pre_grad, *w_in_all],
         out_specs=[
             pl.BlockSpec((1, owners * rows, thin), lambda p, m: (lax.rem(m[0] + n - p, n), 0, 0))
         ],
@@ -283,6 +286,20 @@
         tiled=True,
     )
 
+    scaled, gate, pre_grad = lax.optimization_barrier((scaled, gate, pre_grad))
+    hidden_all = forward([scaled] * n)
+    gate = reduced([gate[:, p] for p in range(n)])
+    hidden_all, gate = lax.optimization_barrier((hidden_all, gate))
+    gate_grad = gate.reshape(1, experts, cap)
+    out_blocks = call(
+        functools.partial(grad_out_kernel, n, cap),
+        [((experts, share, quarter), BF16)] * n,
+        [*hidden_all, up],
+        scratch=[pltpu.VMEM((every, n * share), BF16)],
+        flops=2 * every * quarter * n * share,
+    )
+    out_blocks = backward(out_blocks)
+
     own_grad = pre_grad[0].reshape(experts, n, cap, share).transpose(1, 0, 2, 3)
     own_grad = jnp.stack(turned(own_grad))
     w_in_grad = jnp.einsum("gecd,gecf->edf", inputs, own_grad, preferred_element_type=F32).astype(BF16)

time: 302 us -> 281 us (0.930)
  waiting for transfers between devices: 148 us -> 136 us
  starting transfers between devices: 77.4 us -> 69 us
    all_to_all x1, waiting for transfers between devices: 25.2 us -> 0.01 us  [shards(): lax.all_to_all(outgoing.reshape(n * owners, rows, thin), ('dp', 'expert')...]
    ppermute x27, waiting for transfers between devices: 92.7 us -> 111 us  [shift(): return lax.ppermute(x, 'dp', [(a, (a + s) % n) for a in range(n)])]
    ppermute x27, starting transfers between devices: 42.4 us -> 36.5 us  [shift(): return lax.ppermute(x, 'dp', [(a, (a + s) % n) for a in range(n)])]
    all_to_all x1, waiting for transfers between devices: 20.4 us -> 15.9 us  [shards(): lax.all_to_all(sent.reshape(owners, rows, quarter), 'expert', split_axis=...]
    unnamed x36 -> x26, local copies, waits for them, and re-layouts: 9.06 us -> 7.33 us
  transfers between devices with their start and end apart: 31 -> 31, of which waited for: 15 -> 13; matrix products, arithmetic and copies ran while one was open for 10% -> 11% of each run, Pallas kernels for 4% -> 4%
where the time goes in v2:
time: 281 us; the launch traced here: 280 us
  waiting for transfers between devices  136 us (48%)
  starting transfers between devices  69 us (25%)
  local copies, waits for them, and re-layouts  21.1 us (8%)
  Pallas kernels  21 us (7%)
  matrix products  14.8 us (5%)
  between operations  14.4 us (5%)
  other arithmetic  3.43 us (1%)
    ppermute x27, waiting for transfers between devices, shift(): return lax.ppermute(x, 'dp', [(a, (a + s) % n) for a in range(n)])  111 us
    ppermute x27, starting transfers between devices, shift(): return lax.ppermute(x, 'dp', [(a, (a + s) % n) for a in range(n)])  36.5 us
    pallas_call x5, Pallas kernels, call(): pl.pallas_call(kernel, out_shape=shapes, grid_spec=pltpu.PrefetchScalarGr...  21 us
    all_to_all x1, waiting for transfers between devices, shards(): lax.all_to_all(sent.reshape(owners, rows, quarter), 'expert', split_axis=...  15.9 us
    all_to_all x1, starting transfers between devices, shards(): lax.all_to_all(outgoing.reshape(n * owners, rows, thin), ('dp', 'expert')...  14.1 us
    all_to_all x1, starting transfers between devices, shards(): lax.all_to_all(request, 'expert', split_axis=0, concat_axis=0, tiled=True)  13.6 us
    all_to_all x1, waiting for transfers between devices, shards(): lax.all_to_all(request, 'expert', split_axis=0, concat_axis=0, tiled=True)  9.29 us
    dot_general x1, matrix products, shards(): jnp.einsum('gecd,gecf->edf', inputs, own_grad, preferred_element_type=F32)  8.07 us
  transfers between devices with their start and end apart: 31, of which 13 were waited for; matrix products, arithmetic and copies ran while one was open for 11% of the time, Pallas kernels for 4%

profile of v2, /device:TPU:1, one launch (start us, length us, event | category | flops | bytes accessed | tf_op | source)
XLA Modules:
  0.0 280.2 jit_solution(10463206600979234804)
XLA Ops:
  8.0 2.2 collective-permute-start
  10.2 2.6 collective-permute-start.1
  12.8 1.1 collective-permute-start.2
  15.6 1.7 collective-permute-start.5
  18.5 13.6 %all-to-all-start = ((s32[64,1,32]{2,1,0:T(1,128)}), s32[64,1,32]{2,1,0:T(1,128)S(1)}, u32[]{:S(2)}, u32[]{:S(2)}) async-start(s32[64,1,32]{2,1,0:T(1,128)} %copy.39), calls=%async_computation | async-start | bytes 65536 | tf_op jit(solution)/shard_map/all_to_all | solution.py:205
  32.1 9.3 %all-to-all-done = s32[64,1,32]{2,1,0:T(1,128)S(1)} async-done(((s32[64,1,32]{2,1,0:T(1,128)}), s32[64,1,32]{2,1,0:T(1,128)S(1)}, u32[]{:S(2)}, u32[]{:S(2)}) %all-to-all-start) | async-done | bytes 8224 | tf_op jit(solution)/shard_map/all_to_all | solution.py:205
  42.6 3.0 %shard_map.102 = bf16[1536,1024]{1,0:T(8,128)(2,1)S(1)} custom-call(s32[1536,1]{1,0:T(8,128)S(1)} %reshape.200.pick, bf16[128,1024]{1,0:T(8,128)(2,1)S(1)} %get-tuple-element.79.refs_0_, bf16[128,1024]{1,0:T(8,128)(2,1)S(1)} %collective-permute-done.3.refs_1_, bf16[128,1024]{1,0:T(8,128)(2,1)S(1)} %collective-permute-done.4.refs_2_, ...), custom_call_target="tpu_custom_call" | custom-call | flops 1610612736 | bytes 4200448 | tf_op jit(solution)/shard_map/pallas_call | solution.py:32
  45.7 1.6 copy-done
  47.3 4.8 %all-to-all-start.1 = ((bf16[64,24,1024]{2,1,0:T(8,128)(2,1)}), bf16[64,24,1024]{2,1,0:T(8,128)(2,1)S(1)}, u32[]{:S(2)}, u32[]{:S(2)}) async-start(bf16[64,24,1024]{2,1,0:T(8,128)(2,1)} %bitcast.118), calls=%async_computation.1 | async-start | bytes 6291456 | tf_op jit(solution)/shard_map/all_to_all | solution.py:236
  52.1 3.0 %constant_dynamic-slice_fusion.4 = (bf16[2,128,1024]{2,1,0:T(8,128)(2,1)}, bf16[2,128,1024]{2,1,0:T(8,128)(2,1)}, bf16[2,128,1024]{2,1,0:T(8,128)(2,1)}, bf16[2,128,1024]{2,1,0:T(8,128)(2,1)}) fusion(bf16[2,128,4096]{2,1,0:T(8,128)(2,1)} %param.13, s32[]{:T(128)S(6)} %select_n.71, s32[]{:T(128)S(6)} %select_n.69, s32[]{:T(128)S(6)} %select_n.68, s32[]{:T(128)S(6)} %select_n.70), kind=kLoop, calls=%fused_computation.68 | loop fusion | bytes 4194320 | tf_op jit(solution)/shard_map/dynamic_slice | solution.py:172
  55.5 2.0 collective-permute-start.7
  57.5 2.1 collective-permute-start.8
  59.6 2.9 %constant_dynamic-slice_fusion.8 = (bf16[2,1024,128]{2,1,0:T(8,128)(2,1)}, bf16[2,1024,128]{2,1,0:T(8,128)(2,1)}, bf16[2,1024,128]{2,1,0:T(8,128)(2,1)}, bf16[2,1024,128]{2,1,0:T(8,128)(2,1)}) fusion(bf16[2,4096,128]{2,1,0:T(8,128)(2,1)} %param.12, s32[]{:T(128)S(6)} %select_n.71, s32[]{:T(128)S(6)} %select_n.70, s32[]{:T(128)S(6)} %select_n.69, s32[]{:T(128)S(6)} %select_n.68), kind=kLoop, calls=%fused_computation.72 | loop fusion | bytes 4194320 | tf_op jit(solution)/shard_map/dynamic_slice | solution.py:218
  62.5 19.0 %collective-permute-done.6.refs_1_ = bf16[2,128,1024]{2,1,0:T(8,128)(2,1)} collective-permute-done((bf16[2,128,1024]{2,1,0:T(8,128)(2,1)}, bf16[2,128,1024]{2,1,0:T(8,128)(2,1)}, u32[]{:S(2)}, u32[]{:S(2)}) %collective-permute-start.6) | collective-permute-done | bytes 524320 | tf_op jit(solution)/shard_map/ppermute | solution.py:166
  81.5 22.2 %collective-permute-done.7.refs_2_ = bf16[2,128,1024]{2,1,0:T(8,128)(2,1)} collective-permute-done((bf16[2,128,1024]{2,1,0:T(8,128)(2,1)}, bf16[2,128,1024]{2,1,0:T(8,128)(2,1)}, u32[]{:S(2)}, u32[]{:S(2)}) %collective-permute-start.7) | collective-permute-done | bytes 524320 | tf_op jit(solution)/shard_map/ppermute | solution.py:166
  104.4 2.4 collective-permute-start.13
  106.8 2.1 collective-permute-start.14
  109.0 15.9 %all-to-all-done.1 = bf16[64,24,1024]{2,1,0:T(8,128)(2,1)S(1)} async-done(((bf16[64,24,1024]{2,1,0:T(8,128)(2,1)}), bf16[64,24,1024]{2,1,0:T(8,128)(2,1)S(1)}, u32[]{:S(2)}, u32[]{:S(2)}) %all-to-all-start.1) | async-done | bytes 3145760 | tf_op jit(solution)/shard_map/all_to_all | solution.py:236
  124.9 1.0 copy-done.4
  125.9 7.1 %shard_map.103 = (bf16[1024,1024]{1,0:T(8,128)(2,1)S(1)}, f32[1024,128]{1,0:T(8,128)S(1)}, bf16[1024,128]{1,0:T(8,128)(2,1)S(1)}, bf16[1024,128]{1,0:T(8,128)(2,1)}, bf16[1024,128]{1,0:T(8,128)(2,1)}) custom-call(s32[2,4,128]{2,1,0:T(4,128)S(1)} %add_bitcast_fusion.into, bf16[1536,1024]{1,0:T(8,128)(2,1)S(1)} %bitcast.117, ...), custom_call_target="tpu_custom_call" | custom-call | flops 4294967296 | bytes 8654848 | tf_op jit(solution)/shard_map/pallas_call | solution.py:32
  133.8 1.3 copy-done.6
  135.2 2.4 collective-permute-start.10
  137.6 2.7 collective-permute-start.9
  140.3 3.8 %collective-permute-done.13.refs_6_ = bf16[2,1024,128]{2,1,0:T(8,128)(2,1)} collective-permute-done((bf16[2,1024,128]{2,1,0:T(8,128)(2,1)}, bf16[2,1024,128]{2,1,0:T(8,128)(2,1)}, u32[]{:S(2)}, u32[]{:S(2)}) %collective-permute-start.13) | collective-permute-done | bytes 524320 | tf_op jit(solution)/shard_map/ppermute | solution.py:166
  144.0 6.3 %fusion = f32[2,4,128,128]{3,2,1,0:T(8,128)S(1)} fusion(bf16[4,2,128,4096]{3,2,1,0:T(8,128)(2,1)} %bitcast.120, bf16[2,4096,128]{2,1,0:T(8,128)(2,1)} %param.12), kind=kOutput, calls=%fused_computation | convolution fusion | flops 1073741824 | bytes 11010048 | tf_op jit(solution)/shard_map/gecd,edf->gecf/dot_general | solution.py:240
  150.5 5.2 %collective-permute-done.11 = bf16[1024,128]{1,0:T(8,128)(2,1)S(1)} collective-permute-done((bf16[1024,128]{1,0:T(8,128)(2,1)}, bf16[1024,128]{1,0:T(8,128)(2,1)S(1)}, u32[]{:S(2)}, u32[]{:S(2)}) %collective-permute-start.11) | collective-permute-done | bytes 262176 | tf_op jit(solution)/shard_map/ppermute | solution.py:166
  155.6 1.1 multiply_reduce_fusion
  156.8 1.3 collective-permute-start.16
  158.0 1.6 collective-permute-start.17
  159.7 11.3 %collective-permute-done.15.refs_1_ = bf16[1024,128]{1,0:T(8,128)(2,1)S(1)} collective-permute-done((bf16[1024,128]{1,0:T(8,128)(2,1)S(1)}, bf16[1024,128]{1,0:T(8,128)(2,1)S(1)}, u32[]{:S(2)}, u32[]{:S(2)}) %collective-permute-start.15) | collective-permute-done | bytes 262176 | tf_op jit(solution)/shard_map/ppermute | solution.py:166
  171.3 6.2 %shard_map.104 = bf16[4,1536,256]{2,1,0:T(8,128)(2,1)} custom-call(s32[1]{0:T(128)} %bitcast.13.me, s32[4,256]{1,0:T(4,128)S(1)} %multiply_add_fusion.place, bf16[1024,128]{1,0:T(8,128)(2,1)S(1)} %get-tuple-element.54.refs_0_, bf16[1024,128]{1,0:T(8,128)(2,1)S(1)} %collective-permute-done.15.refs_1_, bf16[1024,128]{1,0:T(8,128)(2,1)S(1)} %collective-permute-done.16.refs_2_, ...), custom_call_target="tpu_custom_call" | custom-call | flops 4294967296 | bytes 6295556 | tf_op jit(solution)/shard_map/pallas_call | solution.py:32
  177.5 14.1 %all-to-all-start.2 = ((bf16[256,24,256]{2,1,0:T(8,128)(2,1)}), bf16[256,24,256]{2,1,0:T(8,128)(2,1)S(1)}, u32[]{:S(2)}, u32[]{:S(2)}) async-start(bf16[256,24,256]{2,1,0:T(8,128)(2,1)} %bitcast.31), calls=%async_computation.2 | async-start | bytes 6291456 | tf_op jit(solution)/shard_map/all_to_all | solution.py:281
  192.1 2.7 collective-permute-start.21
  195.9 1.7 collective-permute-start.19
  197.6 1.0 collective-permute-start.20
  198.6 2.4 collective-permute-start.22
  201.0 19.2 %collective-permute-done.22 = f32[2,128]{1,0:T(2,128)S(1)} collective-permute-done((f32[2,128]{1,0:T(2,128)}, f32[2,128]{1,0:T(2,128)S(1)}, u32[]{:S(2)}, u32[]{:S(2)}) %collective-permute-start.22) | collective-permute-done | bytes 1056 | tf_op jit(solution)/shard_map/ppermute | solution.py:166
  220.2 1.2 fusion.41
  221.4 0.9 copy-done.5
  222.4 1.6 copy-done.7
  223.9 1.3 shard_map.106
  225.3 2.2 collective-permute-start.24
  228.1 8.1 %fusion.2 = bf16[2,4096,128]{2,1,0:T(8,128)(2,1)} fusion(bf16[4,2,128,4096]{3,2,1,0:T(8,128)(2,1)} %bitcast.121, bf16[1,2,128,128]{3,2,1,0:T(8,128)(2,1)S(1)} %get-tuple-element.86, bf16[1,2,128,128]{3,2,1,0:T(8,128)(2,1)S(1)} %get-tuple-element.87, bf16[1,2,128,128]{3,2,1,0:T(8,128)(2,1)S(1)} %get-tuple-element.88, ...), kind=kOutput, calls=%fused_computation.3 | convolution fusion | flops 1075183616 | bytes 10747904 | tf_op jit(solution)/shard_map/gecd,gecf->edf/dot_general | solution.py:305
  236.2 1.6 broadcast_in_dim.51
  238.6 7.8 %collective-permute-done.24 = bf16[2,128,1024]{2,1,0:T(8,128)(2,1)S(1)} collective-permute-done((bf16[2,128,1024]{2,1,0:T(8,128)(2,1)S(1)}, bf16[2,128,1024]{2,1,0:T(8,128)(2,1)S(1)}, u32[]{:S(2)}, u32[]{:S(2)}) %collective-permute-start.24) | collective-permute-done | bytes 524320 | tf_op jit(solution)/shard_map/ppermute | solution.py:166
  247.2 3.1 %collective-permute-done.25 = bf16[2,128,1024]{2,1,0:T(8,128)(2,1)S(1)} collective-permute-done((bf16[2,128,1024]{2,1,0:T(8,128)(2,1)S(1)}, bf16[2,128,1024]{2,1,0:T(8,128)(2,1)S(1)}, u32[]{:S(2)}, u32[]{:S(2)}) %collective-permute-start.25) | collective-permute-done | bytes 524320 | tf_op jit(solution)/shard_map/ppermute | solution.py:166
  251.1 18.0 %collective-permute-done.26 = bf16[2,128,1024]{2,1,0:T(8,128)(2,1)S(1)} collective-permute-done((bf16[2,128,1024]{2,1,0:T(8,128)(2,1)S(1)}, bf16[2,128,1024]{2,1,0:T(8,128)(2,1)S(1)}, u32[]{:S(2)}, u32[]{:S(2)}) %collective-permute-start.26) | collective-permute-done | bytes 524320 | tf_op jit(solution)/shard_map/ppermute | solution.py:166
  269.9 3.4 %shard_map.105 = bf16[128,4096]{1,0:T(8,128)(2,1)} custom-call(s32[1,1536]{1,0:T(1,128)S(1)} %select_n.66.home, bf16[4,1536,256]{2,1,0:T(8,128)(2,1)S(1)} %bitcast.116), custom_call_target="tpu_custom_call" | custom-call | flops 1610612736 | bytes 4200448 | tf_op jit(solution)/shard_map/pallas_call | solution.py:32
  (93 shorter events, 12.9 us)
Async XLA Ops:
  7.2 0.8 copy-start.10
  7.2 0.8 copy-start.11
  7.2 6.7 %copy-start.12 = (s32[1,128]{1,0:T(1,128)S(1)}, s32[1,128]{1,0:T(1,128)}, u32[]{:S(2)}) copy-start(s32[1,128]{1,0:T(1,128)} %param.8) | copy-start | bytes 1540
  7.2 6.7 %copy-start.8 = (bf16[1,128,4096]{2,1,0:T(8,128)(2,1)S(1)}, bf16[1,128,4096]{2,1,0:T(8,128)(2,1)}, u32[]{:S(2)}) copy-start(bf16[1,128,4096]{2,1,0:T(8,128)(2,1)} %param.7) | copy-start | bytes 3145732
  7.2 136.8 %all-gather.2.cloned.1.call-start = ((), (), s32[]{:S(2)}) async-start(), calls=%async_computation.3 | async-start | bytes 10485760 | tf_op jit(solution)/shard_map/all_gather | solution.py:186
  8.0 7.6 %collective-permute-start = (f32[2,256]{1,0:T(2,128)S(1)}, f32[2,256]{1,0:T(2,128)S(1)}, u32[]{:S(2)}, u32[]{:S(2)}) collective-permute-start(f32[2,256]{1,0:T(2,128)S(1)} %get-tuple-element.92), channel_id=1, source_target_pairs={{0,64},{64,128},{128,192},{192,0},{1,65},{65,129},{129,193},{193,1... | collective-permute-start | bytes 6152 | tf_op jit(solution)/shard_map/ppermute | solution.py:166
  10.2 7.1 %collective-permute-start.1 = (f32[2,256]{1,0:T(2,128)S(1)}, f32[2,256]{1,0:T(2,128)S(1)}, u32[]{:S(2)}, u32[]{:S(2)}) collective-permute-start(f32[2,256]{1,0:T(2,128)S(1)} %get-tuple-element.92), channel_id=1, source_target_pairs={{0,128},{64,192},{128,0},{192,64},{1,129},{65,193},{129,1},{193,65... | collective-permute-start | bytes 6152 | tf_op jit(solution)/shard_map/ppermute | solution.py:166
  12.8 4.5 %collective-permute-start.2 = (f32[2,256]{1,0:T(2,128)S(1)}, f32[2,256]{1,0:T(2,128)S(1)}, u32[]{:S(2)}, u32[]{:S(2)}) collective-permute-start(f32[2,256]{1,0:T(2,128)S(1)} %get-tuple-element.92), channel_id=1, source_target_pairs={{0,192},{64,0},{128,64},{192,128},{1,193},{65,1},{129,65},{193,129... | collective-permute-start | bytes 6152 | tf_op jit(solution)/shard_map/ppermute | solution.py:166
  14.3 28.3 %collective-permute-start.3 = (bf16[128,1024]{1,0:T(8,128)(2,1)S(1)}, bf16[128,1024]{1,0:T(8,128)(2,1)S(1)}, u32[]{:S(2)}, u32[]{:S(2)}) collective-permute-start(bf16[128,1024]{1,0:T(8,128)(2,1)S(1)} %get-tuple-element.78), channel_id=1, source_target_pairs={{0,64},{64,128},{128,192},{192,0},{1,65},{65,129},{129,193},{193,1... | collective-permute-start | bytes 786440 | tf_op jit(solution)/shard_map/ppermute | solution.py:166
  14.7 27.8 %collective-permute-start.4 = (bf16[128,1024]{1,0:T(8,128)(2,1)S(1)}, bf16[128,1024]{1,0:T(8,128)(2,1)S(1)}, u32[]{:S(2)}, u32[]{:S(2)}) collective-permute-start(bf16[128,1024]{1,0:T(8,128)(2,1)S(1)} %get-tuple-element.77), channel_id=1, source_target_pairs={{0,128},{64,192},{128,0},{192,64},{1,129},{65,193},{129,1},{193,65... | collective-permute-start | bytes 786440 | tf_op jit(solution)/shard_map/ppermute | solution.py:166
  15.6 27.1 %collective-permute-start.5 = (bf16[128,1024]{1,0:T(8,128)(2,1)S(1)}, bf16[128,1024]{1,0:T(8,128)(2,1)S(1)}, u32[]{:S(2)}, u32[]{:S(2)}) collective-permute-start(bf16[128,1024]{1,0:T(8,128)(2,1)S(1)} %get-tuple-element.76), channel_id=1, source_target_pairs={{0,192},{64,0},{128,64},{192,128},{1,193},{65,1},{129,65},{193,129... | collective-permute-start | bytes 786440 | tf_op jit(solution)/shard_map/ppermute | solution.py:166
  17.3 91.6 %copy-start.9 = (f32[4,2,256]{2,0,1:T(4,128)}, f32[4,2,256]{2,0,1:T(4,128)S(1)}, u32[]{:S(2)}) copy-start(f32[4,2,256]{2,0,1:T(4,128)S(1)} %pad_maximum_fusion.1) | copy-start | bytes 24580
  18.5 22.9 %all-to-all-start = ((s32[64,1,32]{2,1,0:T(1,128)}), s32[64,1,32]{2,1,0:T(1,128)S(1)}, u32[]{:S(2)}, u32[]{:S(2)}) async-start(s32[64,1,32]{2,1,0:T(1,128)} %copy.39), calls=%async_computation | async-start | bytes 65536 | tf_op jit(solution)/shard_map/all_to_all | solution.py:205
  45.6 1.6 copy-start
  47.3 77.6 %all-to-all-start.1 = ((bf16[64,24,1024]{2,1,0:T(8,128)(2,1)}), bf16[64,24,1024]{2,1,0:T(8,128)(2,1)S(1)}, u32[]{:S(2)}, u32[]{:S(2)}) async-start(bf16[64,24,1024]{2,1,0:T(8,128)(2,1)} %bitcast.118), calls=%async_computation.1 | async-start | bytes 6291456 | tf_op jit(solution)/shard_map/all_to_all | solution.py:236
  55.1 26.4 %collective-permute-start.6 = (bf16[2,128,1024]{2,1,0:T(8,128)(2,1)}, bf16[2,128,1024]{2,1,0:T(8,128)(2,1)}, u32[]{:S(2)}, u32[]{:S(2)}) collective-permute-start(bf16[2,128,1024]{2,1,0:T(8,128)(2,1)} %get-tuple-element.67), channel_id=1, source_target_pairs={{0,64},{64,128},{128,192},{192,0},{1,65},{65,129},{129,193},{193,1... | collective-permute-start | bytes 1572872 | tf_op jit(solution)/shard_map/ppermute | solution.py:166
  55.5 48.2 %collective-permute-start.7 = (bf16[2,128,1024]{2,1,0:T(8,128)(2,1)}, bf16[2,128,1024]{2,1,0:T(8,128)(2,1)}, u32[]{:S(2)}, u32[]{:S(2)}) collective-permute-start(bf16[2,128,1024]{2,1,0:T(8,128)(2,1)} %get-tuple-element.69), channel_id=1, source_target_pairs={{0,128},{64,192},{128,0},{192,64},{1,129},{65,193},{129,1},{193,65... | collective-permute-start | bytes 1572872 | tf_op jit(solution)/shard_map/ppermute | solution.py:166
  57.5 46.9 %collective-permute-start.8 = (bf16[2,128,1024]{2,1,0:T(8,128)(2,1)}, bf16[2,128,1024]{2,1,0:T(8,128)(2,1)}, u32[]{:S(2)}, u32[]{:S(2)}) collective-permute-start(bf16[2,128,1024]{2,1,0:T(8,128)(2,1)} %get-tuple-element.66), channel_id=1, source_target_pairs={{0,192},{64,0},{128,64},{192,128},{1,193},{65,1},{129,65},{193,129... | collective-permute-start | bytes 1572872 | tf_op jit(solution)/shard_map/ppermute | solution.py:166
  104.4 33.2 %collective-permute-start.12 = (bf16[2,1024,128]{2,1,0:T(8,128)(2,1)}, bf16[2,1024,128]{2,1,0:T(8,128)(2,1)}, u32[]{:S(2)}, u32[]{:S(2)}) collective-permute-start(bf16[2,1024,128]{2,1,0:T(8,128)(2,1)} %get-tuple-element.43), channel_id=1, source_target_pairs={{0,64},{64,128},{128,192},{192,0},{1,65},{65,129},{129,193},{193,1... | collective-permute-start | bytes 1572872 | tf_op jit(solution)/shard_map/ppermute | solution.py:166
  104.4 39.6 %collective-permute-start.13 = (bf16[2,1024,128]{2,1,0:T(8,128)(2,1)}, bf16[2,1024,128]{2,1,0:T(8,128)(2,1)}, u32[]{:S(2)}, u32[]{:S(2)}) collective-permute-start(bf16[2,1024,128]{2,1,0:T(8,128)(2,1)} %get-tuple-element.44), channel_id=1, source_target_pairs={{0,128},{64,192},{128,0},{192,64},{1,129},{65,193},{129,1},{193,65... | collective-permute-start | bytes 1572872 | tf_op jit(solution)/shard_map/ppermute | solution.py:166
  106.8 37.2 %collective-permute-start.14 = (bf16[2,1024,128]{2,1,0:T(8,128)(2,1)}, bf16[2,1024,128]{2,1,0:T(8,128)(2,1)}, u32[]{:S(2)}, u32[]{:S(2)}) collective-permute-start(bf16[2,1024,128]{2,1,0:T(8,128)(2,1)} %get-tuple-element.45), channel_id=1, source_target_pairs={{0,192},{64,0},{128,64},{192,128},{1,193},{65,1},{129,65},{193,129... | collective-permute-start | bytes 1572872 | tf_op jit(solution)/shard_map/ppermute | solution.py:166
  124.9 1.0 copy-start.4
  133.0 0.8 copy-start.1
  133.8 1.3 copy-start.6
  135.2 15.3 %collective-permute-start.10 = (bf16[1024,128]{1,0:T(8,128)(2,1)}, bf16[1024,128]{1,0:T(8,128)(2,1)S(1)}, u32[]{:S(2)}, u32[]{:S(2)}) collective-permute-start(bf16[1024,128]{1,0:T(8,128)(2,1)} %get-tuple-element.40), channel_id=1, source_target_pairs={{0,128},{64,192},{128,0},{192,64},{1,129},{65,193},{129,1},{193,65... | collective-permute-start | bytes 786440 | tf_op jit(solution)/shard_map/ppermute | solution.py:166
  137.6 18.0 %collective-permute-start.11 = (bf16[1024,128]{1,0:T(8,128)(2,1)}, bf16[1024,128]{1,0:T(8,128)(2,1)S(1)}, u32[]{:S(2)}, u32[]{:S(2)}) collective-permute-start(bf16[1024,128]{1,0:T(8,128)(2,1)} %get-tuple-element.41), channel_id=1, source_target_pairs={{0,64},{64,128},{128,192},{192,0},{1,65},{65,129},{129,193},{193,1... | collective-permute-start | bytes 786440 | tf_op jit(solution)/shard_map/ppermute | solution.py:166
  137.6 18.0 %collective-permute-start.9 = (bf16[1024,128]{1,0:T(8,128)(2,1)S(1)}, bf16[1024,128]{1,0:T(8,128)(2,1)S(1)}, u32[]{:S(2)}, u32[]{:S(2)}) collective-permute-start(bf16[1024,128]{1,0:T(8,128)(2,1)S(1)} %get-tuple-element.39), channel_id=1, source_target_pairs={{0,192},{64,0},{128,64},{192,128},{1,193},{65,1},{129,65},{193,129... | collective-permute-start | bytes 786440 | tf_op jit(solution)/shard_map/ppermute | solution.py:166
  150.3 5.3 %copy-start.2 = (f32[1024,128]{1,0:T(8,128)S(1)}, f32[1024,128]{1,0:T(8,128)}, u32[]{:S(2)}) copy-start(f32[1024,128]{1,0:T(8,128)} %copy-done.1) | copy-start | bytes 1572868
  150.3 5.3 %slice-start = ((f32[4,2,256]{2,0,1:T(4,128)}), f32[4,1,256]{2,0,1:T(4,128)S(1)}, s32[]{:S(2)}) async-start(f32[4,2,256]{2,0,1:T(4,128)} %copy-done.9), calls=%async_computation.4 | async-start | bytes 8192 | tf_op jit(solution)/shard_map/slice | solution.py:213
  150.3 21.0 %copy-start.3 = (bf16[2,1024,128]{2,1,0:T(8,128)(2,1)S(1)}, bf16[2,1024,128]{2,1,0:T(8,128)(2,1)}, u32[]{:S(2)}) copy-start(bf16[2,1024,128]{2,1,0:T(8,128)(2,1)} %get-tuple-element.47.refs_4_) | copy-start | bytes 1572868
  156.8 14.2 %collective-permute-start.15 = (bf16[1024,128]{1,0:T(8,128)(2,1)S(1)}, bf16[1024,128]{1,0:T(8,128)(2,1)S(1)}, u32[]{:S(2)}, u32[]{:S(2)}) collective-permute-start(bf16[1024,128]{1,0:T(8,128)(2,1)S(1)} %get-tuple-element.54.refs_0_), channel_id=1, source_target_pairs={{0,64},{64,128},{128,192},{192,0},{1,65},{65,129},{129,193},{193,1... | collective-permute-start | bytes 786440 | tf_op jit(solution)/shard_map/ppermute | solution.py:166
  156.8 14.2 %collective-permute-start.16 = (bf16[1024,128]{1,0:T(8,128)(2,1)S(1)}, bf16[1024,128]{1,0:T(8,128)(2,1)S(1)}, u32[]{:S(2)}, u32[]{:S(2)}) collective-permute-start(bf16[1024,128]{1,0:T(8,128)(2,1)S(1)} %get-tuple-element.54.refs_0_), channel_id=1, source_target_pairs={{0,128},{64,192},{128,0},{192,64},{1,129},{65,193},{129,1},{193,65... | collective-permute-start | bytes 786440 | tf_op jit(solution)/shard_map/ppermute | solution.py:166
  158.0 13.3 %collective-permute-start.17 = (bf16[1024,128]{1,0:T(8,128)(2,1)S(1)}, bf16[1024,128]{1,0:T(8,128)(2,1)S(1)}, u32[]{:S(2)}, u32[]{:S(2)}) collective-permute-start(bf16[1024,128]{1,0:T(8,128)(2,1)S(1)} %get-tuple-element.54.refs_0_), channel_id=1, source_target_pairs={{0,192},{64,0},{128,64},{192,128},{1,193},{65,1},{129,65},{193,129... | collective-permute-start | bytes 786440 | tf_op jit(solution)/shard_map/ppermute | solution.py:166
  177.5 92.5 %all-to-all-start.2 = ((bf16[256,24,256]{2,1,0:T(8,128)(2,1)}), bf16[256,24,256]{2,1,0:T(8,128)(2,1)S(1)}, u32[]{:S(2)}, u32[]{:S(2)}) async-start(bf16[256,24,256]{2,1,0:T(8,128)(2,1)} %bitcast.31), calls=%async_computation.2 | async-start | bytes 6291456 | tf_op jit(solution)/shard_map/all_to_all | solution.py:281
  192.1 8.8 %collective-permute-start.21 = (f32[2,128]{1,0:T(2,128)}, f32[2,128]{1,0:T(2,128)}, u32[]{:S(2)}, u32[]{:S(2)}) collective-permute-start(f32[2,128]{1,0:T(2,128)} %get-tuple-element.89), channel_id=1, source_target_pairs={{0,192},{64,0},{128,64},{192,128},{1,193},{65,1},{129,65},{193,129... | collective-permute-start | bytes 3080 | tf_op jit(solution)/shard_map/ppermute | solution.py:166
  195.8 25.6 %collective-permute-start.18 = (bf16[1024,128]{1,0:T(8,128)(2,1)}, bf16[1024,128]{1,0:T(8,128)(2,1)S(1)}, u32[]{:S(2)}, u32[]{:S(2)}) collective-permute-start(bf16[1024,128]{1,0:T(8,128)(2,1)} %get-tuple-element.55.refs_0_), channel_id=1, source_target_pairs={{0,64},{64,128},{128,192},{192,0},{1,65},{65,129},{129,193},{193,1... | collective-permute-start | bytes 786440 | tf_op jit(solution)/shard_map/ppermute | solution.py:166
  195.9 25.5 %collective-permute-start.19 = (bf16[1024,128]{1,0:T(8,128)(2,1)}, bf16[1024,128]{1,0:T(8,128)(2,1)S(1)}, u32[]{:S(2)}, u32[]{:S(2)}) collective-permute-start(bf16[1024,128]{1,0:T(8,128)(2,1)} %get-tuple-element.55.refs_0_), channel_id=1, source_target_pairs={{0,128},{64,192},{128,0},{192,64},{1,129},{65,193},{129,1},{193,65... | collective-permute-start | bytes 786440 | tf_op jit(solution)/shard_map/ppermute | solution.py:166
  197.6 23.8 %collective-permute-start.20 = (bf16[1024,128]{1,0:T(8,128)(2,1)}, bf16[1024,128]{1,0:T(8,128)(2,1)S(1)}, u32[]{:S(2)}, u32[]{:S(2)}) collective-permute-start(bf16[1024,128]{1,0:T(8,128)(2,1)} %get-tuple-element.55.refs_0_), channel_id=1, source_target_pairs={{0,192},{64,0},{128,64},{192,128},{1,193},{65,1},{129,65},{193,129... | collective-permute-start | bytes 786440 | tf_op jit(solution)/shard_map/ppermute | solution.py:166
  198.6 21.6 %collective-permute-start.22 = (f32[2,128]{1,0:T(2,128)}, f32[2,128]{1,0:T(2,128)S(1)}, u32[]{:S(2)}, u32[]{:S(2)}) collective-permute-start(f32[2,128]{1,0:T(2,128)} %get-tuple-element.90), channel_id=1, source_target_pairs={{0,128},{64,192},{128,0},{192,64},{1,129},{65,193},{129,1},{193,65... | collective-permute-start | bytes 3080 | tf_op jit(solution)/shard_map/ppermute | solution.py:166
  200.9 19.3 %collective-permute-start.23 = (f32[2,128]{1,0:T(2,128)S(1)}, f32[2,128]{1,0:T(2,128)S(1)}, u32[]{:S(2)}, u32[]{:S(2)}) collective-permute-start(f32[2,128]{1,0:T(2,128)S(1)} %bitcast.133), channel_id=1, source_target_pairs={{0,64},{64,128},{128,192},{192,0},{1,65},{65,129},{129,193},{193,1... | collective-permute-start | bytes 3080 | tf_op jit(solution)/shard_map/ppermute | solution.py:166
  221.4 1.0 copy-start.5
  222.4 1.6 copy-start.7
  225.3 21.1 %collective-permute-start.24 = (bf16[2,128,1024]{2,1,0:T(8,128)(2,1)S(1)}, bf16[2,128,1024]{2,1,0:T(8,128)(2,1)S(1)}, u32[]{:S(2)}, u32[]{:S(2)}) collective-permute-start(bf16[2,128,1024]{2,1,0:T(8,128)(2,1)S(1)} %get-tuple-element.61), channel_id=1, source_target_pairs={{0,192},{64,0},{128,64},{192,128},{1,193},{65,1},{129,65},{193,129... | collective-permute-start | bytes 1572872 | tf_op jit(solution)/shard_map/ppermute | solution.py:166
  227.5 22.8 %collective-permute-start.25 = (bf16[2,128,1024]{2,1,0:T(8,128)(2,1)S(1)}, bf16[2,128,1024]{2,1,0:T(8,128)(2,1)S(1)}, u32[]{:S(2)}, u32[]{:S(2)}) collective-permute-start(bf16[2,128,1024]{2,1,0:T(8,128)(2,1)S(1)} %get-tuple-element.62), channel_id=1, source_target_pairs={{0,128},{64,192},{128,0},{192,64},{1,129},{65,193},{129,1},{193,65... | collective-permute-start | bytes 1572872 | tf_op jit(solution)/shard_map/ppermute | solution.py:166
  227.6 41.5 %collective-permute-start.26 = (bf16[2,128,1024]{2,1,0:T(8,128)(2,1)S(1)}, bf16[2,128,1024]{2,1,0:T(8,128)(2,1)S(1)}, u32[]{:S(2)}, u32[]{:S(2)}) collective-permute-start(bf16[2,128,1024]{2,1,0:T(8,128)(2,1)S(1)} %get-tuple-element.63), channel_id=1, source_target_pairs={{0,64},{64,128},{128,192},{192,0},{1,65},{65,129},{129,193},{193,1... | collective-permute-start | bytes 1572872 | tf_op jit(solution)/shard_map/ppermute | solution.py:166
Sparse Core Ops, SparseCore 0:
  9.8 129.3 all-gather.1

commit v3 on v2

--- a/solution.py
+++ b/solution.py
@@ -12,7 +12,7 @@
 PEER = 6
 F32 = jnp.float32
 BF16 = jnp.bfloat16
-VMEM_BYTES = 40 * 1024 * 1024
+VMEM_BYTES = 28 * 1024 * 1024
 
 
 def dot(a, b, dims):
@@ -66,15 +66,12 @@
     sent[...] = dot(onehot, held[...], ((1,), (0,))).astype(BF16)
 
 
-def project_kernel(n, cap, into, got, *refs):
-    ws, up, outs, wide = refs[:n], refs[n], refs[n + 1 : 2 * n + 1], refs[2 * n + 1]
-    share = ws[0].shape[1]
-    for s in range(n):
-        wide[s * share : (s + 1) * share] = ws[s][0]
+def project_kernel(n, cap, into, got, wide, up, *outs):
+    share = wide.shape[1] // n
     ids = lax.broadcasted_iota(jnp.int32, (n * cap, got.shape[0]), 1)
     onehot = jnp.where(column(into[0]) == ids, 1.0, 0.0).astype(BF16)
     up[...] = dot(onehot, got[...], ((1,), (0,))).astype(BF16)
-    part = dot(up[...], wide[...], ((1,), (1,)))
+    part = dot(up[...], wide[0], ((1,), (1,)))
     for s in range(n):
         for p in range(n):
             low = ((p - s) % n) * cap
@@ -83,9 +80,9 @@
 
 
 def back_kernel(n, cap, me, place, *refs):
-    ps, ws, out = refs[:n], refs[n : 2 * n], refs[2 * n]
-    wide, tall, back = refs[2 * n + 1 :]
-    experts, width, share = ws[0].shape
+    ps, wide, out, tall, back = refs[:n], *refs[n:]
+    experts, width, _ = wide.shape
+    share = wide.shape[2] // n
     thin = width // n
     step = out.shape[1] // 2
     p = pl.program_id(0)
@@ -94,11 +91,10 @@
     def _():
         for e in range(experts):
             for s in range(n):
-                wide[:, s * share : (s + 1) * share] = ws[s][e]
                 for g in range(n):
                     low = (e * n + (g - s) % n) * cap
                     tall[g * cap : (g + 1) * cap, s * share : (s + 1) * share] = ps[s][low : low + cap]
-            mine = dot(tall[...], wide[...], ((1,), (1,))).astype(BF16)
+            mine = dot(tall[...], wide[e], ((1,), (1,))).astype(BF16)
             for g in range(n):
                 back[g, e * cap : (e + 1) * cap] = mine[g * cap : (g + 1) * cap]
 
@@ -219,6 +215,7 @@
     w_out_all = forward(own_out)
     own_in, w_out_all = lax.optimization_barrier((own_in, w_out_all))
     w_in_all = forward(own_in)
+    w_out_wide = jnp.concatenate(w_out_all, axis=1)
     inputs, w_in_all = lax.optimization_barrier((inputs, w_in_all))
 
     start = jnp.arange(n, dtype=jnp.int32)[None, :, None] * tok
@@ -238,6 +235,8 @@
     )
 
     pre = jnp.einsum("gecd,edf->gecf", inputs, w_in, preferred_element_type=F32)
+    pre, w_in_all = lax.optimization_barrier((pre, w_in_all))
+    w_in_wide = jnp.concatenate(w_in_all, axis=2)
     pre = jnp.stack(turned(pre), 1).reshape(every, share)
     normal_cdf = 0.5 * (1.0 + lax.erf(pre * SQRT_HALF))
     slope = scale * (normal_cdf + pre * jnp.exp(-0.5 * pre * pre) * INV_ROOT_TWO_PI)
@@ -249,13 +248,12 @@
     up, *partial = call(
         functools.partial(project_kernel, n, cap),
         [((every, quarter), BF16)] + partials,
-        [into, got.reshape(owners * rows, quarter), *w_out_all],
+        [into, got.reshape(owners * rows, quarter), w_out_wide],
         [pl.BlockSpec((1, n, cap), lambda e: (e, 0, 0)), whole((owners * rows, quarter))]
-        + [pl.BlockSpec((1, share, quarter), lambda e: (e, 0, 0))] * n,
+        + [pl.BlockSpec((1, n * share, quarter), lambda e: (e, 0, 0))],
         [pl.BlockSpec((n * cap, quarter), lambda e: (e, 0))]
         + [pl.BlockSpec((n * cap, share), lambda e: (e, 0))] * n,
         (experts,),
-        [pltpu.VMEM((n * share, quarter), BF16)],
         flops=2 * every * quarter * (n * share + owners * rows),
     )
     project = reduced(partial)
@@ -265,13 +263,12 @@
     (outgoing,) = call(
         functools.partial(back_kernel, n, cap),
         [((n, owners * rows, thin), BF16)],
-        [me.reshape(1), source * 8 + rank, *pre_grad, *w_in_all],
+        [me.reshape(1), source * 8 + rank, *pre_grad, w_in_wide],
         out_specs=[
             pl.BlockSpec((1, owners * rows, thin), lambda p, m: (lax.rem(m[0] + n - p, n), 0, 0))
         ],
         grid=(n,),
         scratch=[
-            pltpu.VMEM((quarter, n * share), BF16),
             pltpu.VMEM((n * cap, n * share), BF16),
             pltpu.VMEM((n, slots, quarter), BF16),
         ],

time: 281 us -> 279 us (level)
  other arithmetic: 3.43 us -> 7.87 us
  waiting for transfers between devices: 136 us -> 132 us
    concatenate x0 -> x2, other arithmetic: none -> 4.44 us  [the longest x1 2.85 us: shards(): w_out_wide = jnp.concatenate(w_out_all, axis=1)]
    unnamed x26 -> x28, local copies, waits for them, and re-layouts: 7.33 us -> 7.88 us
  transfers between devices with their start and end apart: 31 -> 31, of which waited for: 13 -> 13; matrix products, arithmetic and copies ran while one was open for 11% -> 13% of each run, Pallas kernels for 4% -> 4%
where the time goes in v3:
time: 279 us
  waiting for transfers between devices  132 us (47%)
  starting transfers between devices  69 us (25%)
  local copies, waits for them, and re-layouts  21.7 us (8%)
  Pallas kernels  18.4 us (7%)
  matrix products  14.8 us (5%)
  between operations  14.4 us (5%)
  other arithmetic  7.87 us (3%)
    ppermute x27, waiting for transfers between devices, shift(): return lax.ppermute(x, 'dp', [(a, (a + s) % n) for a in range(n)])  109 us
    ppermute x27, starting transfers between devices, shift(): return lax.ppermute(x, 'dp', [(a, (a + s) % n) for a in range(n)])  36.6 us
    pallas_call x5, Pallas kernels, call(): pl.pallas_call(kernel, out_shape=shapes, grid_spec=pltpu.PrefetchScalarGr...  18.4 us
    all_to_all x1, starting transfers between devices, shards(): lax.all_to_all(outgoing.reshape(n * owners, rows, thin), ('dp', 'expert')...  14 us
    all_to_all x1, starting transfers between devices, shards(): lax.all_to_all(request, 'expert', split_axis=0, concat_axis=0, tiled=True)  13.6 us
    all_to_all x1, waiting for transfers between devices, shards(): lax.all_to_all(sent.reshape(owners, rows, quarter), 'expert', split_axis=...  13.1 us
    all_to_all x1, waiting for transfers between devices, shards(): lax.all_to_all(request, 'expert', split_axis=0, concat_axis=0, tiled=True)  9.29 us
    dot_general x1, matrix products, shards(): jnp.einsum('gecd,gecf->edf', inputs, own_grad, preferred_element_type=F32)  8.07 us
  transfers between devices with their start and end apart: 31, of which 13 were waited for; matrix products, arithmetic and copies ran while one was open for 13% of the time, Pallas kernels for 4%

profile of v3, /device:TPU:1, one launch (start us, length us, event | category | flops | bytes accessed | tf_op | source)
XLA Modules:
  0.0 278.5 jit_solution(7520213170296239462)
XLA Ops:
  8.0 2.2 collective-permute-start
  10.2 2.6 collective-permute-start.1
  12.8 1.1 collective-permute-start.2
  15.6 1.7 collective-permute-start.5
  18.5 13.6 %all-to-all-start = ((s32[64,1,32]{2,1,0:T(1,128)}), s32[64,1,32]{2,1,0:T(1,128)S(1)}, u32[]{:S(2)}, u32[]{:S(2)}) async-start(s32[64,1,32]{2,1,0:T(1,128)} %copy.39), calls=%async_computation | async-start | bytes 65536 | tf_op jit(solution)/shard_map/all_to_all | solution.py:201
  32.1 9.3 %all-to-all-done = s32[64,1,32]{2,1,0:T(1,128)S(1)} async-done(((s32[64,1,32]{2,1,0:T(1,128)}), s32[64,1,32]{2,1,0:T(1,128)S(1)}, u32[]{:S(2)}, u32[]{:S(2)}) %all-to-all-start) | async-done | bytes 8224 | tf_op jit(solution)/shard_map/all_to_all | solution.py:201
  42.6 3.0 %shard_map.102 = bf16[1536,1024]{1,0:T(8,128)(2,1)S(1)} custom-call(s32[1536,1]{1,0:T(8,128)S(1)} %reshape.192.pick, bf16[128,1024]{1,0:T(8,128)(2,1)S(1)} %get-tuple-element.89.refs_0_, bf16[128,1024]{1,0:T(8,128)(2,1)S(1)} %collective-permute-done.3.refs_1_, bf16[128,1024]{1,0:T(8,128)(2,1)S(1)} %collective-permute-done.4.refs_2_, ...), custom_call_target="tpu_custom_call" | custom-call | flops 1610612736 | bytes 4200448 | tf_op jit(solution)/shard_map/pallas_call | solution.py:32
  45.7 1.6 copy-done
  47.3 4.8 %all-to-all-start.1 = ((bf16[64,24,1024]{2,1,0:T(8,128)(2,1)}), bf16[64,24,1024]{2,1,0:T(8,128)(2,1)S(1)}, u32[]{:S(2)}, u32[]{:S(2)}) async-start(bf16[64,24,1024]{2,1,0:T(8,128)(2,1)} %bitcast.130), calls=%async_computation.1 | async-start | bytes 6291456 | tf_op jit(solution)/shard_map/all_to_all | solution.py:233
  52.1 3.0 %constant_dynamic-slice_fusion = (bf16[2,128,1024]{2,1,0:T(8,128)(2,1)}, bf16[2,128,1024]{2,1,0:T(8,128)(2,1)}, bf16[2,128,1024]{2,1,0:T(8,128)(2,1)}, bf16[2,128,1024]{2,1,0:T(8,128)(2,1)}) fusion(bf16[2,128,4096]{2,1,0:T(8,128)(2,1)} %param.13, s32[]{:T(128)S(6)} %select_n.71, s32[]{:T(128)S(6)} %select_n.69, s32[]{:T(128)S(6)} %select_n.68, s32[]{:T(128)S(6)} %select_n.70), kind=kLoop, calls=%fused_computation.71 | loop fusion | bytes 4194320 | tf_op jit(solution)/shard_map/dynamic_slice | solution.py:168
  55.5 2.0 collective-permute-start.7
  57.5 2.1 collective-permute-start.8
  59.6 2.9 %constant_dynamic-slice_fusion.4 = (bf16[2,1024,128]{2,1,0:T(8,128)(2,1)}, bf16[2,1024,128]{2,1,0:T(8,128)(2,1)}, bf16[2,1024,128]{2,1,0:T(8,128)(2,1)}, bf16[2,1024,128]{2,1,0:T(8,128)(2,1)}) fusion(bf16[2,4096,128]{2,1,0:T(8,128)(2,1)} %param.12, s32[]{:T(128)S(6)} %select_n.71, s32[]{:T(128)S(6)} %select_n.70, s32[]{:T(128)S(6)} %select_n.69, s32[]{:T(128)S(6)} %select_n.68), kind=kLoop, calls=%fused_computation.75 | loop fusion | bytes 4194320 | tf_op jit(solution)/shard_map/dynamic_slice | solution.py:214
  62.6 18.8 %collective-permute-done.6 = bf16[2,128,1024]{2,1,0:T(8,128)(2,1)} collective-permute-done((bf16[2,128,1024]{2,1,0:T(8,128)(2,1)}, bf16[2,128,1024]{2,1,0:T(8,128)(2,1)}, u32[]{:S(2)}, u32[]{:S(2)}) %collective-permute-start.6) | collective-permute-done | bytes 524320 | tf_op jit(solution)/shard_map/ppermute | solution.py:162
  81.5 22.3 %collective-permute-done.7 = bf16[2,128,1024]{2,1,0:T(8,128)(2,1)} collective-permute-done((bf16[2,128,1024]{2,1,0:T(8,128)(2,1)}, bf16[2,128,1024]{2,1,0:T(8,128)(2,1)}, u32[]{:S(2)}, u32[]{:S(2)}) %collective-permute-start.7) | collective-permute-done | bytes 524320 | tf_op jit(solution)/shard_map/ppermute | solution.py:162
  104.4 2.5 collective-permute-start.13
  106.8 2.1 collective-permute-start.14
  108.9 2.8 %pad_maximum_fusion.wide = bf16[2,512,1024]{2,1,0:T(8,128)(2,1)} fusion(bf16[2,128,1024]{2,1,0:T(8,128)(2,1)} %collective-permute-done.8, bf16[2,128,1024]{2,1,0:T(8,128)(2,1)} %collective-permute-done.7, bf16[2,128,1024]{2,1,0:T(8,128)(2,1)} %collective-permute-done.6, bf16[2,128,1024]{2,1,0:T(8,128)(2,1)S(1)} %copy-done.8), kind=kLoop, calls=%fused_computation.4 | loop fusion | flops 8388608 | bytes 4194304 | tf_op jit(solution)/shard_map/concatenate | solution.py:218
  111.8 13.1 %all-to-all-done.1 = bf16[64,24,1024]{2,1,0:T(8,128)(2,1)S(1)} async-done(((bf16[64,24,1024]{2,1,0:T(8,128)(2,1)}), bf16[64,24,1024]{2,1,0:T(8,128)(2,1)S(1)}, u32[]{:S(2)}, u32[]{:S(2)}) %all-to-all-start.1) | async-done | bytes 3145760 | tf_op jit(solution)/shard_map/all_to_all | solution.py:233
  124.9 1.6 copy-done.1
  126.5 6.0 %shard_map.103 = (bf16[1024,1024]{1,0:T(8,128)(2,1)S(1)}, f32[1024,128]{1,0:T(8,128)S(1)}, bf16[1024,128]{1,0:T(8,128)(2,1)S(1)}, bf16[1024,128]{1,0:T(8,128)(2,1)}, bf16[1024,128]{1,0:T(8,128)(2,1)}) custom-call(s32[2,4,128]{2,1,0:T(4,128)S(1)} %add_bitcast_fusion.into, bf16[1536,1024]{1,0:T(8,128)(2,1)S(1)} %bitcast.129, bf16[2,512,1024]{2,1,0:T(8,128)(2,1)S(1)} %copy-done.1), custom_call_target="tpu_custom_call" | custom-call | flops 4294967296 | bytes 8654848 | tf_op jit(solution)/shard_map/pallas_call | solution.py:32
  133.3 1.3 copy-done.5
  134.6 2.5 collective-permute-start.10
  137.0 2.7 collective-permute-start.9
  139.7 4.3 %collective-permute-done.13 = bf16[2,1024,128]{2,1,0:T(8,128)(2,1)} collective-permute-done((bf16[2,1024,128]{2,1,0:T(8,128)(2,1)}, bf16[2,1024,128]{2,1,0:T(8,128)(2,1)}, u32[]{:S(2)}, u32[]{:S(2)}) %collective-permute-start.13) | collective-permute-done | bytes 524320 | tf_op jit(solution)/shard_map/ppermute | solution.py:162
  144.0 6.3 %fusion.5 = f32[4,2,128,128]{3,2,0,1:T(8,128)S(1)} fusion(bf16[2,4096,128]{2,1,0:T(8,128)(2,1)} %param.12, bf16[4,2,128,4096]{3,2,1,0:T(8,128)(2,1)} %bitcast.132), kind=kOutput, calls=%fused_computation.9 | convolution fusion | flops 1073741824 | bytes 11010048 | tf_op jit(solution)/shard_map/gecd,edf->gecf/dot_general | solution.py:237
  150.5 5.2 %collective-permute-done.11 = bf16[1024,128]{1,0:T(8,128)(2,1)S(1)} collective-permute-done((bf16[1024,128]{1,0:T(8,128)(2,1)}, bf16[1024,128]{1,0:T(8,128)(2,1)S(1)}, u32[]{:S(2)}, u32[]{:S(2)}) %collective-permute-start.11) | collective-permute-done | bytes 262176 | tf_op jit(solution)/shard_map/ppermute | solution.py:162
  155.6 1.1 multiply_reduce_fusion
  156.8 1.5 collective-permute-start.16
  158.3 1.4 collective-permute-start.17
  159.7 1.6 pad_maximum_fusion.1.refs_4_
  161.3 9.7 %collective-permute-done.15.refs_1_ = bf16[1024,128]{1,0:T(8,128)(2,1)S(1)} collective-permute-done((bf16[1024,128]{1,0:T(8,128)(2,1)S(1)}, bf16[1024,128]{1,0:T(8,128)(2,1)S(1)}, u32[]{:S(2)}, u32[]{:S(2)}) %collective-permute-start.15) | collective-permute-done | bytes 262176 | tf_op jit(solution)/shard_map/ppermute | solution.py:162
  171.3 4.6 %shard_map.104 = bf16[4,1536,256]{2,1,0:T(8,128)(2,1)} custom-call(s32[1]{0:T(128)} %bitcast.13.me, s32[4,256]{1,0:T(4,128)S(1)} %multiply_add_fusion.place, bf16[1024,128]{1,0:T(8,128)(2,1)S(1)} %get-tuple-element.64.refs_0_, bf16[1024,128]{1,0:T(8,128)(2,1)S(1)} %collective-permute-done.15.refs_1_, bf16[1024,128]{1,0:T(8,128)(2,1)S(1)} %collective-permute-done.16.refs_2_, ...), custom_call_target="tpu_custom_call" | custom-call | flops 4294967296 | bytes 6295556 | tf_op jit(solution)/shard_map/pallas_call | solution.py:32
  175.9 14.0 %all-to-all-start.2 = ((bf16[256,24,256]{2,1,0:T(8,128)(2,1)}), bf16[256,24,256]{2,1,0:T(8,128)(2,1)S(1)}, u32[]{:S(2)}, u32[]{:S(2)}) async-start(bf16[256,24,256]{2,1,0:T(8,128)(2,1)} %bitcast.36), calls=%async_computation.2 | async-start | bytes 6291456 | tf_op jit(solution)/shard_map/all_to_all | solution.py:278
  190.5 2.7 collective-permute-start.21
  194.3 1.7 collective-permute-start.19
  196.9 2.4 collective-permute-start.22
  199.3 19.2 %collective-permute-done.22 = f32[2,128]{1,0:T(2,128)S(1)} collective-permute-done((f32[2,128]{1,0:T(2,128)}, f32[2,128]{1,0:T(2,128)S(1)}, u32[]{:S(2)}, u32[]{:S(2)}) %collective-permute-start.22) | collective-permute-done | bytes 1056 | tf_op jit(solution)/shard_map/ppermute | solution.py:162
  218.6 1.2 fusion.46
  220.7 1.6 copy-done.6
  222.3 1.3 shard_map.106
  223.7 2.2 collective-permute-start.24
  226.5 8.1 %fusion.2 = bf16[2,4096,128]{2,1,0:T(8,128)(2,1)} fusion(bf16[4,2,128,4096]{3,2,1,0:T(8,128)(2,1)} %bitcast.133, bf16[1,2,128,128]{3,2,1,0:T(8,128)(2,1)S(1)} %get-tuple-element.96, bf16[1,2,128,128]{3,2,1,0:T(8,128)(2,1)S(1)} %get-tuple-element.97, bf16[1,2,128,128]{3,2,1,0:T(8,128)(2,1)S(1)} %get-tuple-element.98, ...), kind=kOutput, calls=%fused_computation.3 | convolution fusion | flops 1075183616 | bytes 10747904 | tf_op jit(solution)/shard_map/gecd,gecf->edf/dot_general | solution.py:302
  234.6 1.6 broadcast_in_dim.51
  237.0 7.8 %collective-permute-done.24 = bf16[2,128,1024]{2,1,0:T(8,128)(2,1)S(1)} collective-permute-done((bf16[2,128,1024]{2,1,0:T(8,128)(2,1)S(1)}, bf16[2,128,1024]{2,1,0:T(8,128)(2,1)S(1)}, u32[]{:S(2)}, u32[]{:S(2)}) %collective-permute-start.24) | collective-permute-done | bytes 524320 | tf_op jit(solution)/shard_map/ppermute | solution.py:162
  245.6 3.0 %collective-permute-done.25 = bf16[2,128,1024]{2,1,0:T(8,128)(2,1)S(1)} collective-permute-done((bf16[2,128,1024]{2,1,0:T(8,128)(2,1)S(1)}, bf16[2,128,1024]{2,1,0:T(8,128)(2,1)S(1)}, u32[]{:S(2)}, u32[]{:S(2)}) %collective-permute-start.25) | collective-permute-done | bytes 524320 | tf_op jit(solution)/shard_map/ppermute | solution.py:162
  249.5 18.0 %collective-permute-done.26 = bf16[2,128,1024]{2,1,0:T(8,128)(2,1)S(1)} collective-permute-done((bf16[2,128,1024]{2,1,0:T(8,128)(2,1)S(1)}, bf16[2,128,1024]{2,1,0:T(8,128)(2,1)S(1)}, u32[]{:S(2)}, u32[]{:S(2)}) %collective-permute-start.26) | collective-permute-done | bytes 524320 | tf_op jit(solution)/shard_map/ppermute | solution.py:162
  268.3 3.4 %shard_map.105 = bf16[128,4096]{1,0:T(8,128)(2,1)} custom-call(s32[1,1536]{1,0:T(1,128)S(1)} %select_n.66.home, bf16[4,1536,256]{2,1,0:T(8,128)(2,1)S(1)} %bitcast.128), custom_call_target="tpu_custom_call" | custom-call | flops 1610612736 | bytes 4200448 | tf_op jit(solution)/shard_map/pallas_call | solution.py:32
  (97 shorter events, 14.8 us)
Async XLA Ops:
  7.2 0.8 copy-start.11
  7.2 0.8 copy-start.12
  7.2 6.7 %copy-start.13 = (s32[1,128]{1,0:T(1,128)S(1)}, s32[1,128]{1,0:T(1,128)}, u32[]{:S(2)}) copy-start(s32[1,128]{1,0:T(1,128)} %param.8) | copy-start | bytes 1540
  7.2 6.7 %copy-start.9 = (bf16[1,128,4096]{2,1,0:T(8,128)(2,1)S(1)}, bf16[1,128,4096]{2,1,0:T(8,128)(2,1)}, u32[]{:S(2)}) copy-start(bf16[1,128,4096]{2,1,0:T(8,128)(2,1)} %param.7) | copy-start | bytes 3145732
  7.2 136.8 %all-gather.2.cloned.1.call-start = ((), (), s32[]{:S(2)}) async-start(), calls=%async_computation.3 | async-start | bytes 10485760 | tf_op jit(solution)/shard_map/all_gather | solution.py:182
  8.0 7.6 %collective-permute-start = (f32[2,256]{1,0:T(2,128)S(1)}, f32[2,256]{1,0:T(2,128)S(1)}, u32[]{:S(2)}, u32[]{:S(2)}) collective-permute-start(f32[2,256]{1,0:T(2,128)S(1)} %get-tuple-element.102), channel_id=1, source_target_pairs={{0,64},{64,128},{128,192},{192,0},{1,65},{65,129},{129,193},{193,1... | collective-permute-start | bytes 6152 | tf_op jit(solution)/shard_map/ppermute | solution.py:162
  10.2 7.1 %collective-permute-start.1 = (f32[2,256]{1,0:T(2,128)S(1)}, f32[2,256]{1,0:T(2,128)S(1)}, u32[]{:S(2)}, u32[]{:S(2)}) collective-permute-start(f32[2,256]{1,0:T(2,128)S(1)} %get-tuple-element.102), channel_id=1, source_target_pairs={{0,128},{64,192},{128,0},{192,64},{1,129},{65,193},{129,1},{193,65... | collective-permute-start | bytes 6152 | tf_op jit(solution)/shard_map/ppermute | solution.py:162
  12.8 4.5 %collective-permute-start.2 = (f32[2,256]{1,0:T(2,128)S(1)}, f32[2,256]{1,0:T(2,128)S(1)}, u32[]{:S(2)}, u32[]{:S(2)}) collective-permute-start(f32[2,256]{1,0:T(2,128)S(1)} %get-tuple-element.102), channel_id=1, source_target_pairs={{0,192},{64,0},{128,64},{192,128},{1,193},{65,1},{129,65},{193,129... | collective-permute-start | bytes 6152 | tf_op jit(solution)/shard_map/ppermute | solution.py:162
  14.3 28.3 %collective-permute-start.3 = (bf16[128,1024]{1,0:T(8,128)(2,1)S(1)}, bf16[128,1024]{1,0:T(8,128)(2,1)S(1)}, u32[]{:S(2)}, u32[]{:S(2)}) collective-permute-start(bf16[128,1024]{1,0:T(8,128)(2,1)S(1)} %get-tuple-element.88), channel_id=1, source_target_pairs={{0,64},{64,128},{128,192},{192,0},{1,65},{65,129},{129,193},{193,1... | collective-permute-start | bytes 786440 | tf_op jit(solution)/shard_map/ppermute | solution.py:162
  14.7 27.8 %collective-permute-start.4 = (bf16[128,1024]{1,0:T(8,128)(2,1)S(1)}, bf16[128,1024]{1,0:T(8,128)(2,1)S(1)}, u32[]{:S(2)}, u32[]{:S(2)}) collective-permute-start(bf16[128,1024]{1,0:T(8,128)(2,1)S(1)} %get-tuple-element.87), channel_id=1, source_target_pairs={{0,128},{64,192},{128,0},{192,64},{1,129},{65,193},{129,1},{193,65... | collective-permute-start | bytes 786440 | tf_op jit(solution)/shard_map/ppermute | solution.py:162
  15.6 27.1 %collective-permute-start.5 = (bf16[128,1024]{1,0:T(8,128)(2,1)S(1)}, bf16[128,1024]{1,0:T(8,128)(2,1)S(1)}, u32[]{:S(2)}, u32[]{:S(2)}) collective-permute-start(bf16[128,1024]{1,0:T(8,128)(2,1)S(1)} %get-tuple-element.86), channel_id=1, source_target_pairs={{0,192},{64,0},{128,64},{192,128},{1,193},{65,1},{129,65},{193,129... | collective-permute-start | bytes 786440 | tf_op jit(solution)/shard_map/ppermute | solution.py:162
  17.3 45.3 %copy-start.10 = (f32[4,2,256]{2,0,1:T(4,128)}, f32[4,2,256]{2,0,1:T(4,128)S(1)}, u32[]{:S(2)}) copy-start(f32[4,2,256]{2,0,1:T(4,128)S(1)} %pad_maximum_fusion.3) | copy-start | bytes 24580
  18.5 22.9 %all-to-all-start = ((s32[64,1,32]{2,1,0:T(1,128)}), s32[64,1,32]{2,1,0:T(1,128)S(1)}, u32[]{:S(2)}, u32[]{:S(2)}) async-start(s32[64,1,32]{2,1,0:T(1,128)} %copy.39), calls=%async_computation | async-start | bytes 65536 | tf_op jit(solution)/shard_map/all_to_all | solution.py:201
  45.7 1.6 copy-start
  47.3 77.6 %all-to-all-start.1 = ((bf16[64,24,1024]{2,1,0:T(8,128)(2,1)}), bf16[64,24,1024]{2,1,0:T(8,128)(2,1)S(1)}, u32[]{:S(2)}, u32[]{:S(2)}) async-start(bf16[64,24,1024]{2,1,0:T(8,128)(2,1)} %bitcast.130), calls=%async_computation.1 | async-start | bytes 6291456 | tf_op jit(solution)/shard_map/all_to_all | solution.py:233
  55.1 26.4 %collective-permute-start.6 = (bf16[2,128,1024]{2,1,0:T(8,128)(2,1)}, bf16[2,128,1024]{2,1,0:T(8,128)(2,1)}, u32[]{:S(2)}, u32[]{:S(2)}) collective-permute-start(bf16[2,128,1024]{2,1,0:T(8,128)(2,1)} %get-tuple-element.77), channel_id=1, source_target_pairs={{0,64},{64,128},{128,192},{192,0},{1,65},{65,129},{129,193},{193,1... | collective-permute-start | bytes 1572872 | tf_op jit(solution)/shard_map/ppermute | solution.py:162
  55.5 48.2 %collective-permute-start.7 = (bf16[2,128,1024]{2,1,0:T(8,128)(2,1)}, bf16[2,128,1024]{2,1,0:T(8,128)(2,1)}, u32[]{:S(2)}, u32[]{:S(2)}) collective-permute-start(bf16[2,128,1024]{2,1,0:T(8,128)(2,1)} %get-tuple-element.79), channel_id=1, source_target_pairs={{0,128},{64,192},{128,0},{192,64},{1,129},{65,193},{129,1},{193,65... | collective-permute-start | bytes 1572872 | tf_op jit(solution)/shard_map/ppermute | solution.py:162
  57.5 46.8 %collective-permute-start.8 = (bf16[2,128,1024]{2,1,0:T(8,128)(2,1)}, bf16[2,128,1024]{2,1,0:T(8,128)(2,1)}, u32[]{:S(2)}, u32[]{:S(2)}) collective-permute-start(bf16[2,128,1024]{2,1,0:T(8,128)(2,1)} %get-tuple-element.76), channel_id=1, source_target_pairs={{0,192},{64,0},{128,64},{192,128},{1,193},{65,1},{129,65},{193,129... | collective-permute-start | bytes 1572872 | tf_op jit(solution)/shard_map/ppermute | solution.py:162
  59.6 49.3 %copy-start.8 = (bf16[2,128,1024]{2,1,0:T(8,128)(2,1)S(1)}, bf16[2,128,1024]{2,1,0:T(8,128)(2,1)}, u32[]{:S(2)}) copy-start(bf16[2,128,1024]{2,1,0:T(8,128)(2,1)} %get-tuple-element.39) | copy-start | bytes 1572868
  104.4 32.7 %collective-permute-start.12 = (bf16[2,1024,128]{2,1,0:T(8,128)(2,1)}, bf16[2,1024,128]{2,1,0:T(8,128)(2,1)}, u32[]{:S(2)}, u32[]{:S(2)}) collective-permute-start(bf16[2,1024,128]{2,1,0:T(8,128)(2,1)} %get-tuple-element.48), channel_id=1, source_target_pairs={{0,64},{64,128},{128,192},{192,0},{1,65},{65,129},{129,193},{193,1... | collective-permute-start | bytes 1572872 | tf_op jit(solution)/shard_map/ppermute | solution.py:162
  104.4 39.6 %collective-permute-start.13 = (bf16[2,1024,128]{2,1,0:T(8,128)(2,1)}, bf16[2,1024,128]{2,1,0:T(8,128)(2,1)}, u32[]{:S(2)}, u32[]{:S(2)}) collective-permute-start(bf16[2,1024,128]{2,1,0:T(8,128)(2,1)} %get-tuple-element.49), channel_id=1, source_target_pairs={{0,128},{64,192},{128,0},{192,64},{1,129},{65,193},{129,1},{193,65... | collective-permute-start | bytes 1572872 | tf_op jit(solution)/shard_map/ppermute | solution.py:162
  106.8 37.2 %collective-permute-start.14 = (bf16[2,1024,128]{2,1,0:T(8,128)(2,1)}, bf16[2,1024,128]{2,1,0:T(8,128)(2,1)}, u32[]{:S(2)}, u32[]{:S(2)}) collective-permute-start(bf16[2,1024,128]{2,1,0:T(8,128)(2,1)} %get-tuple-element.50), channel_id=1, source_target_pairs={{0,192},{64,0},{128,64},{192,128},{1,193},{65,1},{129,65},{193,129... | collective-permute-start | bytes 1572872 | tf_op jit(solution)/shard_map/ppermute | solution.py:162
  124.9 1.6 copy-start.1
  132.5 0.8 copy-start.2
  133.3 1.3 copy-start.5
  134.6 15.9 %collective-permute-start.10 = (bf16[1024,128]{1,0:T(8,128)(2,1)}, bf16[1024,128]{1,0:T(8,128)(2,1)S(1)}, u32[]{:S(2)}, u32[]{:S(2)}) collective-permute-start(bf16[1024,128]{1,0:T(8,128)(2,1)} %get-tuple-element.45), channel_id=1, source_target_pairs={{0,128},{64,192},{128,0},{192,64},{1,129},{65,193},{129,1},{193,65... | collective-permute-start | bytes 786440 | tf_op jit(solution)/shard_map/ppermute | solution.py:162
  137.0 18.6 %collective-permute-start.11 = (bf16[1024,128]{1,0:T(8,128)(2,1)}, bf16[1024,128]{1,0:T(8,128)(2,1)S(1)}, u32[]{:S(2)}, u32[]{:S(2)}) collective-permute-start(bf16[1024,128]{1,0:T(8,128)(2,1)} %get-tuple-element.46), channel_id=1, source_target_pairs={{0,64},{64,128},{128,192},{192,0},{1,65},{65,129},{129,193},{193,1... | collective-permute-start | bytes 786440 | tf_op jit(solution)/shard_map/ppermute | solution.py:162
  137.0 18.6 %collective-permute-start.9 = (bf16[1024,128]{1,0:T(8,128)(2,1)S(1)}, bf16[1024,128]{1,0:T(8,128)(2,1)S(1)}, u32[]{:S(2)}, u32[]{:S(2)}) collective-permute-start(bf16[1024,128]{1,0:T(8,128)(2,1)S(1)} %get-tuple-element.44), channel_id=1, source_target_pairs={{0,192},{64,0},{128,64},{192,128},{1,193},{65,1},{129,65},{193,129... | collective-permute-start | bytes 786440 | tf_op jit(solution)/shard_map/ppermute | solution.py:162
  150.3 5.3 %copy-start.3 = (f32[1024,128]{1,0:T(8,128)S(1)}, f32[1024,128]{1,0:T(8,128)}, u32[]{:S(2)}) copy-start(f32[1024,128]{1,0:T(8,128)} %copy-done.2) | copy-start | bytes 1572868
  150.3 5.3 %slice-start = ((f32[4,2,256]{2,0,1:T(4,128)}), f32[4,1,256]{2,0,1:T(4,128)S(1)}, s32[]{:S(2)}) async-start(f32[4,2,256]{2,0,1:T(4,128)} %copy-done.10), calls=%async_computation.4 | async-start | bytes 8192 | tf_op jit(solution)/shard_map/slice | solution.py:209
  150.3 9.3 %copy-start.7 = (bf16[2,1024,128]{2,1,0:T(8,128)(2,1)S(1)}, bf16[2,1024,128]{2,1,0:T(8,128)(2,1)}, u32[]{:S(2)}) copy-start(bf16[2,1024,128]{2,1,0:T(8,128)(2,1)} %get-tuple-element.57) | copy-start | bytes 1572868
  156.8 14.2 %collective-permute-start.15 = (bf16[1024,128]{1,0:T(8,128)(2,1)S(1)}, bf16[1024,128]{1,0:T(8,128)(2,1)S(1)}, u32[]{:S(2)}, u32[]{:S(2)}) collective-permute-start(bf16[1024,128]{1,0:T(8,128)(2,1)S(1)} %get-tuple-element.64.refs_0_), channel_id=1, source_target_pairs={{0,64},{64,128},{128,192},{192,0},{1,65},{65,129},{129,193},{193,1... | collective-permute-start | bytes 786440 | tf_op jit(solution)/shard_map/ppermute | solution.py:162
  156.8 14.2 %collective-permute-start.16 = (bf16[1024,128]{1,0:T(8,128)(2,1)S(1)}, bf16[1024,128]{1,0:T(8,128)(2,1)S(1)}, u32[]{:S(2)}, u32[]{:S(2)}) collective-permute-start(bf16[1024,128]{1,0:T(8,128)(2,1)S(1)} %get-tuple-element.64.refs_0_), channel_id=1, source_target_pairs={{0,128},{64,192},{128,0},{192,64},{1,129},{65,193},{129,1},{193,65... | collective-permute-start | bytes 786440 | tf_op jit(solution)/shard_map/ppermute | solution.py:162
  158.3 13.0 %collective-permute-start.17 = (bf16[1024,128]{1,0:T(8,128)(2,1)S(1)}, bf16[1024,128]{1,0:T(8,128)(2,1)S(1)}, u32[]{:S(2)}, u32[]{:S(2)}) collective-permute-start(bf16[1024,128]{1,0:T(8,128)(2,1)S(1)} %get-tuple-element.64.refs_0_), channel_id=1, source_target_pairs={{0,192},{64,0},{128,64},{192,128},{1,193},{65,1},{129,65},{193,129... | collective-permute-start | bytes 786440 | tf_op jit(solution)/shard_map/ppermute | solution.py:162
  175.9 92.4 %all-to-all-start.2 = ((bf16[256,24,256]{2,1,0:T(8,128)(2,1)}), bf16[256,24,256]{2,1,0:T(8,128)(2,1)S(1)}, u32[]{:S(2)}, u32[]{:S(2)}) async-start(bf16[256,24,256]{2,1,0:T(8,128)(2,1)} %bitcast.36), calls=%async_computation.2 | async-start | bytes 6291456 | tf_op jit(solution)/shard_map/all_to_all | solution.py:278
  190.5 8.8 %collective-permute-start.21 = (f32[2,128]{1,0:T(2,128)}, f32[2,128]{1,0:T(2,128)}, u32[]{:S(2)}, u32[]{:S(2)}) collective-permute-start(f32[2,128]{1,0:T(2,128)} %get-tuple-element.99), channel_id=1, source_target_pairs={{0,192},{64,0},{128,64},{192,128},{1,193},{65,1},{129,65},{193,129... | collective-permute-start | bytes 3080 | tf_op jit(solution)/shard_map/ppermute | solution.py:162
  194.2 25.6 %collective-permute-start.18 = (bf16[1024,128]{1,0:T(8,128)(2,1)}, bf16[1024,128]{1,0:T(8,128)(2,1)S(1)}, u32[]{:S(2)}, u32[]{:S(2)}) collective-permute-start(bf16[1024,128]{1,0:T(8,128)(2,1)} %get-tuple-element.65.refs_0_), channel_id=1, source_target_pairs={{0,64},{64,128},{128,192},{192,0},{1,65},{65,129},{129,193},{193,1... | collective-permute-start | bytes 786440 | tf_op jit(solution)/shard_map/ppermute | solution.py:162
  194.3 25.5 %collective-permute-start.19 = (bf16[1024,128]{1,0:T(8,128)(2,1)}, bf16[1024,128]{1,0:T(8,128)(2,1)S(1)}, u32[]{:S(2)}, u32[]{:S(2)}) collective-permute-start(bf16[1024,128]{1,0:T(8,128)(2,1)} %get-tuple-element.65.refs_0_), channel_id=1, source_target_pairs={{0,128},{64,192},{128,0},{192,64},{1,129},{65,193},{129,1},{193,65... | collective-permute-start | bytes 786440 | tf_op jit(solution)/shard_map/ppermute | solution.py:162
  196.0 23.8 %collective-permute-start.20 = (bf16[1024,128]{1,0:T(8,128)(2,1)}, bf16[1024,128]{1,0:T(8,128)(2,1)S(1)}, u32[]{:S(2)}, u32[]{:S(2)}) collective-permute-start(bf16[1024,128]{1,0:T(8,128)(2,1)} %get-tuple-element.65.refs_0_), channel_id=1, source_target_pairs={{0,192},{64,0},{128,64},{192,128},{1,193},{65,1},{129,65},{193,129... | collective-permute-start | bytes 786440 | tf_op jit(solution)/shard_map/ppermute | solution.py:162
  196.9 21.6 %collective-permute-start.22 = (f32[2,128]{1,0:T(2,128)}, f32[2,128]{1,0:T(2,128)S(1)}, u32[]{:S(2)}, u32[]{:S(2)}) collective-permute-start(f32[2,128]{1,0:T(2,128)} %get-tuple-element.100), channel_id=1, source_target_pairs={{0,128},{64,192},{128,0},{192,64},{1,129},{65,193},{129,1},{193,65... | collective-permute-start | bytes 3080 | tf_op jit(solution)/shard_map/ppermute | solution.py:162
  199.3 19.3 %collective-permute-start.23 = (f32[2,128]{1,0:T(2,128)S(1)}, f32[2,128]{1,0:T(2,128)S(1)}, u32[]{:S(2)}, u32[]{:S(2)}) collective-permute-start(f32[2,128]{1,0:T(2,128)S(1)} %bitcast.145), channel_id=1, source_target_pairs={{0,64},{64,128},{128,192},{192,0},{1,65},{65,129},{129,193},{193,1... | collective-permute-start | bytes 3080 | tf_op jit(solution)/shard_map/ppermute | solution.py:162
  219.8 1.0 copy-start.4
  220.7 1.6 copy-start.6
  223.7 21.2 %collective-permute-start.24 = (bf16[2,128,1024]{2,1,0:T(8,128)(2,1)S(1)}, bf16[2,128,1024]{2,1,0:T(8,128)(2,1)S(1)}, u32[]{:S(2)}, u32[]{:S(2)}) collective-permute-start(bf16[2,128,1024]{2,1,0:T(8,128)(2,1)S(1)} %get-tuple-element.71), channel_id=1, source_target_pairs={{0,192},{64,0},{128,64},{192,128},{1,193},{65,1},{129,65},{193,129... | collective-permute-start | bytes 1572872 | tf_op jit(solution)/shard_map/ppermute | solution.py:162
  225.8 22.8 %collective-permute-start.25 = (bf16[2,128,1024]{2,1,0:T(8,128)(2,1)S(1)}, bf16[2,128,1024]{2,1,0:T(8,128)(2,1)S(1)}, u32[]{:S(2)}, u32[]{:S(2)}) collective-permute-start(bf16[2,128,1024]{2,1,0:T(8,128)(2,1)S(1)} %get-tuple-element.72), channel_id=1, source_target_pairs={{0,128},{64,192},{128,0},{192,64},{1,129},{65,193},{129,1},{193,65... | collective-permute-start | bytes 1572872 | tf_op jit(solution)/shard_map/ppermute | solution.py:162
  226.0 41.4 %collective-permute-start.26 = (bf16[2,128,1024]{2,1,0:T(8,128)(2,1)S(1)}, bf16[2,128,1024]{2,1,0:T(8,128)(2,1)S(1)}, u32[]{:S(2)}, u32[]{:S(2)}) collective-permute-start(bf16[2,128,1024]{2,1,0:T(8,128)(2,1)S(1)} %get-tuple-element.73), channel_id=1, source_target_pairs={{0,64},{64,128},{128,192},{192,0},{1,65},{65,129},{129,193},{193,1... | collective-permute-start | bytes 1572872 | tf_op jit(solution)/shard_map/ppermute | solution.py:162
Sparse Core Ops, SparseCore 0:
  9.8 129.3 all-gather.1

commit v4 on v3

--- a/solution.py
+++ b/solution.py
@@ -168,10 +168,12 @@
         return lax.dynamic_slice_in_dim(x, at(s) * quarter, quarter, axis=x.ndim - 1)
 
     def forward(blocks):
-        return [blocks[0]] + [shift(blocks[s], s) for s in range(1, n)]
+        moved = {s: shift(blocks[s], s) for s in (2, 1, 3)}
+        return [blocks[0]] + [moved[s] for s in range(1, n)]
 
     def backward(blocks):
-        return [blocks[0]] + [shift(blocks[s], -s) for s in range(1, n)]
+        moved = {s: shift(blocks[s], -s) for s in (2, 1, 3)}
+        return [blocks[0]] + [moved[s] for s in range(1, n)]
 
     def reduced(blocks):
         total = blocks[0]

time: 279 us -> 279 us (level)
  no operation moved by 1% of the time
where the time goes in v4:
time: 279 us
  waiting for transfers between devices  132 us (47%)
  starting transfers between devices  69 us (25%)
  local copies, waits for them, and re-layouts  21.7 us (8%)
  Pallas kernels  18.4 us (7%)
  matrix products  14.8 us (5%)
  between operations  14.4 us (5%)
  other arithmetic  7.87 us (3%)
    ppermute x27, waiting for transfers between devices, shift(): return lax.ppermute(x, 'dp', [(a, (a + s) % n) for a in range(n)])  109 us
    ppermute x27, starting transfers between devices, shift(): return lax.ppermute(x, 'dp', [(a, (a + s) % n) for a in range(n)])  36.6 us
    pallas_call x5, Pallas kernels, call(): pl.pallas_call(kernel, out_shape=shapes, grid_spec=pltpu.PrefetchScalarGr...  18.4 us
    all_to_all x1, starting transfers between devices, shards(): lax.all_to_all(outgoing.reshape(n * owners, rows, thin), ('dp', 'expert')...  14 us
    all_to_all x1, starting transfers between devices, shards(): lax.all_to_all(request, 'expert', split_axis=0, concat_axis=0, tiled=True)  13.6 us
    all_to_all x1, waiting for transfers between devices, shards(): lax.all_to_all(sent.reshape(owners, rows, quarter), 'expert', split_axis=...  13.1 us
    all_to_all x1, waiting for transfers between devices, shards(): lax.all_to_all(request, 'expert', split_axis=0, concat_axis=0, tiled=True)  9.29 us
    dot_general x1, matrix products, shards(): jnp.einsum('gecd,gecf->edf', inputs, own_grad, preferred_element_type=F32)  8.07 us
  transfers between devices with their start and end apart: 31, of which 13 were waited for; matrix products, arithmetic and copies ran while one was open for 13% of the time, Pallas kernels for 4%

profile of v4, /device:TPU:1, one launch (start us, length us, event | category | flops | bytes accessed | tf_op | source)
XLA Modules:
  0.0 278.5 jit_solution(7520213170296239462)
XLA Ops:
  8.0 2.2 collective-permute-start
  10.2 2.6 collective-permute-start.1
  12.8 1.1 collective-permute-start.2
  15.6 1.7 collective-permute-start.5
  18.5 13.6 %all-to-all-start = ((s32[64,1,32]{2,1,0:T(1,128)}), s32[64,1,32]{2,1,0:T(1,128)S(1)}, u32[]{:S(2)}, u32[]{:S(2)}) async-start(s32[64,1,32]{2,1,0:T(1,128)} %copy.39), calls=%async_computation | async-start | bytes 65536 | tf_op jit(solution)/shard_map/all_to_all | solution.py:203
  32.1 9.3 %all-to-all-done = s32[64,1,32]{2,1,0:T(1,128)S(1)} async-done(((s32[64,1,32]{2,1,0:T(1,128)}), s32[64,1,32]{2,1,0:T(1,128)S(1)}, u32[]{:S(2)}, u32[]{:S(2)}) %all-to-all-start) | async-done | bytes 8224 | tf_op jit(solution)/shard_map/all_to_all | solution.py:203
  42.6 3.0 %shard_map.102 = bf16[1536,1024]{1,0:T(8,128)(2,1)S(1)} custom-call(s32[1536,1]{1,0:T(8,128)S(1)} %reshape.192.pick, bf16[128,1024]{1,0:T(8,128)(2,1)S(1)} %get-tuple-element.89.refs_0_, bf16[128,1024]{1,0:T(8,128)(2,1)S(1)} %collective-permute-done.3.refs_1_, bf16[128,1024]{1,0:T(8,128)(2,1)S(1)} %collective-permute-done.4.refs_2_, ...), custom_call_target="tpu_custom_call" | custom-call | flops 1610612736 | bytes 4200448 | tf_op jit(solution)/shard_map/pallas_call | solution.py:32
  45.7 1.6 copy-done
  47.3 4.8 %all-to-all-start.1 = ((bf16[64,24,1024]{2,1,0:T(8,128)(2,1)}), bf16[64,24,1024]{2,1,0:T(8,128)(2,1)S(1)}, u32[]{:S(2)}, u32[]{:S(2)}) async-start(bf16[64,24,1024]{2,1,0:T(8,128)(2,1)} %bitcast.130), calls=%async_computation.1 | async-start | bytes 6291456 | tf_op jit(solution)/shard_map/all_to_all | solution.py:235
  52.1 3.0 %constant_dynamic-slice_fusion = (bf16[2,128,1024]{2,1,0:T(8,128)(2,1)}, bf16[2,128,1024]{2,1,0:T(8,128)(2,1)}, bf16[2,128,1024]{2,1,0:T(8,128)(2,1)}, bf16[2,128,1024]{2,1,0:T(8,128)(2,1)}) fusion(bf16[2,128,4096]{2,1,0:T(8,128)(2,1)} %param.13, s32[]{:T(128)S(6)} %select_n.71, s32[]{:T(128)S(6)} %select_n.69, s32[]{:T(128)S(6)} %select_n.68, s32[]{:T(128)S(6)} %select_n.70), kind=kLoop, calls=%fused_computation.71 | loop fusion | bytes 4194320 | tf_op jit(solution)/shard_map/dynamic_slice | solution.py:168
  55.5 2.0 collective-permute-start.7
  57.5 2.1 collective-permute-start.8
  59.6 2.9 %constant_dynamic-slice_fusion.4 = (bf16[2,1024,128]{2,1,0:T(8,128)(2,1)}, bf16[2,1024,128]{2,1,0:T(8,128)(2,1)}, bf16[2,1024,128]{2,1,0:T(8,128)(2,1)}, bf16[2,1024,128]{2,1,0:T(8,128)(2,1)}) fusion(bf16[2,4096,128]{2,1,0:T(8,128)(2,1)} %param.12, s32[]{:T(128)S(6)} %select_n.71, s32[]{:T(128)S(6)} %select_n.70, s32[]{:T(128)S(6)} %select_n.69, s32[]{:T(128)S(6)} %select_n.68), kind=kLoop, calls=%fused_computation.75 | loop fusion | bytes 4194320 | tf_op jit(solution)/shard_map/dynamic_slice | solution.py:216
  62.6 18.8 %collective-permute-done.6 = bf16[2,128,1024]{2,1,0:T(8,128)(2,1)} collective-permute-done((bf16[2,128,1024]{2,1,0:T(8,128)(2,1)}, bf16[2,128,1024]{2,1,0:T(8,128)(2,1)}, u32[]{:S(2)}, u32[]{:S(2)}) %collective-permute-start.6) | collective-permute-done | bytes 524320 | tf_op jit(solution)/shard_map/ppermute | solution.py:162
  81.5 22.3 %collective-permute-done.7 = bf16[2,128,1024]{2,1,0:T(8,128)(2,1)} collective-permute-done((bf16[2,128,1024]{2,1,0:T(8,128)(2,1)}, bf16[2,128,1024]{2,1,0:T(8,128)(2,1)}, u32[]{:S(2)}, u32[]{:S(2)}) %collective-permute-start.7) | collective-permute-done | bytes 524320 | tf_op jit(solution)/shard_map/ppermute | solution.py:162
  104.4 2.5 collective-permute-start.13
  106.8 2.1 collective-permute-start.14
  108.9 2.8 %pad_maximum_fusion.wide = bf16[2,512,1024]{2,1,0:T(8,128)(2,1)} fusion(bf16[2,128,1024]{2,1,0:T(8,128)(2,1)} %collective-permute-done.8, bf16[2,128,1024]{2,1,0:T(8,128)(2,1)} %collective-permute-done.7, bf16[2,128,1024]{2,1,0:T(8,128)(2,1)} %collective-permute-done.6, bf16[2,128,1024]{2,1,0:T(8,128)(2,1)S(1)} %copy-done.8), kind=kLoop, calls=%fused_computation.4 | loop fusion | flops 8388608 | bytes 4194304 | tf_op jit(solution)/shard_map/concatenate | solution.py:220
  111.8 13.1 %all-to-all-done.1 = bf16[64,24,1024]{2,1,0:T(8,128)(2,1)S(1)} async-done(((bf16[64,24,1024]{2,1,0:T(8,128)(2,1)}), bf16[64,24,1024]{2,1,0:T(8,128)(2,1)S(1)}, u32[]{:S(2)}, u32[]{:S(2)}) %all-to-all-start.1) | async-done | bytes 3145760 | tf_op jit(solution)/shard_map/all_to_all | solution.py:235
  124.9 1.6 copy-done.1
  126.5 6.0 %shard_map.103 = (bf16[1024,1024]{1,0:T(8,128)(2,1)S(1)}, f32[1024,128]{1,0:T(8,128)S(1)}, bf16[1024,128]{1,0:T(8,128)(2,1)S(1)}, bf16[1024,128]{1,0:T(8,128)(2,1)}, bf16[1024,128]{1,0:T(8,128)(2,1)}) custom-call(s32[2,4,128]{2,1,0:T(4,128)S(1)} %add_bitcast_fusion.into, bf16[1536,1024]{1,0:T(8,128)(2,1)S(1)} %bitcast.129, bf16[2,512,1024]{2,1,0:T(8,128)(2,1)S(1)} %copy-done.1), custom_call_target="tpu_custom_call" | custom-call | flops 4294967296 | bytes 8654848 | tf_op jit(solution)/shard_map/pallas_call | solution.py:32
  133.3 1.3 copy-done.5
  134.6 2.5 collective-permute-start.10
  137.0 2.7 collective-permute-start.9
  139.7 4.3 %collective-permute-done.13 = bf16[2,1024,128]{2,1,0:T(8,128)(2,1)} collective-permute-done((bf16[2,1024,128]{2,1,0:T(8,128)(2,1)}, bf16[2,1024,128]{2,1,0:T(8,128)(2,1)}, u32[]{:S(2)}, u32[]{:S(2)}) %collective-permute-start.13) | collective-permute-done | bytes 524320 | tf_op jit(solution)/shard_map/ppermute | solution.py:162
  144.0 6.3 %fusion.5 = f32[4,2,128,128]{3,2,0,1:T(8,128)S(1)} fusion(bf16[2,4096,128]{2,1,0:T(8,128)(2,1)} %param.12, bf16[4,2,128,4096]{3,2,1,0:T(8,128)(2,1)} %bitcast.132), kind=kOutput, calls=%fused_computation.9 | convolution fusion | flops 1073741824 | bytes 11010048 | tf_op jit(solution)/shard_map/gecd,edf->gecf/dot_general | solution.py:239
  150.5 5.2 %collective-permute-done.11 = bf16[1024,128]{1,0:T(8,128)(2,1)S(1)} collective-permute-done((bf16[1024,128]{1,0:T(8,128)(2,1)}, bf16[1024,128]{1,0:T(8,128)(2,1)S(1)}, u32[]{:S(2)}, u32[]{:S(2)}) %collective-permute-start.11) | collective-permute-done | bytes 262176 | tf_op jit(solution)/shard_map/ppermute | solution.py:162
  155.6 1.1 multiply_reduce_fusion
  156.8 1.5 collective-permute-start.16
  158.3 1.4 collective-permute-start.17
  159.7 1.6 pad_maximum_fusion.1.refs_4_
  161.3 9.7 %collective-permute-done.15.refs_1_ = bf16[1024,128]{1,0:T(8,128)(2,1)S(1)} collective-permute-done((bf16[1024,128]{1,0:T(8,128)(2,1)S(1)}, bf16[1024,128]{1,0:T(8,128)(2,1)S(1)}, u32[]{:S(2)}, u32[]{:S(2)}) %collective-permute-start.15) | collective-permute-done | bytes 262176 | tf_op jit(solution)/shard_map/ppermute | solution.py:162
  171.3 4.6 %shard_map.104 = bf16[4,1536,256]{2,1,0:T(8,128)(2,1)} custom-call(s32[1]{0:T(128)} %bitcast.13.me, s32[4,256]{1,0:T(4,128)S(1)} %multiply_add_fusion.place, bf16[1024,128]{1,0:T(8,128)(2,1)S(1)} %get-tuple-element.64.refs_0_, bf16[1024,128]{1,0:T(8,128)(2,1)S(1)} %collective-permute-done.15.refs_1_, bf16[1024,128]{1,0:T(8,128)(2,1)S(1)} %collective-permute-done.16.refs_2_, ...), custom_call_target="tpu_custom_call" | custom-call | flops 4294967296 | bytes 6295556 | tf_op jit(solution)/shard_map/pallas_call | solution.py:32
  175.9 14.0 %all-to-all-start.2 = ((bf16[256,24,256]{2,1,0:T(8,128)(2,1)}), bf16[256,24,256]{2,1,0:T(8,128)(2,1)S(1)}, u32[]{:S(2)}, u32[]{:S(2)}) async-start(bf16[256,24,256]{2,1,0:T(8,128)(2,1)} %bitcast.36), calls=%async_computation.2 | async-start | bytes 6291456 | tf_op jit(solution)/shard_map/all_to_all | solution.py:280
  190.5 2.7 collective-permute-start.21
  194.3 1.7 collective-permute-start.19
  196.9 2.4 collective-permute-start.22
  199.3 19.2 %collective-permute-done.22 = f32[2,128]{1,0:T(2,128)S(1)} collective-permute-done((f32[2,128]{1,0:T(2,128)}, f32[2,128]{1,0:T(2,128)S(1)}, u32[]{:S(2)}, u32[]{:S(2)}) %collective-permute-start.22) | collective-permute-done | bytes 1056 | tf_op jit(solution)/shard_map/ppermute | solution.py:162
  218.6 1.2 fusion.46
  220.7 1.6 copy-done.6
  222.3 1.3 shard_map.106
  223.7 2.2 collective-permute-start.24
  226.5 8.1 %fusion.2 = bf16[2,4096,128]{2,1,0:T(8,128)(2,1)} fusion(bf16[4,2,128,4096]{3,2,1,0:T(8,128)(2,1)} %bitcast.133, bf16[1,2,128,128]{3,2,1,0:T(8,128)(2,1)S(1)} %get-tuple-element.96, bf16[1,2,128,128]{3,2,1,0:T(8,128)(2,1)S(1)} %get-tuple-element.97, bf16[1,2,128,128]{3,2,1,0:T(8,128)(2,1)S(1)} %get-tuple-element.98, ...), kind=kOutput, calls=%fused_computation.3 | convolution fusion | flops 1075183616 | bytes 10747904 | tf_op jit(solution)/shard_map/gecd,gecf->edf/dot_general | solution.py:304
  234.6 1.6 broadcast_in_dim.51
  237.0 7.8 %collective-permute-done.24 = bf16[2,128,1024]{2,1,0:T(8,128)(2,1)S(1)} collective-permute-done((bf16[2,128,1024]{2,1,0:T(8,128)(2,1)S(1)}, bf16[2,128,1024]{2,1,0:T(8,128)(2,1)S(1)}, u32[]{:S(2)}, u32[]{:S(2)}) %collective-permute-start.24) | collective-permute-done | bytes 524320 | tf_op jit(solution)/shard_map/ppermute | solution.py:162
  245.6 3.0 %collective-permute-done.25 = bf16[2,128,1024]{2,1,0:T(8,128)(2,1)S(1)} collective-permute-done((bf16[2,128,1024]{2,1,0:T(8,128)(2,1)S(1)}, bf16[2,128,1024]{2,1,0:T(8,128)(2,1)S(1)}, u32[]{:S(2)}, u32[]{:S(2)}) %collective-permute-start.25) | collective-permute-done | bytes 524320 | tf_op jit(solution)/shard_map/ppermute | solution.py:162
  249.5 18.0 %collective-permute-done.26 = bf16[2,128,1024]{2,1,0:T(8,128)(2,1)S(1)} collective-permute-done((bf16[2,128,1024]{2,1,0:T(8,128)(2,1)S(1)}, bf16[2,128,1024]{2,1,0:T(8,128)(2,1)S(1)}, u32[]{:S(2)}, u32[]{:S(2)}) %collective-permute-start.26) | collective-permute-done | bytes 524320 | tf_op jit(solution)/shard_map/ppermute | solution.py:162
  268.3 3.4 %shard_map.105 = bf16[128,4096]{1,0:T(8,128)(2,1)} custom-call(s32[1,1536]{1,0:T(1,128)S(1)} %select_n.66.home, bf16[4,1536,256]{2,1,0:T(8,128)(2,1)S(1)} %bitcast.128), custom_call_target="tpu_custom_call" | custom-call | flops 1610612736 | bytes 4200448 | tf_op jit(solution)/shard_map/pallas_call | solution.py:32
  (97 shorter events, 14.8 us)
Async XLA Ops:
  7.2 0.8 copy-start.11
  7.2 0.8 copy-start.12
  7.2 6.7 %copy-start.13 = (s32[1,128]{1,0:T(1,128)S(1)}, s32[1,128]{1,0:T(1,128)}, u32[]{:S(2)}) copy-start(s32[1,128]{1,0:T(1,128)} %param.8) | copy-start | bytes 1540
  7.2 6.7 %copy-start.9 = (bf16[1,128,4096]{2,1,0:T(8,128)(2,1)S(1)}, bf16[1,128,4096]{2,1,0:T(8,128)(2,1)}, u32[]{:S(2)}) copy-start(bf16[1,128,4096]{2,1,0:T(8,128)(2,1)} %param.7) | copy-start | bytes 3145732
  7.2 136.8 %all-gather.2.cloned.1.call-start = ((), (), s32[]{:S(2)}) async-start(), calls=%async_computation.3 | async-start | bytes 10485760 | tf_op jit(solution)/shard_map/all_gather | solution.py:184
  8.0 7.6 %collective-permute-start = (f32[2,256]{1,0:T(2,128)S(1)}, f32[2,256]{1,0:T(2,128)S(1)}, u32[]{:S(2)}, u32[]{:S(2)}) collective-permute-start(f32[2,256]{1,0:T(2,128)S(1)} %get-tuple-element.102), channel_id=1, source_target_pairs={{0,64},{64,128},{128,192},{192,0},{1,65},{65,129},{129,193},{193,1... | collective-permute-start | bytes 6152 | tf_op jit(solution)/shard_map/ppermute | solution.py:162
  10.2 7.1 %collective-permute-start.1 = (f32[2,256]{1,0:T(2,128)S(1)}, f32[2,256]{1,0:T(2,128)S(1)}, u32[]{:S(2)}, u32[]{:S(2)}) collective-permute-start(f32[2,256]{1,0:T(2,128)S(1)} %get-tuple-element.102), channel_id=1, source_target_pairs={{0,128},{64,192},{128,0},{192,64},{1,129},{65,193},{129,1},{193,65... | collective-permute-start | bytes 6152 | tf_op jit(solution)/shard_map/ppermute | solution.py:162
  12.8 4.5 %collective-permute-start.2 = (f32[2,256]{1,0:T(2,128)S(1)}, f32[2,256]{1,0:T(2,128)S(1)}, u32[]{:S(2)}, u32[]{:S(2)}) collective-permute-start(f32[2,256]{1,0:T(2,128)S(1)} %get-tuple-element.102), channel_id=1, source_target_pairs={{0,192},{64,0},{128,64},{192,128},{1,193},{65,1},{129,65},{193,129... | collective-permute-start | bytes 6152 | tf_op jit(solution)/shard_map/ppermute | solution.py:162
  14.3 28.3 %collective-permute-start.3 = (bf16[128,1024]{1,0:T(8,128)(2,1)S(1)}, bf16[128,1024]{1,0:T(8,128)(2,1)S(1)}, u32[]{:S(2)}, u32[]{:S(2)}) collective-permute-start(bf16[128,1024]{1,0:T(8,128)(2,1)S(1)} %get-tuple-element.88), channel_id=1, source_target_pairs={{0,64},{64,128},{128,192},{192,0},{1,65},{65,129},{129,193},{193,1... | collective-permute-start | bytes 786440 | tf_op jit(solution)/shard_map/ppermute | solution.py:162
  14.7 27.8 %collective-permute-start.4 = (bf16[128,1024]{1,0:T(8,128)(2,1)S(1)}, bf16[128,1024]{1,0:T(8,128)(2,1)S(1)}, u32[]{:S(2)}, u32[]{:S(2)}) collective-permute-start(bf16[128,1024]{1,0:T(8,128)(2,1)S(1)} %get-tuple-element.87), channel_id=1, source_target_pairs={{0,128},{64,192},{128,0},{192,64},{1,129},{65,193},{129,1},{193,65... | collective-permute-start | bytes 786440 | tf_op jit(solution)/shard_map/ppermute | solution.py:162
  15.6 27.1 %collective-permute-start.5 = (bf16[128,1024]{1,0:T(8,128)(2,1)S(1)}, bf16[128,1024]{1,0:T(8,128)(2,1)S(1)}, u32[]{:S(2)}, u32[]{:S(2)}) collective-permute-start(bf16[128,1024]{1,0:T(8,128)(2,1)S(1)} %get-tuple-element.86), channel_id=1, source_target_pairs={{0,192},{64,0},{128,64},{192,128},{1,193},{65,1},{129,65},{193,129... | collective-permute-start | bytes 786440 | tf_op jit(solution)/shard_map/ppermute | solution.py:162
  17.3 45.3 %copy-start.10 = (f32[4,2,256]{2,0,1:T(4,128)}, f32[4,2,256]{2,0,1:T(4,128)S(1)}, u32[]{:S(2)}) copy-start(f32[4,2,256]{2,0,1:T(4,128)S(1)} %pad_maximum_fusion.3) | copy-start | bytes 24580
  18.5 22.9 %all-to-all-start = ((s32[64,1,32]{2,1,0:T(1,128)}), s32[64,1,32]{2,1,0:T(1,128)S(1)}, u32[]{:S(2)}, u32[]{:S(2)}) async-start(s32[64,1,32]{2,1,0:T(1,128)} %copy.39), calls=%async_computation | async-start | bytes 65536 | tf_op jit(solution)/shard_map/all_to_all | solution.py:203
  45.7 1.6 copy-start
  47.3 77.6 %all-to-all-start.1 = ((bf16[64,24,1024]{2,1,0:T(8,128)(2,1)}), bf16[64,24,1024]{2,1,0:T(8,128)(2,1)S(1)}, u32[]{:S(2)}, u32[]{:S(2)}) async-start(bf16[64,24,1024]{2,1,0:T(8,128)(2,1)} %bitcast.130), calls=%async_computation.1 | async-start | bytes 6291456 | tf_op jit(solution)/shard_map/all_to_all | solution.py:235
  55.1 26.4 %collective-permute-start.6 = (bf16[2,128,1024]{2,1,0:T(8,128)(2,1)}, bf16[2,128,1024]{2,1,0:T(8,128)(2,1)}, u32[]{:S(2)}, u32[]{:S(2)}) collective-permute-start(bf16[2,128,1024]{2,1,0:T(8,128)(2,1)} %get-tuple-element.77), channel_id=1, source_target_pairs={{0,64},{64,128},{128,192},{192,0},{1,65},{65,129},{129,193},{193,1... | collective-permute-start | bytes 1572872 | tf_op jit(solution)/shard_map/ppermute | solution.py:162
  55.5 48.2 %collective-permute-start.7 = (bf16[2,128,1024]{2,1,0:T(8,128)(2,1)}, bf16[2,128,1024]{2,1,0:T(8,128)(2,1)}, u32[]{:S(2)}, u32[]{:S(2)}) collective-permute-start(bf16[2,128,1024]{2,1,0:T(8,128)(2,1)} %get-tuple-element.79), channel_id=1, source_target_pairs={{0,128},{64,192},{128,0},{192,64},{1,129},{65,193},{129,1},{193,65... | collective-permute-start | bytes 1572872 | tf_op jit(solution)/shard_map/ppermute | solution.py:162
  57.5 46.8 %collective-permute-start.8 = (bf16[2,128,1024]{2,1,0:T(8,128)(2,1)}, bf16[2,128,1024]{2,1,0:T(8,128)(2,1)}, u32[]{:S(2)}, u32[]{:S(2)}) collective-permute-start(bf16[2,128,1024]{2,1,0:T(8,128)(2,1)} %get-tuple-element.76), channel_id=1, source_target_pairs={{0,192},{64,0},{128,64},{192,128},{1,193},{65,1},{129,65},{193,129... | collective-permute-start | bytes 1572872 | tf_op jit(solution)/shard_map/ppermute | solution.py:162
  59.6 49.3 %copy-start.8 = (bf16[2,128,1024]{2,1,0:T(8,128)(2,1)S(1)}, bf16[2,128,1024]{2,1,0:T(8,128)(2,1)}, u32[]{:S(2)}) copy-start(bf16[2,128,1024]{2,1,0:T(8,128)(2,1)} %get-tuple-element.39) | copy-start | bytes 1572868
  104.4 32.7 %collective-permute-start.12 = (bf16[2,1024,128]{2,1,0:T(8,128)(2,1)}, bf16[2,1024,128]{2,1,0:T(8,128)(2,1)}, u32[]{:S(2)}, u32[]{:S(2)}) collective-permute-start(bf16[2,1024,128]{2,1,0:T(8,128)(2,1)} %get-tuple-element.48), channel_id=1, source_target_pairs={{0,64},{64,128},{128,192},{192,0},{1,65},{65,129},{129,193},{193,1... | collective-permute-start | bytes 1572872 | tf_op jit(solution)/shard_map/ppermute | solution.py:162
  104.4 39.6 %collective-permute-start.13 = (bf16[2,1024,128]{2,1,0:T(8,128)(2,1)}, bf16[2,1024,128]{2,1,0:T(8,128)(2,1)}, u32[]{:S(2)}, u32[]{:S(2)}) collective-permute-start(bf16[2,1024,128]{2,1,0:T(8,128)(2,1)} %get-tuple-element.49), channel_id=1, source_target_pairs={{0,128},{64,192},{128,0},{192,64},{1,129},{65,193},{129,1},{193,65... | collective-permute-start | bytes 1572872 | tf_op jit(solution)/shard_map/ppermute | solution.py:162
  106.8 37.2 %collective-permute-start.14 = (bf16[2,1024,128]{2,1,0:T(8,128)(2,1)}, bf16[2,1024,128]{2,1,0:T(8,128)(2,1)}, u32[]{:S(2)}, u32[]{:S(2)}) collective-permute-start(bf16[2,1024,128]{2,1,0:T(8,128)(2,1)} %get-tuple-element.50), channel_id=1, source_target_pairs={{0,192},{64,0},{128,64},{192,128},{1,193},{65,1},{129,65},{193,129... | collective-permute-start | bytes 1572872 | tf_op jit(solution)/shard_map/ppermute | solution.py:162
  124.9 1.6 copy-start.1
  132.5 0.8 copy-start.2
  133.3 1.3 copy-start.5
  134.6 15.9 %collective-permute-start.10 = (bf16[1024,128]{1,0:T(8,128)(2,1)}, bf16[1024,128]{1,0:T(8,128)(2,1)S(1)}, u32[]{:S(2)}, u32[]{:S(2)}) collective-permute-start(bf16[1024,128]{1,0:T(8,128)(2,1)} %get-tuple-element.45), channel_id=1, source_target_pairs={{0,128},{64,192},{128,0},{192,64},{1,129},{65,193},{129,1},{193,65... | collective-permute-start | bytes 786440 | tf_op jit(solution)/shard_map/ppermute | solution.py:162
  137.0 18.6 %collective-permute-start.11 = (bf16[1024,128]{1,0:T(8,128)(2,1)}, bf16[1024,128]{1,0:T(8,128)(2,1)S(1)}, u32[]{:S(2)}, u32[]{:S(2)}) collective-permute-start(bf16[1024,128]{1,0:T(8,128)(2,1)} %get-tuple-element.46), channel_id=1, source_target_pairs={{0,64},{64,128},{128,192},{192,0},{1,65},{65,129},{129,193},{193,1... | collective-permute-start | bytes 786440 | tf_op jit(solution)/shard_map/ppermute | solution.py:162
  137.0 18.6 %collective-permute-start.9 = (bf16[1024,128]{1,0:T(8,128)(2,1)S(1)}, bf16[1024,128]{1,0:T(8,128)(2,1)S(1)}, u32[]{:S(2)}, u32[]{:S(2)}) collective-permute-start(bf16[1024,128]{1,0:T(8,128)(2,1)S(1)} %get-tuple-element.44), channel_id=1, source_target_pairs={{0,192},{64,0},{128,64},{192,128},{1,193},{65,1},{129,65},{193,129... | collective-permute-start | bytes 786440 | tf_op jit(solution)/shard_map/ppermute | solution.py:162
  150.3 5.3 %copy-start.3 = (f32[1024,128]{1,0:T(8,128)S(1)}, f32[1024,128]{1,0:T(8,128)}, u32[]{:S(2)}) copy-start(f32[1024,128]{1,0:T(8,128)} %copy-done.2) | copy-start | bytes 1572868
  150.3 5.3 %slice-start = ((f32[4,2,256]{2,0,1:T(4,128)}), f32[4,1,256]{2,0,1:T(4,128)S(1)}, s32[]{:S(2)}) async-start(f32[4,2,256]{2,0,1:T(4,128)} %copy-done.10), calls=%async_computation.4 | async-start | bytes 8192 | tf_op jit(solution)/shard_map/slice | solution.py:211
  150.3 9.3 %copy-start.7 = (bf16[2,1024,128]{2,1,0:T(8,128)(2,1)S(1)}, bf16[2,1024,128]{2,1,0:T(8,128)(2,1)}, u32[]{:S(2)}) copy-start(bf16[2,1024,128]{2,1,0:T(8,128)(2,1)} %get-tuple-element.57) | copy-start | bytes 1572868
  156.8 14.2 %collective-permute-start.15 = (bf16[1024,128]{1,0:T(8,128)(2,1)S(1)}, bf16[1024,128]{1,0:T(8,128)(2,1)S(1)}, u32[]{:S(2)}, u32[]{:S(2)}) collective-permute-start(bf16[1024,128]{1,0:T(8,128)(2,1)S(1)} %get-tuple-element.64.refs_0_), channel_id=1, source_target_pairs={{0,64},{64,128},{128,192},{192,0},{1,65},{65,129},{129,193},{193,1... | collective-permute-start | bytes 786440 | tf_op jit(solution)/shard_map/ppermute | solution.py:162
  156.8 14.2 %collective-permute-start.16 = (bf16[1024,128]{1,0:T(8,128)(2,1)S(1)}, bf16[1024,128]{1,0:T(8,128)(2,1)S(1)}, u32[]{:S(2)}, u32[]{:S(2)}) collective-permute-start(bf16[1024,128]{1,0:T(8,128)(2,1)S(1)} %get-tuple-element.64.refs_0_), channel_id=1, source_target_pairs={{0,128},{64,192},{128,0},{192,64},{1,129},{65,193},{129,1},{193,65... | collective-permute-start | bytes 786440 | tf_op jit(solution)/shard_map/ppermute | solution.py:162
  158.3 13.0 %collective-permute-start.17 = (bf16[1024,128]{1,0:T(8,128)(2,1)S(1)}, bf16[1024,128]{1,0:T(8,128)(2,1)S(1)}, u32[]{:S(2)}, u32[]{:S(2)}) collective-permute-start(bf16[1024,128]{1,0:T(8,128)(2,1)S(1)} %get-tuple-element.64.refs_0_), channel_id=1, source_target_pairs={{0,192},{64,0},{128,64},{192,128},{1,193},{65,1},{129,65},{193,129... | collective-permute-start | bytes 786440 | tf_op jit(solution)/shard_map/ppermute | solution.py:162
  175.9 92.4 %all-to-all-start.2 = ((bf16[256,24,256]{2,1,0:T(8,128)(2,1)}), bf16[256,24,256]{2,1,0:T(8,128)(2,1)S(1)}, u32[]{:S(2)}, u32[]{:S(2)}) async-start(bf16[256,24,256]{2,1,0:T(8,128)(2,1)} %bitcast.36), calls=%async_computation.2 | async-start | bytes 6291456 | tf_op jit(solution)/shard_map/all_to_all | solution.py:280
  190.5 8.8 %collective-permute-start.21 = (f32[2,128]{1,0:T(2,128)}, f32[2,128]{1,0:T(2,128)}, u32[]{:S(2)}, u32[]{:S(2)}) collective-permute-start(f32[2,128]{1,0:T(2,128)} %get-tuple-element.99), channel_id=1, source_target_pairs={{0,192},{64,0},{128,64},{192,128},{1,193},{65,1},{129,65},{193,129... | collective-permute-start | bytes 3080 | tf_op jit(solution)/shard_map/ppermute | solution.py:162
  194.2 25.6 %collective-permute-start.18 = (bf16[1024,128]{1,0:T(8,128)(2,1)}, bf16[1024,128]{1,0:T(8,128)(2,1)S(1)}, u32[]{:S(2)}, u32[]{:S(2)}) collective-permute-start(bf16[1024,128]{1,0:T(8,128)(2,1)} %get-tuple-element.65.refs_0_), channel_id=1, source_target_pairs={{0,64},{64,128},{128,192},{192,0},{1,65},{65,129},{129,193},{193,1... | collective-permute-start | bytes 786440 | tf_op jit(solution)/shard_map/ppermute | solution.py:162
  194.3 25.5 %collective-permute-start.19 = (bf16[1024,128]{1,0:T(8,128)(2,1)}, bf16[1024,128]{1,0:T(8,128)(2,1)S(1)}, u32[]{:S(2)}, u32[]{:S(2)}) collective-permute-start(bf16[1024,128]{1,0:T(8,128)(2,1)} %get-tuple-element.65.refs_0_), channel_id=1, source_target_pairs={{0,128},{64,192},{128,0},{192,64},{1,129},{65,193},{129,1},{193,65... | collective-permute-start | bytes 786440 | tf_op jit(solution)/shard_map/ppermute | solution.py:162
  196.0 23.8 %collective-permute-start.20 = (bf16[1024,128]{1,0:T(8,128)(2,1)}, bf16[1024,128]{1,0:T(8,128)(2,1)S(1)}, u32[]{:S(2)}, u32[]{:S(2)}) collective-permute-start(bf16[1024,128]{1,0:T(8,128)(2,1)} %get-tuple-element.65.refs_0_), channel_id=1, source_target_pairs={{0,192},{64,0},{128,64},{192,128},{1,193},{65,1},{129,65},{193,129... | collective-permute-start | bytes 786440 | tf_op jit(solution)/shard_map/ppermute | solution.py:162
  196.9 21.6 %collective-permute-start.22 = (f32[2,128]{1,0:T(2,128)}, f32[2,128]{1,0:T(2,128)S(1)}, u32[]{:S(2)}, u32[]{:S(2)}) collective-permute-start(f32[2,128]{1,0:T(2,128)} %get-tuple-element.100), channel_id=1, source_target_pairs={{0,128},{64,192},{128,0},{192,64},{1,129},{65,193},{129,1},{193,65... | collective-permute-start | bytes 3080 | tf_op jit(solution)/shard_map/ppermute | solution.py:162
  199.3 19.3 %collective-permute-start.23 = (f32[2,128]{1,0:T(2,128)S(1)}, f32[2,128]{1,0:T(2,128)S(1)}, u32[]{:S(2)}, u32[]{:S(2)}) collective-permute-start(f32[2,128]{1,0:T(2,128)S(1)} %bitcast.145), channel_id=1, source_target_pairs={{0,64},{64,128},{128,192},{192,0},{1,65},{65,129},{129,193},{193,1... | collective-permute-start | bytes 3080 | tf_op jit(solution)/shard_map/ppermute | solution.py:162
  219.8 1.0 copy-start.4
  220.7 1.6 copy-start.6
  223.7 21.2 %collective-permute-start.24 = (bf16[2,128,1024]{2,1,0:T(8,128)(2,1)S(1)}, bf16[2,128,1024]{2,1,0:T(8,128)(2,1)S(1)}, u32[]{:S(2)}, u32[]{:S(2)}) collective-permute-start(bf16[2,128,1024]{2,1,0:T(8,128)(2,1)S(1)} %get-tuple-element.71), channel_id=1, source_target_pairs={{0,192},{64,0},{128,64},{192,128},{1,193},{65,1},{129,65},{193,129... | collective-permute-start | bytes 1572872 | tf_op jit(solution)/shard_map/ppermute | solution.py:162
  225.8 22.8 %collective-permute-start.25 = (bf16[2,128,1024]{2,1,0:T(8,128)(2,1)S(1)}, bf16[2,128,1024]{2,1,0:T(8,128)(2,1)S(1)}, u32[]{:S(2)}, u32[]{:S(2)}) collective-permute-start(bf16[2,128,1024]{2,1,0:T(8,128)(2,1)S(1)} %get-tuple-element.72), channel_id=1, source_target_pairs={{0,128},{64,192},{128,0},{192,64},{1,129},{65,193},{129,1},{193,65... | collective-permute-start | bytes 1572872 | tf_op jit(solution)/shard_map/ppermute | solution.py:162
  226.0 41.4 %collective-permute-start.26 = (bf16[2,128,1024]{2,1,0:T(8,128)(2,1)S(1)}, bf16[2,128,1024]{2,1,0:T(8,128)(2,1)S(1)}, u32[]{:S(2)}, u32[]{:S(2)}) collective-permute-start(bf16[2,128,1024]{2,1,0:T(8,128)(2,1)S(1)} %get-tuple-element.73), channel_id=1, source_target_pairs={{0,64},{64,128},{128,192},{192,0},{1,65},{65,129},{129,193},{193,1... | collective-permute-start | bytes 1572872 | tf_op jit(solution)/shard_map/ppermute | solution.py:162
Sparse Core Ops, SparseCore 0:
  9.8 129.3 all-gather.1
